TPU v7x, 32 devices: a whole 2x2x4 slice. The times are simulated.
32 devices in a mesh: section: 2 (over core), mp: 2 (over x), dp: 8 (over z, y).
Axes of the slice: x: 2, y: 2, z: 4, core: 2. Of those that a mesh axis runs over, the one named last changes fastest.
Arguments:
- tokens: bfloat16 [2, 512, 8, 1024], P(None, 'mp', 'dp'), may hold values from -6 to 6
- valid_mask: int32 [2, 512, 8], P(None, None, 'dp'), may hold values from 0 to 1, as said below
- buckets: int32 [512], replicated, may hold values from 0 to 31, as said below
- state_init: bfloat16 [512, 8, 1024], P('mp', 'dp'), may hold values from -6 to 6
- norm_gain: float32 [2, 2, 1024], P('section'), may hold values from 0.5 to 1.5
- norm_shift: float32 [2, 2, 1024], P('section'), may hold values from -1.75 to 1.75
- w_qkv: bfloat16 [2, 3, 1024, 1024], P('section', None, None, 'mp'), may hold values from -0.1875 to 0.1875
- w_out: bfloat16 [2, 1024, 1024], P('section', 'mp'), may hold values from -1.5 to 1.5
- rel_bias: float32 [2, 32, 8], P('section', None, 'mp'), may hold values from -6 to 6
- w_up: bfloat16 [2, 1024, 4096], P('section', None, 'mp'), may hold values from -0.1875 to 0.1875
- up_bias: float32 [2, 4096], P('section', 'mp'), may hold values from -1.75 to 1.75
- w_down: bfloat16 [2, 4096, 1024], P('section', 'mp'), may hold values from -0.09375 to 0.09375
- down_bias: float32 [2, 1024], P('section'), may hold values from -1.75 to 1.75
- state_gain: float32 [1024], replicated, may hold values from 0.5 to 1.5
- state_shift: float32 [1024], replicated, may hold values from -1.75 to 1.75
- w_state_qkv: bfloat16 [3, 1024, 1024], P(None, None, 'mp'), may hold values from -0.1875 to 0.1875
- w_state_out: bfloat16 [1024, 1024], P('mp'), may hold values from -1.5 to 1.5
- gate_bias: float32 [1024], replicated, may hold values from -2 to 2
- cotangent: bfloat16 [2, 512, 8, 1024], P(None, 'mp', 'dp'), may hold values from -6 to 6
Outputs:
- acts: bfloat16 [2, 2, 512, 8, 1024], P('section', None, 'mp', 'dp')
- input_grads: float32 [2, 2, 512, 8, 1024], P('section', None, 'mp', 'dp')
- final_state: float32 [512, 8, 1024], P('mp', 'dp')
- grad_norm_gain: float32 [2, 2, 1024], P('section')
- grad_norm_shift: float32 [2, 2, 1024], P('section')
- grad_w_qkv: float32 [2, 3, 1024, 1024], P('section', None, None, 'mp')
- grad_w_out: float32 [2, 1024, 1024], P('section', 'mp')
- grad_rel_bias: float32 [2, 32, 8], P('section', None, 'mp')
- grad_w_up: float32 [2, 1024, 4096], P('section', None, 'mp')
- grad_up_bias: float32 [2, 4096], P('section', 'mp')
- grad_w_down: float32 [2, 4096, 1024], P('section', 'mp')
- grad_down_bias: float32 [2, 1024], P('section')
- grad_state_gain: float32 [1024], replicated
- grad_state_shift: float32 [1024], replicated
- grad_w_state_qkv: float32 [3, 1024, 1024], P(None, None, 'mp')
- grad_w_state_out: float32 [1024, 1024], P('mp')
- grad_gate_bias: float32 [1024], replicated
Inputs may be any that keep to these rules, and one draw needn't show every extreme that they name: `valid_mask`: in each block of 512 tokens of a document the valid tokens come first; at most 153 tokens at a block's end are invalid, and in every draw some block has exactly 153 invalid. `buckets`: never falls as the distance grows; distance 0 has bucket 0 and distance 512 - 1 has bucket 32 - 1.
All inputs are finite; a program needn't handle non-finite values.
Results may differ from a plain program's by a relative error of at most 0.03.
Values may be sent and summed in bfloat16 or wider, within the bound.
A program may use at most 320 MiB of HBM per device.

v0:
```python
from functools import partial

import jax
import jax.numpy as jnp
from jax import lax
from jax.sharding import PartitionSpec as P

eps = 1e-05
negative = -1000000000.0
highest = lax.Precision.HIGHEST
band_count = 4


def from_behind(array, axis, by):
    size = lax.axis_size(axis)
    pairs = [(i, i + by) for i in range(size) if 0 <= i + by < size]
    return lax.ppermute(array, axis, pairs)


def layer_norm(values, gain, shift):
    average = jnp.mean(values, axis=-1, keepdims=True)
    centered = values - average
    spread = jnp.mean(centered * centered, axis=-1, keepdims=True)
    return centered * lax.rsqrt(spread + eps) * gain + shift


def window_grid(by_distance):
    head_count, block_len = by_distance.shape
    flipped = by_distance[:, ::-1]
    middle = jnp.broadcast_to(flipped[:, None, :], (head_count, block_len, block_len))
    padded = jnp.concatenate(
        [
            jnp.zeros((head_count, block_len, 1), jnp.float32),
            middle,
            jnp.zeros((head_count, block_len, block_len), jnp.float32),
        ],
        axis=2,
    )
    flattened = padded.reshape(head_count, -1)[:, : 2 * block_len * block_len]
    return flattened.reshape(head_count, block_len, 2 * block_len)


def diagonal_sums(logit_grid, count):
    head_count, row_count, key_len = logit_grid.shape
    flattened = jnp.concatenate(
        [logit_grid.reshape(head_count, -1), jnp.zeros((head_count, row_count), jnp.float32)],
        axis=1,
    )
    skewed = flattened.reshape(head_count, row_count, key_len + 1)[:, :, 1 : count + 1]
    return jnp.sum(skewed, axis=1)[:, ::-1]


def joint_softmax(window_logits, state_logits):
    peak = jnp.maximum(
        jnp.max(window_logits, axis=-1, keepdims=True),
        jnp.max(state_logits, axis=-1, keepdims=True),
    )
    window_exp = jnp.exp(window_logits - peak)
    state_exp = jnp.exp(state_logits - peak)
    denominator = jnp.sum(window_exp, axis=-1, keepdims=True) + jnp.sum(
        state_exp, axis=-1, keepdims=True
    )
    return (window_exp / denominator, state_exp / denominator, peak + jnp.log(denominator))


def local(
    tokens,
    valid_mask,
    buckets,
    state_init,
    norm_gain,
    norm_shift,
    w_qkv,
    w_out,
    rel_bias,
    w_up,
    up_bias,
    w_down,
    down_bias,
    state_gain,
    state_shift,
    w_state_qkv,
    w_state_out,
    gate_bias,
    cotangent,
):
    block_count, tok_rows, doc_count, model_width = tokens.shape
    state_rows = state_init.shape[0]
    block_len = valid_mask.shape[1]
    head_count = rel_bias.shape[2]
    head_cols = w_qkv.shape[3]
    scale_factor = (head_cols // head_count) ** (-0.5)
    group_rows = block_len // band_count
    band_width = block_len + group_rows
    section_now = lax.axis_index("section")
    is_rec = section_now == 1
    valid_all = valid_mask.astype(jnp.float32)
    gain_first, gain_second = (norm_gain[0, 0], norm_gain[0, 1])
    shift_first, shift_second = (norm_shift[0, 0], norm_shift[0, 1])
    qkv_own = w_qkv[0]
    out_own = w_out[0]
    up_own = w_up[0]
    up_bias_own = up_bias[0]
    down_own = w_down[0]
    down_bias_own = down_bias[0]
    gate = jax.nn.sigmoid(gate_bias)
    bucket_onehot = (buckets[:, None] == jnp.arange(rel_bias.shape[1])[None, :]).astype(jnp.float32)
    by_distance = jnp.dot(
        bucket_onehot, rel_bias[0], precision=highest, preferred_element_type=jnp.float32
    ).T
    window_bias = window_grid(by_distance)[:, :group_rows, :band_width]
    query_pos = jnp.arange(group_rows)[:, None]
    key_pos = jnp.arange(band_width)[None, :]
    offset = key_pos - query_pos
    inside = (offset >= 1) & (offset <= block_len)

    def split_heads(array_in):
        return array_in.reshape(array_in.shape[0], array_in.shape[1], head_count, -1)

    def merge_heads(array_in):
        return array_in.reshape(array_in.shape[0], doc_count, head_cols)

    def to_groups(array_in):
        return array_in.reshape((band_count, group_rows) + array_in.shape[1:])

    def from_groups(array_in):
        return array_in.reshape((block_len,) + array_in.shape[2:])

    def band_of(window_rows):
        return jnp.stack(
            [
                window_rows[index * group_rows : index * group_rows + band_width]
                for index in range(band_count)
            ]
        )

    def unband(banded):
        total = None
        for index in range(band_count):
            widths = [(index * group_rows, block_len - (index + 1) * group_rows)] + [(0, 0)] * (
                banded.ndim - 2
            )
            placed = jnp.pad(banded[index], widths)
            total = placed if total is None else total + placed
        return total

    def attention_logits(query_g, key_band, state_key4, valid_win):
        valid_band = jnp.transpose(band_of(valid_win), (0, 2, 1))
        keep = inside[None, None, None] & (valid_band > 0.5)[:, :, None, None, :]
        window_logits = (
            jnp.einsum("gqbhe,gkbhe->gbhqk", query_g, key_band, preferred_element_type=jnp.float32)
            * scale_factor
            + window_bias[None, None]
        )
        window_logits = jnp.where(keep, window_logits, negative)
        state_logits = (
            jnp.einsum("gqbhe,kbhe->gbhqk", query_g, state_key4, preferred_element_type=jnp.float32)
            * scale_factor
        )
        state_logits = jnp.where(is_rec, state_logits, negative)
        return (window_logits, state_logits)

    def recur_logits_of(state_query4, key_cur4, valid_cur):
        logits = (
            jnp.einsum(
                "sbhe,kbhe->bhsk", state_query4, key_cur4, preferred_element_type=jnp.float32
            )
            * scale_factor
        )
        return jnp.where((valid_cur.T > 0.5)[:, None, None, :], logits, negative)

    zero_keys = jnp.zeros((block_len, doc_count, head_cols), jnp.bfloat16)
    key_prev, value_prev = (zero_keys, zero_keys)
    valid_prev = jnp.zeros((block_len, doc_count), jnp.float32)
    state_now = state_init.astype(jnp.float32)
    incoming = jnp.zeros((tok_rows, doc_count, model_width), jnp.bfloat16)
    acts_out = jnp.zeros(tokens.shape, jnp.bfloat16)
    records = []
    for step_index in range(block_count + 1):
        block_now = step_index - section_now
        active = (block_now >= 0) & (block_now < block_count)
        block_safe = jnp.clip(block_now, 0, block_count - 1)
        own_rows = tokens[min(step_index, block_count - 1)].astype(jnp.float32)
        rows_in = jnp.where(is_rec, incoming.astype(jnp.float32), own_rows)
        valid_cur = lax.dynamic_index_in_dim(valid_all, block_safe, 0, keepdims=False)
        normed_loc = layer_norm(rows_in, gain_first, shift_first).astype(jnp.bfloat16)
        state_loc = layer_norm(state_now, state_gain, state_shift).astype(jnp.bfloat16)
        forward_normed = lax.all_gather(normed_loc, "mp", axis=0, tiled=True)
        forward_state_normed = lax.all_gather(state_loc, "mp", axis=0, tiled=True)
        forward_projected = jnp.einsum(
            "tbd,jdc->jtbc", forward_normed, qkv_own, preferred_element_type=jnp.float32
        ).astype(jnp.bfloat16)
        forward_state_projected = jnp.einsum(
            "tbd,jdc->jtbc", forward_state_normed, w_state_qkv, preferred_element_type=jnp.float32
        ).astype(jnp.bfloat16)
        key_win = jnp.concatenate([key_prev, forward_projected[1]], axis=0)
        value_win = jnp.concatenate([value_prev, forward_projected[2]], axis=0)
        forward_valid_win = jnp.concatenate([valid_prev, valid_cur], axis=0)
        forward_query_g = to_groups(split_heads(forward_projected[0]))
        forward_window_logits, forward_state_logits = attention_logits(
            forward_query_g,
            band_of(split_heads(key_win)),
            split_heads(forward_state_projected[1]),
            forward_valid_win,
        )
        forward_window_probs, forward_state_probs, forward_token_lse = joint_softmax(
            forward_window_logits, forward_state_logits
        )
        forward_attended = jnp.einsum(
            "gbhqk,gkbhe->gqbhe",
            forward_window_probs.astype(jnp.bfloat16),
            band_of(split_heads(value_win)),
            preferred_element_type=jnp.float32,
        )
        forward_attended = forward_attended + jnp.einsum(
            "gbhqk,kbhe->gqbhe",
            forward_state_probs.astype(jnp.bfloat16),
            split_heads(forward_state_projected[2]),
            preferred_element_type=jnp.float32,
        )
        forward_attended = merge_heads(from_groups(forward_attended)).astype(jnp.bfloat16)
        forward_recur_logits = recur_logits_of(
            split_heads(forward_state_projected[0]), split_heads(forward_projected[1]), valid_cur
        )
        recur_peak = jnp.max(forward_recur_logits, axis=-1, keepdims=True)
        recur_exp = jnp.exp(forward_recur_logits - recur_peak)
        recur_sum = jnp.sum(recur_exp, axis=-1, keepdims=True)
        forward_recur_probs = recur_exp / recur_sum
        forward_recur_lse = recur_peak + jnp.log(recur_sum)
        forward_recalled = jnp.einsum(
            "bhsk,kbhe->sbhe",
            forward_recur_probs.astype(jnp.bfloat16),
            split_heads(forward_projected[2]),
            preferred_element_type=jnp.float32,
        )
        forward_recalled = merge_heads(forward_recalled).astype(jnp.bfloat16)
        joint_rows = tok_rows + state_rows
        pieces = joint_rows * lax.axis_size("mp") // joint_rows
        token_term = jnp.einsum(
            "tbc,cd->tbd", forward_attended, out_own, preferred_element_type=jnp.float32
        )
        state_term = jnp.einsum(
            "tbc,cd->tbd", forward_recalled, w_state_out, preferred_element_type=jnp.float32
        )
        token_term = token_term.reshape(pieces, tok_rows, doc_count, model_width)
        state_term = state_term.reshape(pieces, state_rows, doc_count, model_width)
        joint = lax.psum_scatter(
            jnp.concatenate([token_term, state_term], axis=1)
            .reshape(pieces * joint_rows, doc_count, model_width)
            .astype(jnp.bfloat16),
            "mp",
            scatter_dimension=0,
            tiled=True,
        ).astype(jnp.float32)
        branch_rows = joint[:tok_rows]
        forward_update_rows = joint[tok_rows:]
        forward_hidden_rows = rows_in + branch_rows
        mlp_loc = layer_norm(forward_hidden_rows, gain_second, shift_second).astype(jnp.bfloat16)
        forward_mlp_in = lax.all_gather(mlp_loc, "mp", axis=0, tiled=True)
        forward_pre_act = (
            jnp.einsum("tbd,df->tbf", forward_mlp_in, up_own, preferred_element_type=jnp.float32)
            + up_bias_own
        )
        forward_activated = jax.nn.gelu(forward_pre_act, approximate=False).astype(jnp.bfloat16)
        result_rows = (
            forward_hidden_rows
            + lax.psum_scatter(
                jnp.einsum(
                    "tbf,fd->tbd", forward_activated, down_own, preferred_element_type=jnp.float32
                ).astype(jnp.bfloat16),
                "mp",
                scatter_dimension=0,
                tiled=True,
            ).astype(jnp.float32)
            + down_bias_own
        )
        state_next = gate * state_now + (1.0 - gate) * forward_update_rows
        forward_kept = (
            forward_normed,
            forward_state_normed,
            forward_projected,
            forward_state_projected,
            forward_token_lse,
            forward_recur_lse,
            forward_attended,
            forward_recalled,
            forward_hidden_rows,
            forward_mlp_in,
            forward_pre_act,
            forward_activated,
            forward_update_rows,
        )
        result_rows, state_next, kept = (result_rows, state_next, forward_kept)
        result_low = result_rows.astype(jnp.bfloat16)
        acts_out = jnp.where(
            active, lax.dynamic_update_index_in_dim(acts_out, result_low, block_safe, 0), acts_out
        )
        records.append(
            (
                kept,
                rows_in,
                state_now,
                key_prev,
                value_prev,
                valid_prev,
                valid_cur,
                block_safe,
                active,
            )
        )
        key_prev = jnp.where(active, kept[2][1], key_prev)
        value_prev = jnp.where(active, kept[2][2], value_prev)
        valid_prev = jnp.where(active, valid_cur, valid_prev)
        state_now = jnp.where(active, state_next, state_now)
        if step_index < block_count:
            incoming = from_behind(result_low, "section", 1)
    received_state = from_behind(state_now.astype(jnp.bfloat16), "section", -1).astype(
        state_now.dtype
    )
    final_state = jnp.where(is_rec, state_now, received_state)
    grad_in = jnp.zeros((tok_rows, doc_count, model_width), jnp.float32)
    key_grad_next = jnp.zeros((block_len, doc_count, head_cols), jnp.float32)
    value_grad_next = jnp.zeros((block_len, doc_count, head_cols), jnp.float32)
    state_grad = jnp.zeros(state_now.shape, jnp.float32)
    input_grads = jnp.zeros(tokens.shape, jnp.float32)
    totals = None
    for step_index in range(block_count + 1):
        kept, rows_in, state_in, key_prev, value_prev, valid_prev, valid_cur, block_safe, active = (
            records[block_count - step_index]
        )
        from_loss = lax.dynamic_index_in_dim(cotangent, block_safe, 0, keepdims=False).astype(
            jnp.float32
        )
        grad_rows = jnp.where(is_rec, from_loss, grad_in)
        (
            normed,
            state_normed,
            projected,
            state_projected,
            token_lse,
            recur_lse,
            attended,
            recalled,
            hidden_rows,
            mlp_in,
            pre_act,
            activated,
            update_rows,
        ) = kept
        grad_all = lax.all_gather(grad_rows.astype(jnp.bfloat16), "mp", axis=0, tiled=True)
        backward_down_grad = jnp.einsum(
            "tbf,tbd->fd", activated, grad_all, preferred_element_type=jnp.float32
        )
        act_grad = jnp.einsum("tbd,fd->tbf", grad_all, down_own, preferred_element_type=jnp.float32)
        unused, gelu_back = jax.vjp(partial(jax.nn.gelu, approximate=False), pre_act)
        pre_grad = gelu_back(act_grad)[0]
        pre_low = pre_grad.astype(jnp.bfloat16)
        backward_up_grad = jnp.einsum(
            "tbd,tbf->df", mlp_in, pre_low, preferred_element_type=jnp.float32
        )
        mlp_in_grad = lax.psum_scatter(
            jnp.einsum("tbf,df->tbd", pre_low, up_own, preferred_element_type=jnp.float32).astype(
                jnp.bfloat16
            ),
            "mp",
            scatter_dimension=0,
            tiled=True,
        ).astype(jnp.float32)
        unused, second_back = jax.vjp(layer_norm, hidden_rows, gain_second, shift_second)
        hidden_from_norm, backward_gain_second_grad, backward_shift_second_grad = second_back(
            mlp_in_grad
        )
        hidden_grad = grad_rows + hidden_from_norm
        update_grad = (1.0 - gate) * state_grad
        backward_gate_grad = jnp.sum(
            state_grad * (state_in - update_rows) * gate * (1.0 - gate), axis=(0, 1)
        )
        branch_all = lax.all_gather(hidden_grad.astype(jnp.bfloat16), "mp", axis=0, tiled=True)
        update_all = lax.all_gather(update_grad.astype(jnp.bfloat16), "mp", axis=0, tiled=True)
        backward_out_grad = jnp.einsum(
            "tbc,tbd->cd", attended, branch_all, preferred_element_type=jnp.float32
        )
        attended_grad = jnp.einsum(
            "tbd,cd->tbc", branch_all, out_own, preferred_element_type=jnp.float32
        )
        backward_state_out_grad = jnp.einsum(
            "tbc,tbd->cd", recalled, update_all, preferred_element_type=jnp.float32
        )
        recalled_grad = jnp.einsum(
            "tbd,cd->tbc", update_all, w_state_out, preferred_element_type=jnp.float32
        )
        backward_query_g = to_groups(split_heads(projected[0]))
        backward_key_cur4 = split_heads(projected[1])
        value_cur4 = split_heads(projected[2])
        backward_key_band = band_of(split_heads(jnp.concatenate([key_prev, projected[1]], axis=0)))
        value_band = band_of(split_heads(jnp.concatenate([value_prev, projected[2]], axis=0)))
        backward_state_query4 = split_heads(state_projected[0])
        backward_state_key4 = split_heads(state_projected[1])
        state_value4 = split_heads(state_projected[2])
        backward_valid_win = jnp.concatenate([valid_prev, valid_cur], axis=0)
        backward_window_logits, backward_state_logits = attention_logits(
            backward_query_g, backward_key_band, backward_state_key4, backward_valid_win
        )
        window_probs = jnp.exp(backward_window_logits - token_lse)
        state_probs = jnp.exp(backward_state_logits - token_lse)
        attended_g = to_groups(split_heads(attended_grad.astype(jnp.bfloat16)))
        window_dp = jnp.einsum(
            "gqbhe,gkbhe->gbhqk", attended_g, value_band, preferred_element_type=jnp.float32
        )
        state_dp = jnp.einsum(
            "gqbhe,kbhe->gbhqk", attended_g, state_value4, preferred_element_type=jnp.float32
        )
        weighted = jnp.sum(window_probs * window_dp, axis=-1, keepdims=True) + jnp.sum(
            state_probs * state_dp, axis=-1, keepdims=True
        )
        window_dl = window_probs * (window_dp - weighted)
        state_dl = state_probs * (state_dp - weighted)
        backward_rel_grad = jnp.dot(
            bucket_onehot.T,
            diagonal_sums(jnp.sum(window_dl, axis=(0, 1)), block_len).T,
            precision=highest,
            preferred_element_type=jnp.float32,
        )
        window_low = (window_dl * scale_factor).astype(jnp.bfloat16)
        state_low = (state_dl * scale_factor).astype(jnp.bfloat16)
        query_grad = jnp.einsum(
            "gbhqk,gkbhe->gqbhe", window_low, backward_key_band, preferred_element_type=jnp.float32
        )
        query_grad = from_groups(
            query_grad
            + jnp.einsum(
                "gbhqk,kbhe->gqbhe",
                state_low,
                backward_state_key4,
                preferred_element_type=jnp.float32,
            )
        )
        key_win_grad = unband(
            jnp.einsum(
                "gbhqk,gqbhe->gkbhe",
                window_low,
                backward_query_g,
                preferred_element_type=jnp.float32,
            )
        )
        state_key_grad = jnp.einsum(
            "gbhqk,gqbhe->kbhe", state_low, backward_query_g, preferred_element_type=jnp.float32
        )
        value_win_grad = unband(
            jnp.einsum(
                "gbhqk,gqbhe->gkbhe",
                window_probs.astype(jnp.bfloat16),
                attended_g,
                preferred_element_type=jnp.float32,
            )
        )
        state_value_grad = jnp.einsum(
            "gbhqk,gqbhe->kbhe",
            state_probs.astype(jnp.bfloat16),
            attended_g,
            preferred_element_type=jnp.float32,
        )
        recur_logits = recur_logits_of(backward_state_query4, backward_key_cur4, valid_cur)
        recur_probs = jnp.exp(recur_logits - recur_lse)
        recalled_low = split_heads(recalled_grad.astype(jnp.bfloat16))
        recur_dp = jnp.einsum(
            "sbhe,kbhe->bhsk", recalled_low, value_cur4, preferred_element_type=jnp.float32
        )
        recur_dl = recur_probs * (
            recur_dp - jnp.sum(recur_probs * recur_dp, axis=-1, keepdims=True)
        )
        recur_low = (recur_dl * scale_factor).astype(jnp.bfloat16)
        state_query_grad = jnp.einsum(
            "bhsk,kbhe->sbhe", recur_low, backward_key_cur4, preferred_element_type=jnp.float32
        )
        key_cur_extra = jnp.einsum(
            "bhsk,sbhe->kbhe", recur_low, backward_state_query4, preferred_element_type=jnp.float32
        )
        value_cur_extra = jnp.einsum(
            "bhsk,sbhe->kbhe",
            recur_probs.astype(jnp.bfloat16),
            recalled_low,
            preferred_element_type=jnp.float32,
        )
        key_cur_grad = merge_heads(key_win_grad[block_len:] + key_cur_extra) + key_grad_next
        value_cur_grad = merge_heads(value_win_grad[block_len:] + value_cur_extra) + value_grad_next
        key_prev_grad = merge_heads(key_win_grad[:block_len])
        value_prev_grad = merge_heads(value_win_grad[:block_len])
        token_low = jnp.stack([merge_heads(query_grad), key_cur_grad, value_cur_grad]).astype(
            jnp.bfloat16
        )
        state_low_all = jnp.stack(
            [
                merge_heads(state_query_grad),
                merge_heads(state_key_grad),
                merge_heads(state_value_grad),
            ]
        ).astype(jnp.bfloat16)
        backward_qkv_grad = jnp.einsum(
            "tbd,jtbc->jdc", normed, token_low, preferred_element_type=jnp.float32
        )
        backward_state_qkv_grad = jnp.einsum(
            "tbd,jtbc->jdc", state_normed, state_low_all, preferred_element_type=jnp.float32
        )
        normed_grad = jnp.einsum(
            "jtbc,jdc->tbd", token_low, qkv_own, preferred_element_type=jnp.float32
        )
        state_normed_grad = jnp.einsum(
            "jtbc,jdc->tbd", state_low_all, w_state_qkv, preferred_element_type=jnp.float32
        )
        normed_rows_grad = lax.psum_scatter(
            normed_grad.astype(jnp.bfloat16), "mp", scatter_dimension=0, tiled=True
        ).astype(jnp.float32)
        state_rows_grad = lax.psum_scatter(
            state_normed_grad.astype(jnp.bfloat16), "mp", scatter_dimension=0, tiled=True
        ).astype(jnp.float32)
        unused, first_back = jax.vjp(layer_norm, rows_in, gain_first, shift_first)
        rows_from_norm, backward_gain_first_grad, backward_shift_first_grad = first_back(
            normed_rows_grad
        )
        unused, state_back = jax.vjp(layer_norm, state_in, state_gain, state_shift)
        state_from_norm, backward_state_gain_grad, backward_state_shift_grad = state_back(
            state_rows_grad
        )
        input_grad = hidden_grad + rows_from_norm
        state_prev_grad = gate * state_grad + state_from_norm
        grads = (
            backward_gain_first_grad,
            backward_gain_second_grad,
            backward_shift_first_grad,
            backward_shift_second_grad,
            jnp.sum(grad_rows, axis=(0, 1)),
            backward_qkv_grad,
            backward_out_grad,
            backward_rel_grad,
            backward_up_grad,
            jnp.sum(pre_grad, axis=(0, 1)),
            backward_down_grad,
            backward_state_gain_grad,
            backward_state_shift_grad,
            backward_state_qkv_grad,
            backward_state_out_grad,
            backward_gate_grad,
        )
        input_grad, state_prev_grad, key_prev_grad, value_prev_grad, grads = (
            input_grad,
            state_prev_grad,
            key_prev_grad,
            value_prev_grad,
            grads,
        )
        active_scale = active.astype(jnp.float32)

        def scale_grad(grad_part):
            return active_scale * grad_part

        scaled = jax.tree.map(scale_grad, grads)
        totals = scaled if totals is None else jax.tree.map(jnp.add, totals, scaled)
        input_grads = jnp.where(
            active,
            lax.dynamic_update_index_in_dim(input_grads, input_grad, block_safe, 0),
            input_grads,
        )
        state_grad = jnp.where(active, state_prev_grad, state_grad)
        key_grad_next = jnp.where(active, key_prev_grad, key_grad_next)
        value_grad_next = jnp.where(active, value_prev_grad, value_grad_next)
        if step_index < block_count:
            grad_in = from_behind(input_grad.astype(jnp.bfloat16), "section", -1).astype(
                jnp.float32
            )
    (
        gain_first_grad,
        gain_second_grad,
        shift_first_grad,
        shift_second_grad,
        down_bias_grad,
        qkv_grad,
        out_grad,
        rel_grad,
        up_grad,
        up_bias_grad,
        down_grad,
        state_gain_grad,
        state_shift_grad,
        state_qkv_grad,
        state_out_grad,
        gate_grad,
    ) = totals
    qkv_sum, out_sum, rel_sum, up_sum, up_bias_sum, down_sum = (
        lax.psum(qkv_grad.astype(jnp.bfloat16), "dp").astype(jnp.float32),
        lax.psum(out_grad.astype(jnp.bfloat16), "dp").astype(jnp.float32),
        lax.psum(rel_grad.astype(jnp.bfloat16), "dp").astype(jnp.float32),
        lax.psum(up_grad.astype(jnp.bfloat16), "dp").astype(jnp.float32),
        lax.psum(up_bias_grad.astype(jnp.bfloat16), "dp").astype(jnp.float32),
        lax.psum(down_grad.astype(jnp.bfloat16), "dp").astype(jnp.float32),
    )
    state_qkv_doc, state_out_doc = (
        lax.psum(state_qkv_grad.astype(jnp.bfloat16), "dp").astype(jnp.float32),
        lax.psum(state_out_grad.astype(jnp.bfloat16), "dp").astype(jnp.float32),
    )
    state_qkv_moved, state_out_moved = (
        from_behind(state_qkv_doc.astype(jnp.bfloat16), "section", -1).astype(state_qkv_doc.dtype),
        from_behind(state_out_doc.astype(jnp.bfloat16), "section", -1).astype(state_out_doc.dtype),
    )
    state_qkv_sum = jnp.where(is_rec, state_qkv_doc, state_qkv_moved)
    state_out_sum = jnp.where(is_rec, state_out_doc, state_out_moved)
    layer_small = jnp.stack(
        [gain_first_grad, gain_second_grad, shift_first_grad, shift_second_grad, down_bias_grad]
    )
    slotted = jnp.where((jnp.arange(2) == section_now)[:, None, None], layer_small[None], 0.0)
    state_small = jnp.stack([state_gain_grad, state_shift_grad, gate_grad])
    slot_sum, state_small_sum = lax.psum((slotted, state_small), ("section", "mp", "dp"))
    own_small = lax.dynamic_index_in_dim(slot_sum, section_now, 0, keepdims=False)
    return (
        acts_out[None],
        input_grads[None],
        final_state,
        jnp.stack([own_small[0], own_small[1]])[None],
        jnp.stack([own_small[2], own_small[3]])[None],
        qkv_sum[None],
        out_sum[None],
        rel_sum[None],
        up_sum[None],
        up_bias_sum[None],
        down_sum[None],
        own_small[4][None],
        state_small_sum[0],
        state_small_sum[1],
        state_qkv_sum,
        state_out_sum,
        state_small_sum[2],
    )


def solution(mesh):
    in_specs = (
        P(None, "mp", "dp", None),
        P(None, None, "dp"),
        P(),
        P("mp", "dp", None),
        P("section", None, None),
        P("section", None, None),
        P("section", None, None, "mp"),
        P("section", "mp", None),
        P("section", None, "mp"),
        P("section", None, "mp"),
        P("section", "mp"),
        P("section", "mp", None),
        P("section", None),
        P(),
        P(),
        P(None, None, "mp"),
        P("mp", None),
        P(),
        P(None, "mp", "dp", None),
    )
    out_specs = (
        P("section", None, "mp", "dp", None),
        P("section", None, "mp", "dp", None),
        P("mp", "dp", None),
        P("section", None, None),
        P("section", None, None),
        P("section", None, None, "mp"),
        P("section", "mp", None),
        P("section", None, "mp"),
        P("section", None, "mp"),
        P("section", "mp"),
        P("section", "mp", None),
        P("section", None),
        P(),
        P(),
        P(None, None, "mp"),
        P("mp", None),
        P(),
    )
    return jax.shard_map(local, mesh=mesh, in_specs=in_specs, out_specs=out_specs, check_vma=False)
```

profile of v0, /device:TPU:0, one launch (start us, length us, event | category | flops | bytes accessed | tf_op | source)
XLA Modules:
  0.0 1936.6 jit_solution(13073407334515424284)
XLA Ops:
  28.1 11.5 concatenate.93
  39.7 12.9 reshape.3244
  52.6 10.6 reshape.3145
  66.6 4.9 copy.1062
  126.8 33.6 %reduce-scatter.16.cloned.1.call-done = bf16[512,1,1024]{2,0,1:T(8,128)(2,1)} async-done(((bf16[1024,1,1024]{2,0,1:T(8,128)(2,1)}), bf16[512,1,1024]{2,0,1:T(8,128)(2,1)}) %reduce-scatter.16.cloned.1.call-update) | async-done | bytes 1048592 | tf_op jit(solution)/shard_map/reduce_scatter | solution.py:247
  168.0 21.4 %all-gather.23.cloned.1.call-done = bf16[512,1,1024]{2,0,1:T(8,128)(2,1)} async-done(((bf16[256,1,1024]{2,0,1:T(8,128)(2,1)}), bf16[512,1,1024]{2,0,1:T(8,128)(2,1)}) %all-gather.23.cloned.1.call-update) | async-done | bytes 1048592 | tf_op jit(solution)/shard_map/all_gather | solution.py:259
  189.4 15.0 multiply_convert_fusion.8
  209.1 20.4 %reduce-scatter.18.cloned.1.call-done = bf16[256,1,1024]{2,0,1:T(8,128)(2,1)} async-done(((bf16[512,1,1024]{2,0,1:T(8,128)(2,1)}), bf16[256,1,1024]{2,0,1:T(8,128)(2,1)}) %reduce-scatter.18.cloned.1.call-update) | async-done | bytes 524304 | tf_op jit(solution)/shard_map/reduce_scatter | solution.py:267
  242.7 15.9 all-gather.27.cloned.1.call-done
  263.9 18.1 all-gather.25.cloned.1.call-done
  333.7 31.9 %reduce-scatter.20.cloned.1.call-done = bf16[512,1,1024]{2,0,1:T(8,128)(2,1)} async-done(((bf16[1024,1,1024]{2,0,1:T(8,128)(2,1)}), bf16[512,1,1024]{2,0,1:T(8,128)(2,1)}) %reduce-scatter.20.cloned.1.call-update) | async-done | bytes 1048592 | tf_op jit(solution)/shard_map/reduce_scatter | solution.py:247
  373.4 21.4 %all-gather.29.cloned.1.call-done = bf16[512,1,1024]{2,0,1:T(8,128)(2,1)} async-done(((bf16[256,1,1024]{2,0,1:T(8,128)(2,1)}), bf16[512,1,1024]{2,0,1:T(8,128)(2,1)}) %all-gather.29.cloned.1.call-update) | async-done | bytes 1048592 | tf_op jit(solution)/shard_map/all_gather | solution.py:259
  394.8 15.0 multiply_convert_fusion.7
  414.6 20.4 %reduce-scatter.22.cloned.1.call-done = bf16[256,1,1024]{2,0,1:T(8,128)(2,1)} async-done(((bf16[512,1,1024]{2,0,1:T(8,128)(2,1)}), bf16[256,1,1024]{2,0,1:T(8,128)(2,1)}) %reduce-scatter.22.cloned.1.call-update) | async-done | bytes 524304 | tf_op jit(solution)/shard_map/reduce_scatter | solution.py:267
  448.5 15.9 all-gather.33.cloned.1.call-done
  469.7 18.0 all-gather.31.cloned.1.call-done
  537.4 31.9 %reduce-scatter.24.cloned.1.call-done = bf16[512,1,1024]{2,0,1:T(8,128)(2,1)} async-done(((bf16[1024,1,1024]{2,0,1:T(8,128)(2,1)}), bf16[512,1,1024]{2,0,1:T(8,128)(2,1)}) %reduce-scatter.24.cloned.1.call-update) | async-done | bytes 1048592 | tf_op jit(solution)/shard_map/reduce_scatter | solution.py:247
  579.6 18.8 all-gather.35.cloned.1.call-done
  598.4 15.2 multiply_convert_fusion.6
  613.6 8.2 all-gather.37.cloned.1.call-done
  621.8 9.4 fusion.702
  636.9 19.5 %reduce-scatter.28.cloned.1.call-done = bf16[256,1,1024]{2,0,1:T(8,128)(2,1)} async-done(((bf16[512,1,1024]{2,0,1:T(8,128)(2,1)}), bf16[256,1,1024]{2,0,1:T(8,128)(2,1)}) %reduce-scatter.28.cloned.1.call-update) | async-done | bytes 524304 | tf_op jit(solution)/shard_map/reduce_scatter | solution.py:361
  662.8 16.8 all-gather.41.cloned.1.call-done
  686.6 16.4 all-gather.39.cloned.1.call-done
  712.2 5.5 multiply_reduce_fusion.2
  744.8 9.7 fusion.389
  770.0 20.2 %reduce-scatter.30.cloned.1.call-done = bf16[256,1,1024]{2,0,1:T(8,128)(2,1)} async-done(((bf16[512,1,1024]{2,0,1:T(8,128)(2,1)}), bf16[256,1,1024]{2,0,1:T(8,128)(2,1)}) %reduce-scatter.30.cloned.1.call-update) | async-done | bytes 524304 | tf_op jit(solution)/shard_map/reduce_scatter | solution.py:511
  800.1 9.2 fusion.434
  825.2 5.2 fusion.296
  830.9 5.7 all-gather.43.cloned.1.call-done
  836.6 9.4 fusion.701
  854.9 4.9 reduce-scatter.34.cloned.1.call-done
  866.7 16.3 reduce-scatter.32.cloned.1.call-done
  891.5 15.1 all-gather.47.cloned.1.call-done
  913.5 16.5 all-gather.45.cloned.1.call-done
  939.2 5.5 multiply_reduce_fusion.1
  945.8 4.9 fusion.254
  971.0 9.9 fusion.404
  997.2 20.2 %reduce-scatter.36.cloned.1.call-done = bf16[256,1,1024]{2,0,1:T(8,128)(2,1)} async-done(((bf16[512,1,1024]{2,0,1:T(8,128)(2,1)}), bf16[256,1,1024]{2,0,1:T(8,128)(2,1)}) %reduce-scatter.36.cloned.1.call-update) | async-done | bytes 524304 | tf_op jit(solution)/shard_map/reduce_scatter | solution.py:511
  1024.2 9.1 fusion.431
  1050.3 5.2 fusion.300
  1056.1 5.6 all-gather.49.cloned.1.call-done
  1061.7 8.8 fusion.700
  1075.2 9.5 reduce-scatter.40.cloned.1.call-done
  1091.5 16.5 reduce-scatter.38.cloned.1.call-done
  1118.3 6.1 fusion.275
  1124.7 7.7 fusion.507
  1132.5 5.8 fusion.510
  1151.5 5.7 fusion.498
  1157.3 6.0 fusion.519
  1181.4 8.9 fusion.428
  1197.0 12.3 fusion.79
  1209.3 6.8 fusion.78
  1255.4 10.4 fusion.401
  1287.7 8.5 fusion.83
  1349.7 24.0 %all-reduce.31 = (bf16[1,32,4]{1,2,0:T(4,128)(2,1)S(1)}, bf16[1,2048]{1,0:T(2,128)(2,1)S(1)}) all-reduce(bf16[1,32,4]{1,2,0:T(4,128)(2,1)S(1)} %fusion.459, bf16[1,2048]{1,0:T(2,128)(2,1)S(1)} %broadcast_in_dim.432), channel_id=1, replica_groups=mesh['section'=2,'mp'=2,'dp'=8] {'dp'}, use_global_device_ids=true, to_apply=%region_99.100 | all-reduce | flops 2176 | bytes 8704 | tf_op jit(solution)/shard_map/psum | solution.py:592
  1378.5 446.6 %all-reduce.35.cloned.1.call-done = (bf16[1,3,1024,512]{2,3,1,0:T(8,128)(2,1)}, bf16[1,512,1024]{2,1,0:T(8,128)(2,1)}, bf16[1,1024,2048]{2,1,0:T(8,128)(2,1)}, b...) async-done(((bf16[1,3,1024,512]{2,3,1,0:T(8,128)(2,1)}, bf16[1,512,1024]{2,1,0:T(8,128)(2,1)}, ...) | async-done | bytes 16777232 | tf_op jit(solution)/shard_map/psum | solution.py:590
  1830.4 5.1 copy.852
  1835.6 10.9 reduce-scatter.44.cloned.1.call-done
  1850.3 41.5 %all-reduce.30 = (f32[2,5,1024]{2,1,0:T(8,128)S(1)}, f32[3,1024]{1,0:T(4,128)S(1)}) all-reduce(f32[2,5,1024]{2,1,0:T(8,128)S(1)} %broadcast_select_fusion.4, f32[3,1024]{1,0:T(4,128)S(1)} %pad_maximum_fusion.25), channel_id=1, replica_groups=mesh['section'=2,'mp'=2,'dp'=8] {'section','mp','dp'}, use_global_device_ids=true, to_apply=%region_90.91 | all-reduce | flops 13312 | bytes 106496 | tf_op jit(solution)/shard_map/psum | solution.py:612
  1894.2 6.8 broadcast_in_dim.431
  1905.5 5.4 copy.854
  1917.0 5.9 convert_select_fusion
  1923.0 6.6 copy.855
  (1022 shorter events, 650.9 us)
Async XLA Ops:
  7.2 66.0 %copy-start = (bf16[1,3,1024,512]{3,2,1,0:T(8,128)(2,1)S(1)}, bf16[1,3,1024,512]{3,2,1,0:T(8,128)(2,1)}, u32[]{:S(2)}) copy-start(bf16[1,3,1024,512]{3,2,1,0:T(8,128)(2,1)} %param.25) | copy-start | bytes 9437188
  7.2 65.9 %all-gather.19.cloned.1.call-start = ((), (), s32[]{:S(2)}) async-start(), calls=%async_computation.15 | async-start | bytes 1572864 | tf_op jit(solution)/shard_map/all_gather | solution.py:188
  14.9 75.9 %all-gather.21.cloned.1.call-start = ((), (), s32[]{:S(2)}) async-start(), calls=%async_computation.16 | async-start | bytes 1572864 | tf_op jit(solution)/shard_map/all_gather | solution.py:189
  19.7 140.8 %reduce-scatter.16.cloned.1.call-start = ((), (), s32[]{:S(2)}) async-start(), calls=%async_computation.17 | async-start | bytes 3145728 | tf_op jit(solution)/shard_map/reduce_scatter | solution.py:247
  125.8 63.6 %all-gather.23.cloned.1.call-start = ((), (), s32[]{:S(2)}) async-start(), calls=%async_computation.18 | async-start | bytes 1572864 | tf_op jit(solution)/shard_map/all_gather | solution.py:259
  163.3 26.1 %copy-start.254 = (f32[1,2048]{1,0:T(1,128)S(1)}, f32[1,2048]{1,0:T(1,128)}, u32[]{:S(2)}) copy-start(f32[1,2048]{1,0:T(1,128)} %param.29) | copy-start | bytes 24580
  165.9 38.5 %copy-start.185 = (f32[256]{0:T(256)}, f32[256]{0:T(256)S(1)}, u32[]{:S(2)}) copy-start(f32[256]{0:T(256)S(1)} %broadcast_multiply_fusion.7) | copy-start | bytes 3076
  166.1 38.2 %copy-start.223 = (f32[256]{0:T(256)}, f32[256]{0:T(256)S(1)}, u32[]{:S(2)}) copy-start(f32[256]{0:T(256)S(1)} %multiply_reduce_fusion.14) | copy-start | bytes 3076
  166.1 38.2 %copy-start.191 = (f32[256]{0:T(256)}, f32[256]{0:T(256)S(1)}, u32[]{:S(2)}) copy-start(f32[256]{0:T(256)S(1)} %fusion.632) | copy-start | bytes 3076
  167.9 61.6 %reduce-scatter.18.cloned.1.call-start = ((), (), s32[]{:S(2)}) async-start(), calls=%async_computation.19 | async-start | bytes 1572864 | tf_op jit(solution)/shard_map/reduce_scatter | solution.py:267
  205.7 24.9 %copy-start.173 = (f32[1,1024]{1,0:T(1,128)S(1)}, f32[1,1024]{1,0:T(1,128)}, u32[]{:S(2)}) copy-start(f32[1,1024]{1,0:T(1,128)} %param.31) | copy-start | bytes 12292
  209.0 27.0 %copy-start.163 = (f32[1024]{0:T(1024)S(1)}, f32[1024]{0:T(1024)}, u32[]{:S(2)}) copy-start(f32[1024]{0:T(1024)} %param.32) | copy-start | bytes 12292
  209.0 27.0 %copy-start.172 = (f32[1024]{0:T(1024)S(1)}, f32[1024]{0:T(1024)}, u32[]{:S(2)}) copy-start(f32[1024]{0:T(1024)} %param.33) | copy-start | bytes 12292
  209.0 49.5 %all-gather.27.cloned.1.call-start = ((), (), s32[]{:S(2)}) async-start(), calls=%async_computation.21 | async-start | bytes 1572864 | tf_op jit(solution)/shard_map/all_gather | solution.py:189
  209.1 31.0 %copy-start.175 = (f32[256]{0:T(256)}, f32[256]{0:T(256)S(1)}, u32[]{:S(2)}) copy-start(f32[256]{0:T(256)S(1)} %broadcast_multiply_fusion.5) | copy-start | bytes 3076
  233.2 4.0 collective-permute-start
  237.1 44.9 %all-gather.25.cloned.1.call-start = ((), (), s32[]{:S(2)}) async-start(), calls=%async_computation.20 | async-start | bytes 1572864 | tf_op jit(solution)/shard_map/all_gather | solution.py:188
  242.5 123.1 %reduce-scatter.20.cloned.1.call-start = ((), (), s32[]{:S(2)}) async-start(), calls=%async_computation.22 | async-start | bytes 3145728 | tf_op jit(solution)/shard_map/reduce_scatter | solution.py:247
  333.6 61.2 %all-gather.29.cloned.1.call-start = ((), (), s32[]{:S(2)}) async-start(), calls=%async_computation.23 | async-start | bytes 1572864 | tf_op jit(solution)/shard_map/all_gather | solution.py:259
  371.3 38.6 %copy-start.177 = (f32[256]{0:T(256)}, f32[256]{0:T(256)S(1)}, u32[]{:S(2)}) copy-start(f32[256]{0:T(256)S(1)} %broadcast_multiply_fusion.4) | copy-start | bytes 3076
  371.5 38.3 %copy-start.229 = (f32[256]{0:T(256)}, f32[256]{0:T(256)S(1)}, u32[]{:S(2)}) copy-start(f32[256]{0:T(256)S(1)} %multiply_reduce_fusion.11) | copy-start | bytes 3076
  372.3 37.6 %copy-start.195 = (f32[256]{0:T(256)}, f32[256]{0:T(256)S(1)}, u32[]{:S(2)}) copy-start(f32[256]{0:T(256)S(1)} %fusion.635) | copy-start | bytes 3076
  373.3 61.6 %reduce-scatter.22.cloned.1.call-start = ((), (), s32[]{:S(2)}) async-start(), calls=%async_computation.24 | async-start | bytes 1572864 | tf_op jit(solution)/shard_map/reduce_scatter | solution.py:267
  414.5 49.9 %all-gather.33.cloned.1.call-start = ((), (), s32[]{:S(2)}) async-start(), calls=%async_computation.26 | async-start | bytes 1572864 | tf_op jit(solution)/shard_map/all_gather | solution.py:189
  414.6 31.4 %copy-start.189 = (f32[256]{0:T(256)}, f32[256]{0:T(256)S(1)}, u32[]{:S(2)}) copy-start(f32[256]{0:T(256)S(1)} %broadcast_multiply_fusion.2) | copy-start | bytes 3076
  437.8 5.2 collective-permute-start.1
  441.8 26.6 %copy-start.231 = (f32[256]{0:T(256)}, f32[256]{0:T(256)S(1)}, u32[]{:S(2)}) copy-start(f32[256]{0:T(256)S(1)} %multiply_reduce_fusion.9) | copy-start | bytes 3076
  441.9 26.6 %copy-start.212 = (f32[256]{0:T(256)}, f32[256]{0:T(256)S(1)}, u32[]{:S(2)}) copy-start(f32[256]{0:T(256)S(1)} %fusion.637) | copy-start | bytes 3076
  442.9 44.8 %all-gather.31.cloned.1.call-start = ((), (), s32[]{:S(2)}) async-start(), calls=%async_computation.25 | async-start | bytes 1572864 | tf_op jit(solution)/shard_map/all_gather | solution.py:188
  448.3 121.1 %reduce-scatter.24.cloned.1.call-start = ((), (), s32[]{:S(2)}) async-start(), calls=%async_computation.27 | async-start | bytes 3145728 | tf_op jit(solution)/shard_map/reduce_scatter | solution.py:247
  537.4 61.0 %all-gather.35.cloned.1.call-start = ((), (), s32[]{:S(2)}) async-start(), calls=%async_computation.28 | async-start | bytes 1572864 | tf_op jit(solution)/shard_map/all_gather | solution.py:259
  576.9 44.8 %all-gather.37.cloned.1.call-start = ((), (), s32[]{:S(2)}) async-start(), calls=%async_computation.30 | async-start | bytes 1572864 | tf_op jit(solution)/shard_map/all_gather | solution.py:350
  579.6 76.8 %reduce-scatter.28.cloned.1.call-start = ((), (), s32[]{:S(2)}) async-start(), calls=%async_computation.31 | async-start | bytes 1572864 | tf_op jit(solution)/shard_map/reduce_scatter | solution.py:361
  635.9 43.8 %all-gather.41.cloned.1.call-start = ((), (), s32[]{:S(2)}) async-start(), calls=%async_computation.33 | async-start | bytes 1572864 | tf_op jit(solution)/shard_map/all_gather | solution.py:379
  636.8 66.2 %all-gather.39.cloned.1.call-start = ((), (), s32[]{:S(2)}) async-start(), calls=%async_computation.32 | async-start | bytes 1572864 | tf_op jit(solution)/shard_map/all_gather | solution.py:378
  662.6 127.6 %reduce-scatter.30.cloned.1.call-start = ((), (), s32[]{:S(2)}) async-start(), calls=%async_computation.34 | async-start | bytes 1572864 | tf_op jit(solution)/shard_map/reduce_scatter | solution.py:511
  769.8 66.8 %all-gather.43.cloned.1.call-start = ((), (), s32[]{:S(2)}) async-start(), calls=%async_computation.35 | async-start | bytes 1572864 | tf_op jit(solution)/shard_map/all_gather | solution.py:350
  798.8 12.5 collective-permute-start.2
  813.6 46.3 %reduce-scatter.34.cloned.1.call-start = ((), (), s32[]{:S(2)}) async-start(), calls=%async_computation.38 | async-start | bytes 1572864 | tf_op jit(solution)/shard_map/reduce_scatter | solution.py:514
  830.4 52.6 %reduce-scatter.32.cloned.1.call-start = ((), (), s32[]{:S(2)}) async-start(), calls=%async_computation.36 | async-start | bytes 1572864 | tf_op jit(solution)/shard_map/reduce_scatter | solution.py:361
  850.7 55.9 %all-gather.47.cloned.1.call-start = ((), (), s32[]{:S(2)}) async-start(), calls=%async_computation.39 | async-start | bytes 1572864 | tf_op jit(solution)/shard_map/all_gather | solution.py:379
  850.8 4.1 collective-permute-start.4
  866.7 24.8 %copy-start.166 = (f32[4,4,128]{2,1,0:T(4,128)S(1)}, f32[4,4,128]{2,1,0:T(4,128)}, u32[]{:S(2)}) copy-start(f32[4,4,128]{2,1,0:T(4,128)} %get-tuple-element.157) | copy-start | bytes 24580
  866.7 24.9 %copy-start.171 = (f32[4,512]{1,0:T(4,128)S(1)}, f32[4,512]{1,0:T(4,128)}, u32[]{:S(2)}) copy-start(f32[4,512]{1,0:T(4,128)} %copy-done.170) | copy-start | bytes 24580
  866.7 24.9 %copy-start.184 = (f32[4,512]{1,0:T(4,128)S(1)}, f32[4,512]{1,0:T(4,128)}, u32[]{:S(2)}) copy-start(f32[4,512]{1,0:T(4,128)} %copy-done.183) | copy-start | bytes 24580
  866.7 63.3 %all-gather.45.cloned.1.call-start = ((), (), s32[]{:S(2)}) async-start(), calls=%async_computation.37 | async-start | bytes 1572864 | tf_op jit(solution)/shard_map/all_gather | solution.py:378
  891.3 126.1 %reduce-scatter.36.cloned.1.call-start = ((), (), s32[]{:S(2)}) async-start(), calls=%async_computation.40 | async-start | bytes 1572864 | tf_op jit(solution)/shard_map/reduce_scatter | solution.py:511
  992.7 24.7 %copy-start.211 = (f32[256]{0:T(256)S(1)}, f32[256]{0:T(256)}, u32[]{:S(2)}) copy-start(f32[256]{0:T(256)} %copy-done.210) | copy-start | bytes 3076
  992.7 27.2 %copy-start.228 = (f32[256]{0:T(256)S(1)}, f32[256]{0:T(256)}, u32[]{:S(2)}) copy-start(f32[256]{0:T(256)} %copy-done.227) | copy-start | bytes 3076
  996.9 64.8 %all-gather.49.cloned.1.call-start = ((), (), s32[]{:S(2)}) async-start(), calls=%async_computation.41 | async-start | bytes 1572864 | tf_op jit(solution)/shard_map/all_gather | solution.py:350
  1022.9 12.5 collective-permute-start.3
  1038.7 46.0 %reduce-scatter.40.cloned.1.call-start = ((), (), s32[]{:S(2)}) async-start(), calls=%async_computation.44 | async-start | bytes 1572864 | tf_op jit(solution)/shard_map/reduce_scatter | solution.py:514
  1055.5 52.4 %reduce-scatter.38.cloned.1.call-start = ((), (), s32[]{:S(2)}) async-start(), calls=%async_computation.42 | async-start | bytes 1572864 | tf_op jit(solution)/shard_map/reduce_scatter | solution.py:361
  1075.2 99.4 %all-gather.53.cloned.1.call-start = ((), (), s32[]{:S(2)}) async-start(), calls=%async_computation.45 | async-start | bytes 1572864 | tf_op jit(solution)/shard_map/all_gather | solution.py:379
  1091.4 124.7 %all-gather.51.cloned.1.call-start = ((), (), s32[]{:S(2)}) async-start(), calls=%async_computation.43 | async-start | bytes 1572864 | tf_op jit(solution)/shard_map/all_gather | solution.py:378
  1114.7 187.8 %reduce-scatter.26.cloned.1.call-start = ((), (), s32[]{:S(2)}) async-start(), calls=%async_computation.29 | async-start | bytes 1572864 | tf_op jit(solution)/shard_map/reduce_scatter | solution.py:267
  1124.5 250.5 %reduce-scatter.42.cloned.1.call-start = ((), (), s32[]{:S(2)}) async-start(), calls=%async_computation.46 | async-start | bytes 1572864 | tf_op jit(solution)/shard_map/reduce_scatter | solution.py:511
  1282.9 542.2 %all-reduce.35.cloned.1.call-start = ((), (), s32[]{:S(2)}) async-start(), calls=%async_computation.48 | async-start | bytes 33554432 | tf_op jit(solution)/shard_map/psum | solution.py:590
  1300.1 546.3 %reduce-scatter.44.cloned.1.call-start = ((), (), s32[]{:S(2)}) async-start(), calls=%async_computation.47 | async-start | bytes 1572864 | tf_op jit(solution)/shard_map/reduce_scatter | solution.py:514
  1339.8 35.1 %copy-start.180 = (f32[256]{0:T(256)S(1)}, f32[256]{0:T(256)}, u32[]{:S(2)}) copy-start(f32[256]{0:T(256)} %copy-done.179) | copy-start | bytes 3076
  1342.0 34.6 %copy-start.220 = (f32[256]{0:T(256)S(1)}, f32[256]{0:T(256)}, u32[]{:S(2)}) copy-start(f32[256]{0:T(256)} %copy-done.219) | copy-start | bytes 3076
  1342.0 34.6 %copy-start.218 = (f32[256]{0:T(256)S(1)}, f32[256]{0:T(256)}, u32[]{:S(2)}) copy-start(f32[256]{0:T(256)} %copy-done.217) | copy-start | bytes 3076
  1825.1 91.9 %collective-permute-start.5 = (bf16[3,1024,512]{1,2,0:T(8,128)(2,1)}, bf16[3,1024,512]{1,2,0:T(8,128)(2,1)}, u32[]{:S(2)}, u32[]{:S(2)}) collective-permute-start(bf16[3,1024,512]{1,2,0:T(8,128)(2,1)} %get-tuple-element.147), channel_id=1, source_target_pairs={{16,0},{17,1},{18,2},{19,3},{20,4},{21,5},{22,6},{23,7},{24,8},{25... | collective-permute-start | bytes 9437192 | tf_op jit(solution)/shard_map/ppermute | solution.py:17
  1848.9 64.9 %collective-permute-start.6 = (bf16[512,1024]{1,0:T(8,128)(2,1)}, bf16[512,1024]{1,0:T(8,128)(2,1)}, u32[]{:S(2)}, u32[]{:S(2)}) collective-permute-start(bf16[512,1024]{1,0:T(8,128)(2,1)} %get-tuple-element.148), channel_id=1, source_target_pairs={{16,0},{17,1},{18,2},{19,3},{20,4},{21,5},{22,6},{23,7},{24,8},{25... | collective-permute-start | bytes 3145736 | tf_op jit(solution)/shard_map/ppermute | solution.py:17
  (256 other events, 1553.7 us)
Sparse Core Ops, SparseCore 0:
  15.0 23.9 all-gather.18
  41.2 21.4 all-gather.20
  125.9 34.5 reduce-scatter.15
  168.0 21.2 all-gather.22
  209.2 20.3 reduce-scatter.17
  237.2 21.2 all-gather.26
  260.7 21.2 all-gather.24
  333.7 31.8 reduce-scatter.19
  373.5 21.3 all-gather.28
  414.6 20.3 reduce-scatter.21
  443.1 21.2 all-gather.32
  466.4 21.2 all-gather.30
  537.5 31.8 reduce-scatter.23
  577.1 21.2 all-gather.34
  600.5 21.2 all-gather.36
  636.0 20.3 reduce-scatter.27
  658.3 21.2 all-gather.40
  681.6 21.2 all-gather.38
  769.9 20.3 reduce-scatter.29
  813.7 22.8 all-gather.42
  839.5 20.3 reduce-scatter.33
  862.7 20.3 reduce-scatter.31
  885.3 21.2 all-gather.46
  908.6 21.2 all-gather.44
  997.0 20.3 reduce-scatter.35
  1038.8 22.8 all-gather.48
  1064.4 20.3 reduce-scatter.39
  1087.6 20.3 reduce-scatter.37
  1110.1 21.2 all-gather.52
  1132.8 21.2 all-gather.50
  1156.4 20.3 reduce-scatter.25
  1283.0 20.4 reduce-scatter.41
  1309.4 515.6 all-reduce.34
  1827.3 19.0 reduce-scatter.43
where the time goes:
time: 1950 us; the launch traced here: 1940 us
  waiting for transfers between devices  920 us (47%)
  matrix products  442 us (23%)
  local copies, waits for them, and re-layouts  281 us (14%)
  other arithmetic  194 us (10%)
  blocking collectives  65.5 us (3%)
    psum x1, waiting for transfers between devices, local(): lax.psum(qkv_grad.astype(jnp.bfloat16), 'dp').astype(jnp.float32)  447 us
    reduce_scatter x3, waiting for transfers between devices, local(): lax.psum_scatter(jnp.concatenate([token_term, state_term], axis=1).reshap...  97.5 us
    unnamed x570, local copies, waits for them, and re-layouts  84.5 us
    all_gather x3, waiting for transfers between devices, local(): forward_mlp_in = lax.all_gather(mlp_loc, 'mp', axis=0, tiled=True)  61.6 us
    reduce_scatter x3, waiting for transfers between devices, local(): lax.psum_scatter(jnp.einsum('tbf,df->tbd', pre_low, up_own, preferred_ele...  52.3 us
    dot_general x3, matrix products, local(): jnp.einsum('tbd,df->tbf', forward_mlp_in, up_own, preferred_element_type=...  45.2 us
    psum x1, blocking collectives, local(): lax.psum((slotted, state_small), ('section', 'mp', 'dp'))  41.5 us
    reduce_scatter x3, waiting for transfers between devices, local(): lax.psum_scatter(jnp.einsum('tbf,fd->tbd', forward_activated, down_own, p...  40.8 us
  transfers between devices with their start and end apart: 41, of which 29 were waited for; matrix products, arithmetic and copies ran while one was open for 26% of the time, Pallas kernels for 0%

commit v1 on v0

v1 whole, which is shorter than its diff:
```python
from functools import partial
from types import SimpleNamespace

import jax
import jax.numpy as jnp
from jax import lax
from jax.experimental import pallas as pl
from jax.experimental.pallas import tpu as pltpu
from jax.sharding import PartitionSpec as P

MESH = pl.DeviceIdType.MESH
f32, bf16 = jnp.float32, jnp.bfloat16
eps = 1e-05
negative = -1000000000.0
VMEM_LIMIT = 60 * 1024 * 1024


def dot(left, right):
    return lax.dot_general(left, right, (((1,), (0,)), ((), ())), preferred_element_type=f32)


def dot_nt(left, right):
    return lax.dot_general(left, right, (((1,), (1,)), ((), ())), preferred_element_type=f32)


def dot_tn(left, right):
    return lax.dot_general(left, right, (((0,), (0,)), ((), ())), preferred_element_type=f32)


def norm_parts(values):
    average = jnp.mean(values, axis=-1, keepdims=True)
    centered = values - average
    spread = jnp.mean(centered * centered, axis=-1, keepdims=True)
    scale = lax.rsqrt(spread + eps)
    return centered * scale, scale


def layer_norm(values, gain, shift):
    return norm_parts(values)[0] * gain + shift


class Place:
    def __init__(self, rows):
        self.c, self.x = lax.axis_index("section"), lax.axis_index("mp")
        self.core = {"section": 1 - self.c}
        self.chip = {"mp": 1 - self.x}
        self.quarter, self.half = rows // 4, rows // 2

    def rows(self, x_other=False, c_other=False):
        x = 1 - self.x if x_other else self.x
        c = 1 - self.c if c_other else self.c
        return pl.ds(pl.multiple_of(x * self.half + c * self.quarter, self.quarter), self.quarter)

    def chip_rows(self, x_other=False):
        x = 1 - self.x if x_other else self.x
        return pl.ds(pl.multiple_of(x * self.half, self.half), self.half)

    def core_rows(self, c_other=False):
        c = 1 - self.c if c_other else self.c
        return pl.ds(pl.multiple_of(c * self.quarter, self.quarter), self.quarter)

    def meet(self):
        barrier = pltpu.get_barrier_semaphore()
        for other in (self.core, self.chip):
            pl.semaphore_signal(barrier, inc=1, device_id=other, device_id_type=MESH)
        pl.semaphore_wait(barrier, 2)


class Net:
    def __init__(self, send_sems, recv_sems):
        self.send_sems, self.recv_sems, self.copies = send_sems, recv_sems, []

    def copy(self, source, target, device):
        index = len(self.copies)
        made = pltpu.make_async_remote_copy(
            src_ref=source,
            dst_ref=target,
            send_sem=self.send_sems.at[index],
            recv_sem=self.recv_sems.at[index],
            device_id=device,
            device_id_type=MESH,
        )
        made.start()
        self.copies.append(made)
        return made

    def drain(self):
        for made in self.copies:
            made.wait_send()


class Local:
    def __init__(self, sems):
        self.sems, self.copies, self.waited = sems, [], set()

    def copy(self, source, target):
        made = pltpu.make_async_copy(source, target, self.sems.at[len(self.copies)])
        made.start()
        self.copies.append(made)
        return len(self.copies) - 1

    def wait(self, *indices):
        for index in indices:
            if index not in self.waited:
                self.waited.add(index)
                self.copies[index].wait()

    def drain(self):
        self.wait(*range(len(self.copies)))


class Gather:
    def __init__(self, place, net, buffer):
        self.place, self.net, self.buffer = place, net, buffer

    def start(self):
        own = self.buffer.at[self.place.rows()]
        self.from_chip = self.net.copy(own, own, self.place.chip)
        self.from_core = self.net.copy(own, own, self.place.core)

    def forward(self):
        self.from_chip.wait_recv()
        passed = self.buffer.at[self.place.rows(x_other=True)]
        self.passed = self.net.copy(passed, passed, self.place.core)

    def finish(self):
        self.from_core.wait_recv()
        self.passed.wait_recv()


class Scatter:
    def __init__(self, place, net, part, near, out, far):
        self.place, self.net, self.part = place, net, part
        self.near, self.out, self.far = near, out, far

    def send(self, x_other):
        slot = 0 if x_other else 1
        rows = self.place.rows(x_other=x_other, c_other=True)
        made = self.net.copy(self.part.at[rows], self.near.at[slot], self.place.core)
        if x_other:
            self.first = made
        else:
            self.second = made

    def middle(self):
        self.first.wait_recv()
        mine = self.part[self.place.rows(x_other=True), :].astype(f32)
        self.out[...] = (mine + self.near[0].astype(f32)).astype(bf16)
        self.across = self.net.copy(self.out, self.far, self.place.chip)

    def finish(self):
        self.second.wait_recv()
        total = self.part[self.place.rows(), :].astype(f32) + self.near[1].astype(f32)
        self.across.wait_recv()
        return total + self.far[...].astype(f32)


def share_kernel(place_rows, qkv, out, up, down, sqkv, sout, small, *rest):
    targets, staged, (local_sems, send_sems, recv_sems) = rest[:7], rest[7:14], rest[14:]
    place = Place(place_rows)
    net, local = Net(send_sems, recv_sems), Local(local_sems)
    layer = place.c

    def half(array, axis, c):
        width = array.shape[axis] // 2
        index = [slice(None)] * len(array.shape)
        index[axis] = pl.ds(pl.multiple_of(c * width, width), width)
        return array.at[tuple(index)]

    shared = ((qkv, 2), (out, 0), (up, 1), (down, 0))
    kept = [half(array, axis, place.c) for array, axis in shared + ((sqkv, 2), (sout, 0))] + [small]
    sent = [half(array, axis, 1 - place.c) for array, axis in shared] + [small]
    finals = [target.at[layer] for target in targets[:4]] + [targets[4], targets[5], targets[6].at[layer]]
    place.meet()
    for source, target in zip(sent, finals[:4] + finals[6:]):
        net.copy(source, target, place.core)
    inward = [local.copy(source, stage) for source, stage in zip(kept, staged)]
    for index, stage, target in zip(inward, staged, finals):
        local.wait(index)
        local.copy(stage, target)
    for made in net.copies:
        made.wait_recv()
    local.drain()
    net.drain()


def share_weights(block_len, qkv, out, up, down, sqkv, sout, small):
    def halved(shape, axis, stacked=True):
        shape = list(shape)
        shape[axis] //= 2
        return jax.ShapeDtypeStruct(([2] if stacked else []) + shape, bf16)

    anywhere = pl.BlockSpec(memory_space=pl.ANY)
    return pl.pallas_call(
        partial(share_kernel, block_len),
        out_shape=(
            halved(qkv.shape, 2),
            halved(out.shape, 0),
            halved(up.shape, 1),
            halved(down.shape, 0),
            halved(sqkv.shape, 2, False),
            halved(sout.shape, 0, False),
            jax.ShapeDtypeStruct((2,) + small.shape, f32),
        ),
        in_specs=[anywhere] * 7,
        out_specs=[anywhere] * 7,
        scratch_shapes=[
            pltpu.VMEM(halved(array.shape, axis, False).shape, bf16)
            for array, axis in ((qkv, 2), (out, 0), (up, 1), (down, 0), (sqkv, 2), (sout, 0))
        ]
        + [
            pltpu.VMEM(small.shape, f32),
            pltpu.SemaphoreType.DMA((14,)),
            pltpu.SemaphoreType.DMA((5,)),
            pltpu.SemaphoreType.DMA((5,)),
        ],
        compiler_params=pltpu.CompilerParams(
            collective_id=0, has_side_effects=True, vmem_limit_bytes=VMEM_LIMIT
        ),
        name="share_weights",
    )(qkv, out, up, down, sqkv, sout, small)


def fill_bias(bias, row0):
    head_count, length = row0.shape
    for head in range(head_count):
        start = jnp.broadcast_to(row0[head : head + 1, :], (bias.shape[1], length))
        rolled = pltpu.roll(start, 0, axis=1, stride=1, stride_axis=0)
        bias[head, :, :length] = rolled
        bias[head, :, length:] = rolled


def bias_columns(index, chunk, length):
    return pl.ds(pl.multiple_of(length - index * chunk, chunk), length)


def window_logits(query, key_cur, key_prev, bias, valid, block, first_row, scale):
    logits = dot_nt(query, key_cur)
    rows = first_row + lax.broadcasted_iota(jnp.int32, logits.shape, 0)
    here = lax.broadcasted_iota(jnp.int32, logits.shape, 1) <= rows
    usable = valid[block : block + 1, :] > 0.5
    if key_prev is None:
        keep = here & usable
    else:
        logits = jnp.where(here, logits, dot_nt(query, key_prev))
        keep = jnp.where(here, valid[block : block + 1, :], valid[block - 1 : block, :]) > 0.5
    return jnp.where(keep, logits * scale + bias, negative), here


def forward_kernel(layer, names, *refs):
    r = SimpleNamespace(**dict(zip(names, refs)))
    rec = layer == 1
    length = r.u_v.shape[1]
    heads = r.row0.shape[0]
    head_size = r.att_v.shape[2] // heads
    width = heads * head_size
    scale = head_size ** (-0.5)
    place = Place(length)
    net, local = Net(r.send_sems, r.recv_sems), Local(r.local_sems)
    chunk = min(128, length)

    place.meet()
    load = [local.copy(r.wqkv.at[layer], r.wqkv_v), local.copy(r.wout.at[layer], r.wout_v)]
    load_mlp = [local.copy(r.wup.at[layer], r.wup_v), local.copy(r.wdown.at[layer], r.wdown_v)]
    load_state = []
    if rec:
        load_state = [local.copy(r.wsqkv, r.wsqkv_v), local.copy(r.wsout, r.wsout_v)]

    gain = lambda index: r.gain[index : index + 1, :]
    shift = lambda index: r.shift[index : index + 1, :]

    def gather(buffer):
        return Gather(place, net, buffer)

    scatter_count = [0]

    def scatter():
        index = scatter_count[0]
        scatter_count[0] += 1
        return Scatter(
            place, net, r.part.at[index], r.near.at[index], r.out.at[index], r.far.at[index]
        )

    def norm_state(rows, index):
        r.sn_v[index, place.rows(), :] = layer_norm(rows, r.sgain[...], r.sshift[...]).astype(bf16)

    def norm_first(block):
        rows = r.x[block, place.core_rows(), :].astype(f32)
        r.u_v[block, place.rows(), :] = layer_norm(rows, gain(0), shift(0)).astype(bf16)

    def project(source, weights, target):
        for part in range(3):
            target[:, part * width : (part + 1) * width] = dot(source[...], weights[part]).astype(bf16)

    def reduce_from(values, weights, to):
        columns = weights.shape[1]
        step = min(512, columns)
        for x_other in (True, False):
            rows = place.chip_rows(x_other)

            @pl.loop(0, columns // step)
            def _(index):
                at = pl.ds(pl.multiple_of(index * step, step), step)
                to.part[rows, at] = dot(values[rows, :], weights[:, at]).astype(bf16)

            to.send(x_other)

    def attend(block):
        qkv = r.qkv_v.at[block]
        prev = r.qkv_v.at[block - 1] if block > 0 else None

        @pl.loop(0, length // chunk)
        def _(index):
            at = pl.ds(pl.multiple_of(index * chunk, chunk), chunk)
            lses = []
            for head in range(heads):
                q_at = slice(head * head_size, (head + 1) * head_size)
                k_at = slice(width + head * head_size, width + (head + 1) * head_size)
                v_at = slice(2 * width + head * head_size, 2 * width + (head + 1) * head_size)
                query = qkv[at, q_at]
                logits, here = window_logits(
                    query,
                    qkv[:, k_at],
                    None if prev is None else prev[:, k_at],
                    r.bias[head, :, bias_columns(index, chunk, length)],
                    r.valid,
                    block,
                    index * chunk,
                    scale,
                )
                peak = jnp.max(logits, axis=-1, keepdims=True)
                if rec:
                    state = r.sqkv_v.at[block]
                    state_logits = dot_nt(query, state[:, k_at]) * scale
                    peak = jnp.maximum(peak, jnp.max(state_logits, axis=-1, keepdims=True))
                probs = jnp.exp(logits - peak)
                total = jnp.sum(probs, axis=-1, keepdims=True)
                if prev is None:
                    result = dot(probs.astype(bf16), qkv[:, v_at])
                else:
                    result = dot(jnp.where(here, probs, 0.0).astype(bf16), qkv[:, v_at])
                    result += dot(jnp.where(here, 0.0, probs).astype(bf16), prev[:, v_at])
                if rec:
                    state_probs = jnp.exp(state_logits - peak)
                    total += jnp.sum(state_probs, axis=-1, keepdims=True)
                    result += dot(state_probs.astype(bf16), state[:, v_at])
                r.att_v[block, at, q_at] = (result / total).astype(bf16)
                lses.append(peak + jnp.log(total))
            lane = lax.broadcasted_iota(jnp.int32, (chunk, 128), 1)
            packed = jnp.zeros((chunk, 128), f32)
            for head in range(heads):
                packed = jnp.where(lane == head, lses[head], packed)
            r.lse_v[block, at, :] = packed

    def recur(block):
        qkv, state = r.qkv_v.at[block], r.sqkv_v.at[block]

        @pl.loop(0, length // chunk)
        def _(index):
            at = pl.ds(pl.multiple_of(index * chunk, chunk), chunk)
            lses = []
            for head in range(heads):
                q_at = slice(head * head_size, (head + 1) * head_size)
                k_at = slice(width + head * head_size, width + (head + 1) * head_size)
                v_at = slice(2 * width + head * head_size, 2 * width + (head + 1) * head_size)
                logits = dot_nt(state[at, q_at], qkv[:, k_at]) * scale
                logits = jnp.where(r.valid[block : block + 1, :] > 0.5, logits, negative)
                peak = jnp.max(logits, axis=-1, keepdims=True)
                probs = jnp.exp(logits - peak)
                total = jnp.sum(probs, axis=-1, keepdims=True)
                r.sout_v[block, at, q_at] = (dot(probs.astype(bf16), qkv[:, v_at]) / total).astype(bf16)
                lses.append(peak + jnp.log(total))
            if block == 0:
                lane = lax.broadcasted_iota(jnp.int32, (chunk, 128), 1)
                packed = jnp.zeros((chunk, 128), f32)
                for head in range(heads):
                    packed = jnp.where(lane == head, lses[head], packed)
                r.rlse_v[at, :] = packed

    def take_branch(block, from_out):
        rows = r.x[block, place.core_rows(), :].astype(f32) + from_out.finish()
        r.h_v[block] = rows
        r.wn_v[block, place.rows(), :] = layer_norm(rows, gain(1), shift(1)).astype(bf16)

    def feed_up(block):
        columns = r.wup_v.shape[1]
        step = 256

        @pl.loop(0, columns // step)
        def _(index):
            at = pl.ds(pl.multiple_of(index * step, step), step)
            pre = dot(r.wn_v[block], r.wup_v[:, at]) + r.up_bias[:, at]
            r.pre_v[block, :, at] = pre.astype(bf16)
            r.act[block, :, at] = (0.5 * pre * (1.0 + lax.erf(pre * (0.5**0.5)))).astype(bf16)

    def take_result(block, from_down):
        rows = r.h_v[block] + from_down.finish() + r.down_bias[...]
        own = r.acts_v.at[block, place.core_rows()]
        own[...] = rows.astype(bf16)
        return net.copy(own, own, place.core)

    branch = [scatter(), scatter()]
    result = [scatter(), scatter()]
    first = [gather(r.u_v.at[block]) for block in range(2)]
    second = [gather(r.wn_v.at[block]) for block in range(2)]
    if rec:
        update = [scatter(), scatter()]
        state = [gather(r.sn_v.at[block]) for block in range(2)]
        gate = r.gate[...]
        norm_state(r.state[place.core_rows(), :].astype(f32), 0)
        state[0].start()
    norm_first(0)
    first[0].start()
    norm_first(1)
    first[1].start()
    fill_bias(r.bias, r.row0)
    if rec:
        state[0].forward()
    first[0].forward()
    if rec:
        state[0].finish()
        local.wait(*load_state)
        project(r.sn_v.at[0], r.wsqkv_v, r.sqkv_v.at[0])
    first[0].finish()
    local.wait(*load)
    project(r.u_v.at[0], r.wqkv_v, r.qkv_v.at[0])
    if rec:
        recur(0)
        reduce_from(r.sout_v.at[0], r.wsout_v, update[0])
    first[1].forward()
    if rec:
        update[0].middle()
    attend(0)
    reduce_from(r.att_v.at[0], r.wout_v, branch[0])
    first[1].finish()
    project(r.u_v.at[1], r.wqkv_v, r.qkv_v.at[1])
    local.copy(r.u_v, r.u)
    local.copy(r.qkv_v, r.qkv)
    branch[0].middle()
    if rec:
        update_rows = update[0].finish()
        r.z_v[...] = update_rows
        state_rows = gate * r.state[place.core_rows(), :].astype(f32) + (1.0 - gate) * update_rows
        r.s1_v[...] = state_rows
        norm_state(state_rows, 1)
        state[1].start()
        local.copy(r.z_v, r.z)
        local.copy(r.s1_v, r.s1)
    else:
        attend(1)
        reduce_from(r.att_v.at[1], r.wout_v, branch[1])
    take_branch(0, branch[0])
    second[0].start()
    if rec:
        state[1].forward()
        state[1].finish()
        project(r.sn_v.at[1], r.wsqkv_v, r.sqkv_v.at[1])
        local.copy(r.sn_v, r.sn)
        local.copy(r.sqkv_v, r.sqkv)
        attend(1)
        reduce_from(r.att_v.at[1], r.wout_v, branch[1])
    local.copy(r.att_v, r.att)
    local.copy(r.lse_v, r.lse)
    second[0].forward()
    branch[1].middle()
    second[0].finish()
    local.wait(*load_mlp)
    feed_up(0)
    reduce_from(r.act.at[0], r.wdown_v, result[0])
    take_branch(1, branch[1])
    second[1].start()
    local.copy(r.h_v, r.h)
    result[0].middle()
    if rec:
        recur(1)
        reduce_from(r.sout_v.at[1], r.wsout_v, update[1])
        local.copy(r.sout_v, r.sout)
        local.copy(r.rlse_v, r.rlse)
    second[1].forward()
    second[1].finish()
    local.copy(r.wn_v, r.wn)
    feed_up(1)
    local.copy(r.pre_v, r.pre)
    reduce_from(r.act.at[1], r.wdown_v, result[1])
    sent = [take_result(0, result[0])]
    result[1].middle()
    if rec:
        update[1].middle()
    sent.append(take_result(1, result[1]))
    if rec:
        own = r.final_v.at[place.core_rows()]
        own[...] = gate * r.s1_v[...] + (1.0 - gate) * update[1].finish()
        sent.append(net.copy(own, own, place.core))
    for made in sent:
        made.wait_recv()
    local.copy(r.acts_v, r.acts)
    if rec:
        local.copy(r.final_v, r.final)
    local.drain()
    net.drain()


def forward_layer(layer, block_len, small, row0, valid, weights, rows, state):
    rec = layer == 1
    wqkv, wout, wup, wdown = weights[:4]
    model = rows.shape[2]
    width, hidden = wqkv.shape[3], wup.shape[2]
    quarter = block_len // 4
    heads = row0.shape[0]

    def held(shape, dtype):
        return jax.ShapeDtypeStruct(shape, dtype)

    outs = dict(
        u=held((2, block_len, model), bf16),
        qkv=held((2, block_len, 3 * width), bf16),
        lse=held((2, block_len, 128), f32),
        att=held((2, block_len, width), bf16),
        wn=held((2, block_len, model), bf16),
        pre=held((2, block_len, hidden), bf16),
        h=held((2, quarter, model), f32),
        acts=held((2, 2 * quarter, model), bf16),
    )
    ins = dict(
        x=rows,
        gain=small.gain[layer],
        shift=small.shift[layer],
        up_bias=small.up_bias[layer],
        down_bias=small.down_bias[layer],
        row0=row0,
        valid=valid,
    )
    far_ins = dict(wqkv=wqkv, wout=wout, wup=wup, wdown=wdown)
    if rec:
        outs.update(
            sn=held((2, block_len, model), bf16),
            sqkv=held((2, block_len, 3 * width), bf16),
            rlse=held((block_len, 128), f32),
            sout=held((2, block_len, width), bf16),
            s1=held((quarter, model), f32),
            z=held((quarter, model), f32),
            final=held((2 * quarter, model), f32),
        )
        ins.update(state=state, sgain=small.sgain, sshift=small.sshift, gate=small.gate)
        far_ins.update(wsqkv=weights[4], wsout=weights[5])
    scatters = 6 if rec else 4
    copies = (3 * 6 + 3 * 6 + 3) if rec else (3 * 4 + 3 * 4 + 2)
    scratch = {name + "_v": pltpu.VMEM(kind.shape, kind.dtype) for name, kind in outs.items()}
    scratch.update(
        wqkv_v=pltpu.VMEM(wqkv.shape[1:], bf16),
        wout_v=pltpu.VMEM(wout.shape[1:], bf16),
        wup_v=pltpu.VMEM(wup.shape[1:], bf16),
        wdown_v=pltpu.VMEM(wdown.shape[1:], bf16),
        act=pltpu.VMEM((2, block_len, hidden), bf16),
        bias=pltpu.VMEM((heads, min(128, block_len), 2 * block_len), f32),
        part=pltpu.VMEM((scatters, block_len, model), bf16),
        near=pltpu.VMEM((scatters, 2, quarter, model), bf16),
        out=pltpu.VMEM((scatters, quarter, model), bf16),
        far=pltpu.VMEM((scatters, quarter, model), bf16),
        send_sems=pltpu.SemaphoreType.DMA((copies,)),
        recv_sems=pltpu.SemaphoreType.DMA((copies,)),
        local_sems=pltpu.SemaphoreType.DMA((6 + len(outs),)),
    )
    if rec:
        scratch.update(
            wsqkv_v=pltpu.VMEM(weights[4].shape, bf16),
            wsout_v=pltpu.VMEM(weights[5].shape, bf16),
        )
    anywhere = pl.BlockSpec(memory_space=pl.ANY)
    inside = pl.BlockSpec(memory_space=pltpu.VMEM)
    results = pl.pallas_call(
        partial(forward_kernel, layer, [*ins, *far_ins, *outs, *scratch]),
        out_shape=tuple(outs.values()),
        in_specs=[inside] * len(ins) + [anywhere] * len(far_ins),
        out_specs=[anywhere] * len(outs),
        scratch_shapes=list(scratch.values()),
        compiler_params=pltpu.CompilerParams(
            collective_id=1 + layer, has_side_effects=True, vmem_limit_bytes=VMEM_LIMIT
        ),
        name="forward_recurrent" if rec else "forward_local",
    )(*ins.values(), *far_ins.values())
    return SimpleNamespace(**dict(zip(outs, results)))


def norm_back(rows, gain, grad):
    normed, scale = norm_parts(rows)
    inner = grad * gain
    means = jnp.mean(inner, axis=-1, keepdims=True), jnp.mean(inner * normed, axis=-1, keepdims=True)
    by_rows = scale * (inner - means[0] - normed * means[1])
    return by_rows, jnp.sum(grad * normed, axis=0, keepdims=True), jnp.sum(grad, axis=0, keepdims=True)


GAIN0, GAIN1, SHIFT0, SHIFT1, DOWN_BIAS, SGAIN, SSHIFT, GATE, UP_BIAS, BY_DISTANCE = range(10)
SMALL_ROWS = 16


def backward_kernel(layer, names, *refs):
    r = SimpleNamespace(**dict(zip(names, refs)))
    rec = layer == 1
    heads, length = r.row0.shape
    head_size = r.att_v.shape[1] // heads
    width = heads * head_size
    hidden = r.wup_v.shape[1]
    model = r.wup_v.shape[0]
    scale = head_size ** (-0.5)
    place = Place(length)
    net, local = Net(r.send_sems, r.recv_sems), Local(r.local_sems)
    chunk = min(128, length)

    place.meet()
    wdown = local.copy(r.wdown.at[layer], r.wdown_v)
    pre = local.copy(r.pre, r.pre_v)
    wup = local.copy(r.wup.at[layer], r.wup_v)
    hidden_rows = local.copy(r.h, r.h_v)
    wn = local.copy(r.wn, r.wn_v)
    attention = [
        local.copy(r.wout.at[layer], r.wout_v),
        local.copy(r.qkv, r.qkv_v),
        local.copy(r.att, r.att_v),
        local.copy(r.lse, r.lse_v),
    ]
    if rec:
        attention += [local.copy(r.sqkv, r.sqkv_v), local.copy(r.wsqkv, r.wsqkv_v)]
        chain = [
            local.copy(r.s1, r.s1_v),
            local.copy(r.z, r.z_v),
            local.copy(r.wsout, r.wsout_v),
            local.copy(r.sout, r.sout_v),
            local.copy(r.rlse, r.rlse_v),
        ]
    wqkv = local.copy(r.wqkv.at[layer], r.wqkv_v)

    gain = lambda index: r.gain[index : index + 1, :]
    small = r.small_v
    small[...] = jnp.zeros(small.shape, f32)
    r.dkv[...] = jnp.zeros(r.dkv.shape, f32)
    r.dbias[...] = jnp.zeros(r.dbias.shape, f32)
    if rec:
        r.dskv[...] = jnp.zeros(r.dskv.shape, f32)

    def add_small(index, value):
        small[index : index + 1, :] += value

    def gather(buffer):
        return Gather(place, net, buffer)

    scatter_count = [0]

    def scatter():
        index = scatter_count[0]
        scatter_count[0] += 1
        return Scatter(
            place, net, r.part.at[index], r.near.at[index], r.out.at[index], r.far.at[index]
        )

    def block_rows(block):
        return slice(block * length, (block + 1) * length)

    def own_grad(block):
        return r.gy[block, place.core_rows(), :].astype(bf16).astype(f32)

    def feed_back(block):
        step = 256
        rows = block_rows(block)

        @pl.loop(0, hidden // step)
        def _(index):
            at = pl.ds(pl.multiple_of(index * step, step), step)
            pre = r.pre_v[rows, at].astype(f32)
            by_act = dot_nt(r.g[rows, :], r.wdown_v[at, :])
            below = 0.5 * (1.0 + lax.erf(pre * (0.5**0.5)))
            r.act[rows, at] = (pre * below).astype(bf16)
            by_pre = by_act * (below + pre * jnp.exp(-0.5 * pre * pre) * 0.3989422804014327)
            small[UP_BIAS : UP_BIAS + 1, at] += jnp.sum(by_pre, axis=0, keepdims=True)
            r.dpre[rows, at] = by_pre.astype(bf16)

    def reduce_back(terms, to):
        step = min(512, model)
        for x_other in (True, False):
            rows = place.chip_rows(x_other)

            @pl.loop(0, model // step)
            def _(index):
                at = pl.ds(pl.multiple_of(index * step, step), step)
                total = None
                for values, weights in terms:
                    term = dot_nt(values[rows, :], weights[at, :])
                    total = term if total is None else total + term
                to.part[rows, at] = total.astype(bf16)

            to.send(x_other)

    def take_feed(block, from_feed):
        by_norm = from_feed.finish()
        grad = own_grad(block)
        by_rows, by_gain, by_shift = norm_back(r.h_v[block], gain(1), by_norm)
        add_small(GAIN1, by_gain)
        add_small(SHIFT1, by_shift)
        add_small(DOWN_BIAS, jnp.sum(grad, axis=0, keepdims=True))
        total = grad + by_rows
        r.dh[block] = total
        r.hg[pl.ds(place_row(block), place.quarter), :] = total.astype(bf16)

    def place_row(block):
        return pl.multiple_of(block * length + place.x * place.half + place.c * place.quarter, place.quarter)

    def weight_grad(left, right, target, at_row=0):
        step = 256

        @pl.loop(0, left.shape[1] // step)
        def _(index):
            at = pl.ds(pl.multiple_of(index * step, step), step)
            to = pl.ds(pl.multiple_of(at_row + index * step, step), step)
            target[to, :] = dot_tn(left[:, at], right[...]).astype(bf16)

    def projection_grad(normed, grads, target):
        for part in range(3):
            to = slice(part * width, (part + 1) * width)

            @pl.loop(0, model // width)
            def _(index):
                at = pl.ds(pl.multiple_of(index * width, width), width)
                target[to, at] = dot_tn(normed[:, at], grads[:, to]).astype(bf16)

    def branch_back(block):
        r.datt[block] = dot_nt(r.hg[block_rows(block), :], r.wout_v[...]).astype(bf16)

    def columns(head, part):
        return slice(part * width + head * head_size, part * width + (head + 1) * head_size)

    def attend_back(block):
        qkv = r.qkv_v.at[block]
        prev = r.qkv_v.at[block - 1] if block > 0 else None
        state = r.sqkv_v.at[block] if rec else None

        @pl.loop(0, length // chunk)
        def _(index):
            at = pl.ds(pl.multiple_of(index * chunk, chunk), chunk)
            block_at = pl.ds(pl.multiple_of(block * length + index * chunk, chunk), chunk)
            for head in range(heads):
                q_at, k_at, v_at = (columns(head, part) for part in range(3))
                query, key, value = qkv[at, q_at], qkv[:, k_at], qkv[:, v_at]
                logits, here = window_logits(
                    query,
                    key,
                    None if prev is None else prev[:, k_at],
                    r.bias[head, :, bias_columns(index, chunk, length)],
                    r.valid,
                    block,
                    index * chunk,
                    scale,
                )
                lse = r.lse_v[block, at, head : head + 1]
                probs = jnp.exp(logits - lse)
                grad = r.datt[block, at, q_at]
                delta = jnp.sum(
                    grad.astype(f32) * r.att_v[block_at, q_at].astype(f32), axis=-1, keepdims=True
                )
                by_probs = dot_nt(grad, value)
                if prev is not None:
                    by_probs = jnp.where(here, by_probs, dot_nt(grad, prev[:, v_at]))
                by_logits = probs * (by_probs - delta)
                r.dbias[head, :, bias_columns(index, chunk, length)] += by_logits
                by_logits = by_logits * scale
                if prev is None:
                    low = by_logits.astype(bf16)
                    low_probs = probs.astype(bf16)
                    by_query = dot(low, key)
                else:
                    low = jnp.where(here, by_logits, 0.0).astype(bf16)
                    low_probs = jnp.where(here, probs, 0.0).astype(bf16)
                    low_prev = jnp.where(here, 0.0, by_logits).astype(bf16)
                    low_probs_prev = jnp.where(here, 0.0, probs).astype(bf16)
                    by_query = dot(low, key) + dot(low_prev, prev[:, k_at])
                    r.dkv[block - 1, :, q_at] += dot_tn(low_prev, query)
                    r.dkv[block - 1, :, k_at] += dot_tn(low_probs_prev, grad)
                r.dkv[block, :, q_at] += dot_tn(low, query)
                r.dkv[block, :, k_at] += dot_tn(low_probs, grad)
                if rec:
                    state_probs = jnp.exp(dot_nt(query, state[:, k_at]) * scale - lse)
                    by_state = state_probs * (dot_nt(grad, state[:, v_at]) - delta) * scale
                    low_state = by_state.astype(bf16)
                    by_query += dot(low_state, state[:, k_at])
                    r.dskv[:, q_at] += dot_tn(low_state, query)
                    r.dskv[:, k_at] += dot_tn(state_probs.astype(bf16), grad)
                r.dqkv[block_at, q_at] = by_query.astype(bf16)

    def recur_back():
        qkv, state = r.qkv_v.at[0], r.sqkv_v.at[0]

        @pl.loop(0, length // chunk)
        def _(index):
            at = pl.ds(pl.multiple_of(index * chunk, chunk), chunk)
            for head in range(heads):
                q_at, k_at, v_at = (columns(head, part) for part in range(3))
                query, key, value = state[at, q_at], qkv[:, k_at], qkv[:, v_at]
                logits = dot_nt(query, key) * scale
                logits = jnp.where(r.valid[0:1, :] > 0.5, logits, negative)
                probs = jnp.exp(logits - r.rlse_v[at, head : head + 1])
                grad = r.dsout[at, q_at]
                delta = jnp.sum(
                    grad.astype(f32) * r.sout_v[0, at, q_at].astype(f32), axis=-1, keepdims=True
                )
                low = (probs * (dot_nt(grad, value) - delta) * scale).astype(bf16)
                r.dsqkv[at, q_at] = dot(low, key).astype(bf16)
                r.dkv[0, :, q_at] += dot_tn(low, query)
                r.dkv[0, :, k_at] += dot_tn(probs.astype(bf16), grad)

    def close_keys(block):
        r.dqkv[block_rows(block), width:] = r.dkv[block].astype(bf16)

    def close_state(block):
        r.dsqkv[block_rows(block), width:] = r.dskv[...].astype(bf16)
        if block == 1:
            r.dskv[...] = jnp.zeros(r.dskv.shape, f32)

    def input_back(block, to):
        rows = block_rows(block)
        reduce_back(
            [
                (r.dqkv.at[rows, part * width : (part + 1) * width], r.wqkv_v.at[part])
                for part in range(3)
            ],
            to,
        )

    def state_back(block, to):
        rows = block_rows(block)
        reduce_back(
            [
                (r.dsqkv.at[rows, part * width : (part + 1) * width], r.wsqkv_v.at[part])
                for part in ((0, 1, 2) if block == 0 else (1, 2))
            ],
            to,
        )

    def take_input(block, from_input):
        by_norm = from_input.finish()
        rows = r.x[block, place.core_rows(), :].astype(f32)
        by_rows, by_gain, by_shift = norm_back(rows, gain(0), by_norm)
        add_small(GAIN0, by_gain)
        add_small(SHIFT0, by_shift)
        own = r.ig_v.at[block, place.core_rows()]
        own[...] = r.dh[block] + by_rows
        return net.copy(own, own, place.core)

    def take_state(rows, from_state):
        by_rows, by_gain, by_shift = norm_back(rows, r.sgain[...], from_state.finish())
        add_small(SGAIN, by_gain)
        add_small(SSHIFT, by_shift)
        return by_rows

    def close_bias():
        tile = r.dbias.shape[1]
        for head in range(heads):
            folded = r.dbias[head, :, :length] + r.dbias[head, :, length:]
            row = lax.broadcasted_iota(jnp.int32, folded.shape, 0)
            bit = 1
            while bit < tile:
                moved = pltpu.roll(folded, length - bit, axis=1)
                folded = jnp.where((row & bit) != 0, moved, folded)
                bit *= 2
            small[BY_DISTANCE : BY_DISTANCE + 1, head * length : (head + 1) * length] = jnp.sum(
                folded, axis=0, keepdims=True
            )

    at_qkv, at_out, at_up = 0, 3 * width, 4 * width
    at_down = at_up + model
    at_sqkv = at_down + hidden
    at_sout = at_sqkv + 3 * width

    feed = [scatter(), scatter()]
    inputs = [scatter(), scatter()]
    grads = [gather(r.g.at[block_rows(block)]) for block in range(2)]
    hiddens = [gather(r.hg.at[block_rows(block)]) for block in range(2)]
    if rec:
        states = [scatter(), scatter()]
        updates = gather(r.ug)
    for block in (1, 0):
        r.g[pl.ds(place_row(block), place.quarter), :] = own_grad(block).astype(bf16)
        grads[block].start()
    fill_bias(r.bias, r.row0)
    grads[1].forward()
    local.wait(wdown, pre, wup)
    grads[1].finish()
    feed_back(1)
    reduce_back([(r.dpre.at[block_rows(1)], r.wup_v)], feed[1])
    grads[0].forward()
    grads[0].finish()
    feed_back(0)
    feed[1].middle()
    reduce_back([(r.dpre.at[block_rows(0)], r.wup_v)], feed[0])
    local.wait(hidden_rows)
    take_feed(1, feed[1])
    hiddens[1].start()
    feed[0].middle()
    weight_grad(r.act, r.g, r.pre_v)
    down_out = local.copy(r.pre_v, r.dw.at[at_down:at_sqkv])
    hiddens[1].forward()
    take_feed(0, feed[0])
    hiddens[0].start()
    hiddens[1].finish()
    local.wait(*attention)
    branch_back(1)
    attend_back(1)
    close_keys(1)
    if rec:
        close_state(1)
        state_back(1, states[1])
    hiddens[0].forward()
    local.wait(wqkv)
    input_back(1, inputs[1])
    if rec:
        states[1].middle()
    hiddens[0].finish()
    branch_back(0)
    inputs[1].middle()
    if rec:
        local.wait(*chain)
        gate = r.gate[...]
        by_state = take_state(r.s1_v[...], states[1])
        before = r.state[place.core_rows(), :].astype(f32)
        add_small(
            GATE,
            jnp.sum(by_state * (before - r.z_v[...]) * gate * (1.0 - gate), axis=0, keepdims=True),
        )
        r.ug[place.rows(), :] = ((1.0 - gate) * by_state).astype(bf16)
        updates.start()
    attend_back(0)
    if rec:
        updates.forward()
        updates.finish()
        r.dsout[...] = dot_nt(r.ug[...], r.wsout_v[...]).astype(bf16)
        recur_back()
    close_keys(0)
    input_back(0, inputs[0])
    if rec:
        close_state(0)
        state_back(0, states[0])
    sent = [take_input(1, inputs[1])]
    inputs[0].middle()
    if rec:
        states[0].middle()
    local.wait(wn)
    weight_grad(r.wn_v, r.dpre, r.act)
    up_out = local.copy(r.act, r.dw.at[at_up:at_down])
    u_in = local.copy(r.u, r.wn_v)
    weight_grad(r.att_v, r.hg, r.dpre, at_out)
    if rec:
        local.wait(down_out)
        sn_in = local.copy(r.sn, r.pre_v)
    close_bias()
    local.wait(u_in)
    projection_grad(r.wn_v, r.dqkv, r.dpre)
    local.copy(r.dpre, r.dw.at[at_qkv:at_up])
    if rec:
        local.wait(sn_in, up_out)
        r.dsqkv[block_rows(1), 0:width] = jnp.zeros((length, width), bf16)
        projection_grad(r.pre_v, r.dsqkv, r.act)
        weight_grad(r.sout_v.at[0], r.ug, r.act, at_sout - at_sqkv)
        local.copy(r.act, r.dw.at[at_sqkv:])
    sent.append(take_input(0, inputs[0]))
    if rec:
        take_state(r.state[place.core_rows(), :].astype(f32), states[0])
    local.copy(small, r.small)
    for made in sent:
        made.wait_recv()
    local.copy(r.ig_v, r.ig)
    local.drain()
    net.drain()


def backward_layer(layer, block_len, small, row0, valid, weights, grad_rows, rows, state, kept):
    rec = layer == 1
    wqkv, wout, wup, wdown = weights[:4]
    model = rows.shape[2]
    width, hidden = wqkv.shape[3], wup.shape[2]
    quarter = block_len // 4
    heads = row0.shape[0]

    def held(shape, dtype):
        return jax.ShapeDtypeStruct(shape, dtype)

    dw_rows = 4 * width + model + hidden + (4 * width if rec else 0)
    outs = dict(
        dw=held((dw_rows, model), bf16),
        small=held((SMALL_ROWS, model), f32),
        ig=held((2, 2 * quarter, model), f32),
    )
    ins = dict(
        gy=grad_rows, x=rows, gain=small.gain[layer], shift=small.shift[layer], row0=row0, valid=valid
    )

    def flat(array):
        return array.reshape((-1,) + array.shape[2:])

    stacked = dict(wqkv=wqkv, wout=wout, wup=wup, wdown=wdown)
    copied = dict(
        qkv=kept.qkv, lse=kept.lse, att=flat(kept.att), wn=flat(kept.wn), pre=flat(kept.pre), h=kept.h
    )
    late = dict(u=flat(kept.u))
    if rec:
        ins.update(state=state, sgain=small.sgain, sshift=small.sshift, gate=small.gate)
        copied.update(wsqkv=weights[4], wsout=weights[5])
        copied.update(sqkv=kept.sqkv, rlse=kept.rlse, sout=kept.sout, s1=kept.s1, z=kept.z)
        late.update(sn=flat(kept.sn))
    far_ins = {**stacked, **copied, **late}
    scatters = 6 if rec else 4
    copies = (3 * 6 + 3 * 5 + 2) if rec else (3 * 4 + 3 * 4 + 2)
    scratch = dict(small_v=pltpu.VMEM(outs["small"].shape, f32), ig_v=pltpu.VMEM(outs["ig"].shape, f32))
    for name, array in stacked.items():
        scratch[name + "_v"] = pltpu.VMEM(array.shape[1:], array.dtype)
    for name, array in copied.items():
        scratch[name + "_v"] = pltpu.VMEM(array.shape, array.dtype)
    scratch.update(
        g=pltpu.VMEM((2 * block_len, model), bf16),
        hg=pltpu.VMEM((2 * block_len, model), bf16),
        act=pltpu.VMEM((2 * block_len, hidden), bf16),
        dpre=pltpu.VMEM((2 * block_len, hidden), bf16),
        dh=pltpu.VMEM((2, quarter, model), f32),
        datt=pltpu.VMEM((2, block_len, width), bf16),
        dkv=pltpu.VMEM((2, block_len, 2 * width), f32),
        dqkv=pltpu.VMEM((2 * block_len, 3 * width), bf16),
        dbias=pltpu.VMEM((heads, min(128, block_len), 2 * block_len), f32),
        bias=pltpu.VMEM((heads, min(128, block_len), 2 * block_len), f32),
        part=pltpu.VMEM((scatters, block_len, model), bf16),
        near=pltpu.VMEM((scatters, 2, quarter, model), bf16),
        out=pltpu.VMEM((scatters, quarter, model), bf16),
        far=pltpu.VMEM((scatters, quarter, model), bf16),
        send_sems=pltpu.SemaphoreType.DMA((copies,)),
        recv_sems=pltpu.SemaphoreType.DMA((copies,)),
        local_sems=pltpu.SemaphoreType.DMA((len(far_ins) + 6,)),
    )
    if rec:
        scratch.update(
            ug=pltpu.VMEM((block_len, model), bf16),
            dsout=pltpu.VMEM((block_len, width), bf16),
            dskv=pltpu.VMEM((block_len, 2 * width), f32),
            dsqkv=pltpu.VMEM((2 * block_len, 3 * width), bf16),
        )
    anywhere = pl.BlockSpec(memory_space=pl.ANY)
    inside = pl.BlockSpec(memory_space=pltpu.VMEM)
    results = pl.pallas_call(
        partial(backward_kernel, layer, [*ins, *far_ins, *outs, *scratch]),
        out_shape=tuple(outs.values()),
        in_specs=[inside] * len(ins) + [anywhere] * len(far_ins),
        out_specs=[anywhere] * len(outs),
        scratch_shapes=list(scratch.values()),
        compiler_params=pltpu.CompilerParams(
            collective_id=3 + layer, has_side_effects=True, vmem_limit_bytes=VMEM_LIMIT
        ),
        name="backward_recurrent" if rec else "backward_local",
    )(*ins.values(), *far_ins.values())
    return SimpleNamespace(**dict(zip(outs, results)))


def ring_place(n, c, d):
    if n % 2:
        at = d

        def index_at(p):
            return p

    else:
        a, b = d // 2, d % 2
        at = a + b * (n - 1 - 2 * a)

        def index_at(p):
            b = p // (n // 2)
            return 2 * (p + b * (n - 1 - 2 * p)) + b

    def flip(p):
        return p + c * (n - 1 - 2 * p)

    return flip(at), lambda p: index_at(flip(p))


def sum_kernel(
    n, subs, parts_1, parts_0, small, full, small_out, mine, held, small_held, small_sum, small_far,
    rs_send, rs_recv, ag_send, ag_recv, core_send, core_recv, small_send, small_recv, local_sems,
):
    c, x, d = lax.axis_index("section"), lax.axis_index("mp"), lax.axis_index("dp")
    q, index_at = ring_place(n, c, d)
    after, before = {"dp": index_at((q + 1) % n)}, {"dp": index_at((q + n - 1) % n)}
    core, chip = {"section": 1 - c}, {"mp": 1 - x}
    chunk = mine.shape[0] // n
    sub = chunk // subs

    def rows(owner, k):
        return pl.ds(pl.multiple_of(owner * chunk + k * sub, sub), sub)

    def piece(k):
        return slice(k * sub, (k + 1) * sub)

    def remote(source, target, send, recv, to):
        return pltpu.make_async_remote_copy(
            src_ref=source, dst_ref=target, send_sem=send, recv_sem=recv, device_id=to, device_id_type=MESH
        )

    def reduce_first(k):
        return remote(mine.at[rows(q, k)], held.at[0, piece(k)], rs_send.at[0, k], rs_recv.at[0, k], after)

    def reduce_next(s, k):
        return remote(held.at[s - 1, piece(k)], held.at[s, piece(k)], rs_send.at[s, k], rs_recv.at[s, k], after)

    def gathered(s, k):
        return full.at[c, rows((q + 1 - s + n) % n, k)]

    def gather(s, k, source=None):
        target = gathered(s, k)
        source = target if source is None else source
        return remote(source, target, ag_send.at[s, k], ag_recv.at[s, k], after)

    def to_core(s, k, source=None):
        target = gathered(s, k)
        source = target if source is None else source
        return remote(source, target, core_send.at[s, k], core_recv.at[s, k], core)

    def from_core(s, k):
        target = full.at[1 - c, rows((n - q - s + n) % n, k)]
        return remote(target, target, core_send.at[s, k], core_recv.at[s, k], core)

    def small_step(s, first):
        source = small if first else small_held.at[s - 1]
        return remote(source, small_held.at[s], small_send.at[s], small_recv.at[s], after)

    barrier = pltpu.get_barrier_semaphore()
    for other in (after, before, core, chip):
        pl.semaphore_signal(barrier, inc=1, device_id=other, device_id_type=MESH)
    size_1 = parts_1.shape[0]
    loads = [
        pltpu.make_async_copy(parts_1, mine.at[:size_1], local_sems.at[0]),
        pltpu.make_async_copy(parts_0, mine.at[size_1:], local_sems.at[1]),
    ]
    for made in loads:
        made.start()
    pl.semaphore_wait(barrier, 4)
    small_step(0, True).start()
    for made in loads:
        made.wait()
    for k in range(subs):
        reduce_first(k).start()

    def add_own(s, k):
        held[s, piece(k), :] = (
            held[s, piece(k), :].astype(f32) + mine[rows((q + n - 1 - s) % n, k), :].astype(f32)
        ).astype(bf16)

    @pl.loop(0, n - 2)
    def _(s):
        for k in range(subs):
            remote(held.at[s, piece(k)], held.at[s, piece(k)], rs_send.at[s, k], rs_recv.at[s, k], after).wait_recv()
            add_own(s, k)
            reduce_next(s + 1, k).start()
        small_step(s, True).wait_recv()
        small_step(s + 1, False).start()

    last = n - 2
    finals = []
    for k in range(subs):
        summed = held.at[last, piece(k)]
        remote(summed, summed, rs_send.at[last, k], rs_recv.at[last, k], after).wait_recv()
        add_own(last, k)
        gather(0, k, summed).start()
        to_core(0, k, summed).start()
        made = pltpu.make_async_copy(summed, gathered(0, k), local_sems.at[k])
        made.start()
        finals.append(made)

    small_step(last, True).wait_recv()
    small_out[0] = small[...]

    @pl.loop(0, n - 1)
    def _(s):
        small_out[0] += small_held[s]

    between = remote(small_out.at[0], small_out.at[1], small_send.at[n - 1], small_recv.at[n - 1], core)
    between.start()
    between.wait_recv()
    small_sum[...] = small_out[0] + small_out[1]
    across = remote(small_sum, small_far, small_send.at[n], small_recv.at[n], chip)
    across.start()
    across.wait_recv()
    small_out[2] = small_sum[...] + small_far[...]

    @pl.loop(0, n - 2)
    def _(s):
        for k in range(subs):
            gather(s, k, gathered(s + 1, k)).wait_recv()
            gather(s + 1, k).start()
            to_core(s + 1, k).start()

    for k in range(subs):
        gather(last, k, gathered(last + 1, k)).wait_recv()
        to_core(last + 1, k).start()

    @pl.loop(0, n)
    def _(s):
        for k in range(subs):
            from_core(s, k).wait_recv()
            to_core(s, k).wait_send()

    @pl.loop(0, n - 1)
    def _(s):
        for k in range(subs):
            remote(held.at[s, piece(k)], held.at[s, piece(k)], rs_send.at[s, k], rs_recv.at[s, k], after).wait_send()
            gather(s, k).wait_send()
        small_step(s, True).wait_send()

    between.wait_send()
    across.wait_send()
    for made in finals:
        made.wait()


def sum_gradients(n, parts_1, parts_0, small):
    total, model = parts_1.shape[0] + parts_0.shape[0], parts_1.shape[1]
    chunk = total // n
    subs = max(k for k in range(1, 9) if chunk % (16 * k) == 0)
    anywhere = pl.BlockSpec(memory_space=pl.ANY)
    inside = pl.BlockSpec(memory_space=pltpu.VMEM)
    sems = pltpu.SemaphoreType.DMA
    return pl.pallas_call(
        partial(sum_kernel, n, subs),
        out_shape=(
            jax.ShapeDtypeStruct((2, total, model), bf16),
            jax.ShapeDtypeStruct((3,) + small.shape, f32),
        ),
        in_specs=[anywhere, anywhere, inside],
        out_specs=[anywhere, inside],
        scratch_shapes=[
            pltpu.VMEM((total, model), bf16),
            pltpu.VMEM((n - 1, chunk, model), bf16),
            pltpu.VMEM((n - 1,) + small.shape, f32),
            pltpu.VMEM(small.shape, f32),
            pltpu.VMEM(small.shape, f32),
            sems((n - 1, subs)),
            sems((n - 1, subs)),
            sems((n - 1, subs)),
            sems((n - 1, subs)),
            sems((n, subs)),
            sems((n, subs)),
            sems((n + 1,)),
            sems((n + 1,)),
            sems((max(2, subs),)),
        ],
        compiler_params=pltpu.CompilerParams(
            collective_id=5, has_side_effects=True, vmem_limit_bytes=VMEM_LIMIT
        ),
        name="sum_gradients",
    )(parts_1, parts_0, small)


def place_kernel(width, hidden, size_1, full, qkv, out, up, down, sqkv, sout, inward, outward, in_sems, out_sems):
    model = full.shape[2]
    base = (1 - lax.axis_index("section")) * size_1
    slots = inward.shape[0]
    at_out, at_up = 3 * width, 4 * width
    at_down = at_up + model
    at_sqkv = at_down + hidden
    at_sout = at_sqkv + 3 * width
    jobs = []
    for half in range(2):
        columns = slice(half * width, (half + 1) * width)

        def projection(target, row):
            return [target.at[index : index + width, columns] for index in range(0, model, width)]

        for part in range(3):
            jobs.append((half, base + part * width, projection(qkv.at[0, part], part)))
            jobs.append((half, at_sqkv + part * width, projection(sqkv.at[part], part)))
        jobs.append((half, base + at_out, [out.at[0, columns]]))
        jobs.append((half, at_sout, [sout.at[columns]]))
        for row in range(0, model, width):
            wide = slice(half * hidden, (half + 1) * hidden)
            jobs.append((half, base + at_up + row, [up.at[0, row : row + width, wide]]))
        for row in range(0, hidden, width):
            at = half * hidden + row
            jobs.append((half, base + at_down + row, [down.at[0, at : at + width]]))

    def load(index):
        half, row, _ = jobs[index]
        at = row if isinstance(row, int) else pl.multiple_of(row, width)
        slot = index % slots
        return pltpu.make_async_copy(full.at[half, pl.ds(at, width)], inward.at[slot], in_sems.at[slot])

    def stores(index):
        targets, slot = jobs[index][2], index % slots
        step = model // len(targets)
        return [
            pltpu.make_async_copy(
                outward.at[slot, :, k * step : (k + 1) * step], target, out_sems.at[slot, k]
            )
            for k, target in enumerate(targets)
        ]

    for index in range(slots):
        load(index).start()
    for index in range(len(jobs)):
        slot = index % slots
        load(index).wait()
        if index >= slots:
            for made in stores(index - slots):
                made.wait()
        outward[slot] = inward[slot].astype(f32)
        for made in stores(index):
            made.start()
        if index + slots < len(jobs):
            load(index + slots).start()
    for index in range(len(jobs) - slots, len(jobs)):
        for made in stores(index):
            made.wait()


def place_gradients(full, width, hidden, size_1):
    model = full.shape[2]
    anywhere = pl.BlockSpec(memory_space=pl.ANY)
    slots = 4
    shapes = (
        (1, 3, model, 2 * width),
        (1, 2 * width, model),
        (1, model, 2 * hidden),
        (1, 2 * hidden, model),
        (3, model, 2 * width),
        (2 * width, model),
    )
    return pl.pallas_call(
        partial(place_kernel, width, hidden, size_1),
        out_shape=[jax.ShapeDtypeStruct(shape, f32) for shape in shapes],
        in_specs=[anywhere],
        out_specs=[anywhere] * 6,
        scratch_shapes=[
            pltpu.VMEM((slots, width, model), bf16),
            pltpu.VMEM((slots, width, model), f32),
            pltpu.SemaphoreType.DMA((slots,)),
            pltpu.SemaphoreType.DMA((slots, model // width)),
        ],
        compiler_params=pltpu.CompilerParams(vmem_limit_bytes=VMEM_LIMIT),
        name="place_gradients",
    )(full)


def pack_small(arrays, width):
    flat = jnp.concatenate([array.astype(f32).reshape(-1) for array in arrays])
    return jnp.pad(flat, (0, -flat.size % (8 * width))).reshape(-1, width)


def unpack_small(packed, shapes):
    flat = packed.reshape(packed.shape[0], -1)
    found, at = [], 0
    for shape in shapes:
        size = 1
        for extent in shape:
            size *= extent
        found.append(flat[:, at : at + size].reshape((packed.shape[0],) + tuple(shape)))
        at += size
    return found


def local_part(
    tokens, valid_mask, buckets, state_init, norm_gain, norm_shift, w_qkv, w_out, rel_bias, w_up, up_bias,
    w_down, down_bias, state_gain, state_shift, w_state_qkv, w_state_out, gate_bias, cotangent,
):
    block_len = valid_mask.shape[1]
    model = tokens.shape[3]
    core = lax.axis_index("section")
    bucket_count, chip_heads = rel_bias.shape[1:]
    heads = chip_heads // 2
    hidden = w_up.shape[2] // 2
    valid = valid_mask[:, :, 0].astype(f32)
    packed = pack_small([norm_gain[0], norm_shift[0], down_bias[0], up_bias[0], rel_bias[0]], model)
    *weights, small_all = share_weights(
        block_len, w_qkv[0], w_out[0], w_up[0], w_down[0], w_state_qkv, w_state_out, packed
    )
    gains, shifts, down_biases, up_biases, rels = unpack_small(
        small_all, [(2, model), (2, model), (1, model), (1, 2 * hidden), (bucket_count, chip_heads)]
    )
    small = SimpleNamespace(
        gain=gains,
        shift=shifts,
        down_bias=down_biases,
        up_bias=lax.dynamic_slice_in_dim(up_biases, core * hidden, hidden, 2),
        sgain=state_gain[None],
        sshift=state_shift[None],
        gate=jax.nn.sigmoid(gate_bias)[None],
    )
    rels = lax.dynamic_slice_in_dim(rels, core * heads, heads, 2)
    back = jnp.concatenate([buckets[:1], buckets[:0:-1]])
    back_hot = back[:, None] == jnp.arange(bucket_count)[None, :]
    row0 = jnp.sum(jnp.where(back_hot[None, None], jnp.swapaxes(rels, 1, 2)[:, :, None, :], 0.0), axis=-1)
    rows = tokens[:, :, 0, :]
    state = state_init[:, 0, :]
    kept0 = forward_layer(0, block_len, small, row0[0], valid, weights, rows, state)
    kept1 = forward_layer(1, block_len, small, row0[1], valid, weights, kept0.acts, state)
    acts = jnp.where(core == 0, kept0.acts, kept1.acts)[None, :, :, None, :]
    final_state = kept1.final[:, None, :]
    grad1 = backward_layer(
        1, block_len, small, row0[1], valid, weights, cotangent[:, :, 0, :], kept0.acts, state, kept1
    )
    grad0 = backward_layer(0, block_len, small, row0[0], valid, weights, grad1.ig, rows, state, kept0)
    input_grads = jnp.where(core == 0, grad0.ig, grad1.ig)[None, :, :, None, :]
    full, sums = sum_gradients(
        lax.axis_size("dp"), grad1.dw, grad0.dw, jnp.concatenate([grad0.small, grad1.small])
    )
    width = heads * (w_qkv.shape[3] // chip_heads)
    sums = sums.reshape(3, 2, SMALL_ROWS, model)
    everywhere = sums[2]
    own = lax.dynamic_index_in_dim(everywhere, core, 0, keepdims=False)
    by_core = jnp.where(core == 0, sums[:2], sums[1::-1])
    by_core = lax.dynamic_index_in_dim(by_core, core, 1, keepdims=False)
    qkv_grad, out_grad, up_grad, down_grad, state_qkv_grad, state_out_grad = place_gradients(
        full, width, hidden, grad1.dw.shape[0]
    )
    by_distance = by_core[:, BY_DISTANCE, : heads * block_len].reshape(chip_heads, block_len)
    by_bucket = jnp.sum(jnp.where(back_hot[:, :, None], by_distance.T[:, None, :], 0.0), axis=0)
    return (
        acts,
        input_grads,
        final_state,
        own[GAIN0 : GAIN1 + 1][None],
        own[SHIFT0 : SHIFT1 + 1][None],
        qkv_grad,
        out_grad,
        by_bucket[None],
        up_grad,
        by_core[:, UP_BIAS, :hidden].reshape(1, 2 * hidden),
        down_grad,
        own[DOWN_BIAS][None],
        everywhere[1, SGAIN],
        everywhere[1, SSHIFT],
        state_qkv_grad,
        state_out_grad,
        everywhere[1, GATE],
    )


def solution(mesh):
    in_specs = (
        P(None, "mp", "dp", None),
        P(None, None, "dp"),
        P(),
        P("mp", "dp", None),
        P("section", None, None),
        P("section", None, None),
        P("section", None, None, "mp"),
        P("section", "mp", None),
        P("section", None, "mp"),
        P("section", None, "mp"),
        P("section", "mp"),
        P("section", "mp", None),
        P("section", None),
        P(),
        P(),
        P(None, None, "mp"),
        P("mp", None),
        P(),
        P(None, "mp", "dp", None),
    )
    out_specs = (
        P("section", None, "mp", "dp", None),
        P("section", None, "mp", "dp", None),
        P("mp", "dp", None),
        P("section", None, None),
        P("section", None, None),
        P("section", None, None, "mp"),
        P("section", "mp", None),
        P("section", None, "mp"),
        P("section", None, "mp"),
        P("section", "mp"),
        P("section", "mp", None),
        P("section", None),
        P(),
        P(),
        P(None, None, "mp"),
        P("mp", None),
        P(),
    )
    return jax.shard_map(local_part, mesh=mesh, in_specs=in_specs, out_specs=out_specs, check_vma=False)
```

time: 1950 us -> 697 us (0.36)
  waiting for transfers between devices: 920 us -> 0 us
  Pallas kernels: 0 us -> 658 us
  matrix products: 442 us -> 0 us
  local copies, waits for them, and re-layouts: 281 us -> 20.7 us
  other arithmetic: 194 us -> 7.88 us
  blocking collectives: 65.5 us -> 0 us
    pallas_call x0 -> x7, Pallas kernels: none -> 658 us  [the longest x1 299 us: sum_gradients(): pl.pallas_call(partial(sum_kernel, n, subs), out_shape=(jax.ShapeDtypeStr...]
    psum x1 -> x0, waiting for transfers between devices: 447 us -> none  [local(): lax.psum(qkv_grad.astype(jnp.bfloat16), 'dp').astype(jnp.float32)]
    dot_general x112 -> x0, matrix products: 442 us -> none  [the longest x3 45.2 us: local(): jnp.einsum('tbd,df->tbf', forward_mlp_in, up_own, preferred_element_type=...]
    reduce_scatter x15 -> x0, waiting for transfers between devices: 256 us -> none  [the longest x3 97.5 us: local(): lax.psum_scatter(jnp.concatenate([token_term, state_term], axis=1).reshap...]
    all_gather x18 -> x0, waiting for transfers between devices: 214 us -> none  [the longest x3 61.6 us: local(): forward_mlp_in = lax.all_gather(mlp_loc, 'mp', axis=0, tiled=True)]
    reduce_sum x50 -> x2, other arithmetic: 90 us -> 0.8 us  [the longest x1 0.68 us: local_part(): jnp.sum(jnp.where(back_hot[:, :, None], by_distance.T[:, None, :], 0.0),...]
    another operation x42 -> x2, local copies, waits for them, and re-layouts: 85.7 us -> 0.12 us  [the longest x1 0.1 us: pack_small(): flat = jnp.concatenate([array.astype(f32).reshape(-1) for array in arrays])]
    unnamed x570 -> x20, local copies, waits for them, and re-layouts: 84.5 us -> 10.2 us
  transfers between devices with their start and end apart: 41 -> 0, of which waited for: 29 -> 0; matrix products, arithmetic and copies ran while one was open for 26% -> 0% of each run, Pallas kernels for 0% -> 0%
where the time goes in v1:
time: 697 us; the launch traced here: 687 us
  Pallas kernels  658 us (94%)
  local copies, waits for them, and re-layouts  20.7 us (3%)
  other arithmetic  7.88 us (1%)
    pallas_call x1, Pallas kernels, sum_gradients(): pl.pallas_call(partial(sum_kernel, n, subs), out_shape=(jax.ShapeDtypeStr...  299 us
    pallas_call x2, Pallas kernels, backward_layer(): pl.pallas_call(partial(backward_kernel, layer, [*ins, *far_ins, *outs, *s...  172 us
    pallas_call x2, Pallas kernels, forward_layer(): pl.pallas_call(partial(forward_kernel, layer, [*ins, *far_ins, *outs, *sc...  155 us
    pallas_call x1, Pallas kernels, place_gradients(): pl.pallas_call(partial(place_kernel, width, hidden, size_1), out_shape=[j...  17.8 us

profile of v1, /device:TPU:0, one launch (start us, length us, event | category | flops | bytes accessed | tf_op | source)
XLA Modules:
  0.0 687.5 jit_solution(4991093223480317117)
XLA Ops:
  0.7 1.2 slice.110
  1.9 0.8 slice.111
  2.6 0.1 reverse
  2.7 0.1 slice.153
  2.8 0.7 pad_add_fusion
  3.5 1.3 fusion.1.refs_6_.refs_5_
  4.8 1.3 add_divide_fusion
  6.1 0.8 copy.52
  6.9 0.1 reshape_squeeze.17
  7.0 0.7 bitcast_dynamic-update-slice_fusion.1
  7.7 0.7 bitcast_dynamic-update-slice_fusion
  8.4 0.7 constant_dynamic-update-slice_fusion.2
  9.1 0.7 constant_dynamic-update-slice_fusion.1
  9.8 0.6 reshape.140.small
  10.4 13.3 %share_weights.1 = (bf16[2,3,1024,256]{3,2,1,0:T(8,128)(2,1)}, bf16[2,256,1024]{2,1,0:T(8,128)(2,1)}, bf16[2,1024,1024]{2,1,0:T(8,128)(2,1)}, bf16[2,1024,1024]{...) custom-call(bf16[3,1024,512]{2,1,0:T(8,128)(2,1)} %bitcast.61, ...), custom_call_target="tpu_custom_call" | custom-call | tf_op jit(solution)/shard_map/share_weights/pallas_call | solution.py:194
  23.7 0.9 copy.62
  24.6 0.7 fusion.4
  25.3 0.1 slice_reduce_fusion.1
  25.4 0.6 squeeze.85.refs_2_.refs_3_
  26.0 0.6 squeeze.84.refs_1_.refs_2_
  26.6 0.6 squeeze.82.refs_2_.refs_3_
  27.2 0.6 squeeze.81.refs_1_.refs_2_
  27.8 0.1 reshape.142
  27.9 0.1 dynamic-slice_bitcast_fusion
  28.0 0.1 copy.53
  28.1 0.1 select_reduce_fusion.1
  28.2 0.6 slice_bitcast_fusion
  28.8 65.0 %forward_local.1 = (bf16[2,512,1024]{2,1,0:T(8,128)(2,1)}, bf16[2,512,768]{2,1,0:T(8,128)(2,1)}, f32[2,512,128]{2,1,0:T(8,128)}, bf16[2,512,256]{2,1,0:T(8,128)(...) custom-call(bf16[2,256,1024]{2,1,0:T(8,128)(2,1)} %bitcast.59, ...), custom_call_target="tpu_custom_call" | custom-call | tf_op jit(solution)/shard_map/forward_local/pallas_call | solution.py:571
  93.8 0.0 copy-start
  93.9 90.2 %forward_recurrent.1 = (bf16[2,512,1024]{2,1,0:T(8,128)(2,1)}, bf16[2,512,768]{2,1,0:T(8,128)(2,1)}, f32[2,512,128]{2,1,0:T(8,128)}, bf16[2,512,256]{2,1,0:T(8,1...) custom-call(bf16[2,256,1024]{2,1,0:T(8,128)(2,1)} %get-tuple-element, ...), custom_call_target="tpu_custom_call" | custom-call | tf_op jit(solution)/shard_map/forward_recurrent/pallas_call | solution.py:571
  184.1 0.0 copy-done
  184.1 1.1 select_bitcast_fusion.1
  185.2 101.6 %backward_recurrent.1 = (bf16[4096,1024]{1,0:T(8,128)(2,1)}, f32[16,1024]{1,0:T(8,128)}, f32[2,256,1024]{2,1,0:T(8,128)}) custom-call(bf16[2,256,1024]{2,1,0:T(8,128)(2,1)} %bitcast.74, bf16[2,256,1024]{2,1,0:T(8,128)(2,1)} %get-tuple-element.66.refs_0_.refs_1_, f32[2,1024]{1,0:T(2,128)} %squeeze.84.refs_1_.refs_2_, f32[2,1024]{1,0:T(2,128)} %squeeze.85.refs_2_.refs_3_, ...), custom_call_target="tpu_custom_call" | custom-call | tf_op jit(solution)/shard_map/backward_recurrent/pallas_call | solution.py:1043
  286.8 0.0 copy-start.1
  286.8 70.5 %backward_local.1 = (bf16[3072,1024]{1,0:T(8,128)(2,1)}, f32[16,1024]{1,0:T(8,128)}, f32[2,256,1024]{2,1,0:T(8,128)}) custom-call(f32[2,256,1024]{2,1,0:T(8,128)} %get-tuple-element.83.refs_0_, bf16[2,256,1024]{2,1,0:T(8,128)(2,1)} %bitcast.60, f32[2,1024]{1,0:T(2,128)} %squeeze.81.refs_1_.refs_2_, f32[2,1024]{1,0:T(2,128)} %squeeze.82.refs_2_.refs_3_, ...), custom_call_target="tpu_custom_call" | custom-call | tf_op jit(solution)/shard_map/backward_local/pallas_call | solution.py:1043
  357.3 0.0 copy-done.1
  357.3 2.0 select_bitcast_fusion
  359.3 0.0 copy-start.3
  359.3 0.0 copy-start.4
  359.3 0.0 copy-start.2
  359.4 3.5 copy.58
  362.8 0.0 copy-done.3
  362.8 0.0 copy-done.4
  362.8 0.7 pad_maximum_fusion.small
  363.5 0.0 copy-done.2
  363.5 2.0 copy.59
  365.6 299.1 %sum_gradients.1 = (bf16[2,7168,1024]{2,1,0:T(8,128)(2,1)}, f32[3,32,1024]{2,1,0:T(8,128)}) custom-call(bf16[4096,1024]{1,0:T(8,128)(2,1)} %get-tuple-element.93.parts_1, bf16[3072,1024]{1,0:T(8,128)(2,1)} %get-tuple-element.94.parts_0, f32[32,1024]{1,0:T(8,128)} %pad_maximum_fusion.small), custom_call_target="tpu_custom_call" | custom-call | tf_op jit(solution)/shard_map/sum_gradients/pallas_call | solution.py:1223
  664.7 0.9 slice.119
  665.6 1.0 slice.122
  666.6 0.6 fusion.2
  667.2 0.6 constant_dynamic-slice_fusion
  667.9 0.6 fusion.3
  668.5 0.7 select_reduce_fusion
  669.2 17.8 %place_gradients.1 = (f32[1,3,1024,512]{3,2,1,0:T(8,128)}, f32[1,512,1024]{2,1,0:T(8,128)}, f32[1,1024,2048]{2,1,0:T(8,128)}, f32[1,2048,1024]{2,1,0:T(8,128)}, ...) custom-call(bf16[2,7168,1024]{2,1,0:T(8,128)(2,1)} %get-tuple-element.98.full), custom_call_target="tpu_custom_call" | custom-call | tf_op jit(solution)/shard_map/place_gradients/pallas_call | solution.py:1327
  (9 shorter events, 0.1 us)
Async XLA Ops:
  93.8 90.3 %copy-start = (bf16[2,256,1024]{2,1,0:T(8,128)(2,1)S(1)}, bf16[2,256,1024]{2,1,0:T(8,128)(2,1)}, u32[]{:S(2)}) copy-start(bf16[2,256,1024]{2,1,0:T(8,128)(2,1)} %get-tuple-element.66.refs_0_.refs_1_) | copy-start | bytes 3145732
  286.8 70.5 %copy-start.1 = (f32[2,256,1024]{2,1,0:T(8,128)S(1)}, f32[2,256,1024]{2,1,0:T(8,128)}, u32[]{:S(2)}) copy-start(f32[2,256,1024]{2,1,0:T(8,128)} %get-tuple-element.83.refs_0_) | copy-start | bytes 6291460
  359.3 3.5 copy-start.3
  359.3 3.5 copy-start.4
  359.3 4.2 copy-start.2

commit v2 on v1

--- a/solution.py
+++ b/solution.py
@@ -84,9 +84,15 @@
         self.copies.append(made)
         return made
 
+    def sent(self, *copies):
+        for made in copies:
+            made.wait_send()
+        self.copies = [None if any(held is made for made in copies) else held for held in self.copies]
+
     def drain(self):
         for made in self.copies:
-            made.wait_send()
+            if made is not None:
+                made.wait_send()
 
 
 class Local:
@@ -153,6 +159,9 @@
         total = self.part[self.place.rows(), :].astype(f32) + self.near[1].astype(f32)
         self.across.wait_recv()
         return total + self.far[...].astype(f32)
+
+    def release(self):
+        self.net.sent(self.first, self.second, self.across)
 
 
 def share_kernel(place_rows, qkv, out, up, down, sqkv, sout, small, *rest):
@@ -582,6 +591,305 @@
     return SimpleNamespace(**dict(zip(outs, results)))
 
 
+def ring_place(n, c, d):
+    if n % 2:
+        at = d
+
+        def index_at(p):
+            return p
+
+    else:
+        a, b = d // 2, d % 2
+        at = a + b * (n - 1 - 2 * a)
+
+        def index_at(p):
+            b = p // (n // 2)
+            return 2 * (p + b * (n - 1 - 2 * p)) + b
+
+    def flip(p):
+        return p + c * (n - 1 - 2 * p)
+
+    return flip(at), lambda p: index_at(flip(p))
+
+
+class Ring:
+    def __init__(self, n):
+        self.n, self.c = n, lax.axis_index("section")
+        self.q, index_at = ring_place(n, self.c, lax.axis_index("dp"))
+        self.after = {"dp": index_at((self.q + 1) % n)}
+        self.before = {"dp": index_at((self.q + n - 1) % n)}
+        self.core, self.chip = {"section": 1 - self.c}, {"mp": 1 - lax.axis_index("mp")}
+
+    def meet(self):
+        barrier = pltpu.get_barrier_semaphore()
+        for other in (self.after, self.before, self.core, self.chip):
+            pl.semaphore_signal(barrier, inc=1, device_id=other, device_id_type=MESH)
+        pl.semaphore_wait(barrier, 4)
+
+
+def remote(source, target, send, recv, to):
+    return pltpu.make_async_remote_copy(
+        src_ref=source, dst_ref=target, send_sem=send, recv_sem=recv, device_id=to, device_id_type=MESH
+    )
+
+
+def ring_subs(n, rows, most):
+    return max(k for k in range(1, most + 1) if rows // n % (16 * k) == 0)
+
+
+def ring_scratch(n, rows, model, most):
+    subs = ring_subs(n, rows, most)
+    sems = pltpu.SemaphoreType.DMA
+    return dict(
+        held=pltpu.VMEM((n - 1, rows // n, model), bf16),
+        rs_send=sems((n - 1, subs)),
+        rs_recv=sems((n - 1, subs)),
+        ag_send=sems((n - 1, subs)),
+        ag_recv=sems((n - 1, subs)),
+        core_send=sems((n, subs)),
+        core_recv=sems((n, subs)),
+        own_sems=sems((subs,)),
+    )
+
+
+class RingSum:
+    def __init__(self, ring, mine, full, held, rs_send, rs_recv, ag_send, ag_recv, core_send, core_recv, own_sems):
+        self.ring, self.mine, self.full, self.held = ring, mine, full, held
+        self.rs_send, self.rs_recv, self.ag_send, self.ag_recv = rs_send, rs_recv, ag_send, ag_recv
+        self.core_send, self.core_recv, self.own_sems = core_send, core_recv, own_sems
+        self.chunk, self.subs = held.shape[1], own_sems.shape[0]
+        self.sub = self.chunk // self.subs
+        self.half = (ring.n - 1) * self.subs
+        self.total = 2 * self.half
+        self.done = 0
+
+    def rows(self, owner, k):
+        owner = (owner + 2 * self.ring.n) % self.ring.n
+        return pl.ds(pl.multiple_of(owner * self.chunk + k * self.sub, self.sub), self.sub)
+
+    def piece(self, k):
+        return slice(k * self.sub, (k + 1) * self.sub) if isinstance(k, int) else pl.ds(
+            pl.multiple_of(k * self.sub, self.sub), self.sub
+        )
+
+    def summed(self, s, k):
+        return self.held.at[s, self.piece(k)]
+
+    def gathered(self, s, k):
+        return self.full.at[self.ring.c, self.rows(self.ring.q + 1 - s, k)]
+
+    def reduce(self, s, k, source):
+        return remote(source, self.summed(s, k), self.rs_send.at[s, k], self.rs_recv.at[s, k], self.ring.after)
+
+    def gather(self, s, k, source):
+        return remote(source, self.gathered(s, k), self.ag_send.at[s, k], self.ag_recv.at[s, k], self.ring.after)
+
+    def to_core(self, s, k, source):
+        return remote(source, self.gathered(s, k), self.core_send.at[s, k], self.core_recv.at[s, k], self.ring.core)
+
+    def from_core(self, s, k):
+        n, q = self.ring.n, self.ring.q
+        target = self.full.at[1 - self.ring.c, self.rows(n - q - s, k)]
+        return remote(target, target, self.core_send.at[s, k], self.core_recv.at[s, k], self.ring.core)
+
+    def own(self, k):
+        return pltpu.make_async_copy(self.summed(self.ring.n - 2, k), self.gathered(0, k), self.own_sems.at[k])
+
+    def start(self):
+        for k in range(self.subs):
+            self.reduce(0, k, self.mine.at[self.rows(self.ring.q, k)]).start()
+
+    def add(self, s, k):
+        self.reduce(s, k, self.summed(s, k)).wait_recv()
+        self.held[s, self.piece(k), :] = (
+            self.held[s, self.piece(k), :].astype(f32)
+            + self.mine[self.rows(self.ring.q - 1 - s, k), :].astype(f32)
+        ).astype(bf16)
+
+    def add_middle(self, s, k):
+        self.add(s, k)
+        self.reduce(s + 1, k, self.summed(s, k)).start()
+
+    def add_last(self, s, k):
+        self.add(s, k)
+        self.gather(0, k, self.summed(s, k)).start()
+        self.to_core(0, k, self.summed(s, k)).start()
+        self.own(k).start()
+
+    def pass_middle(self, s, k):
+        at = self.gathered(s + 1, k)
+        self.gather(s, k, at).wait_recv()
+        self.gather(s + 1, k, at).start()
+        self.to_core(s + 1, k, at).start()
+
+    def pass_last(self, s, k):
+        at = self.gathered(s + 1, k)
+        self.gather(s, k, at).wait_recv()
+        self.to_core(s + 1, k, at).start()
+
+    def pump_one(self, t):
+        last = self.ring.n - 2
+        s, k = t // self.subs, t % self.subs
+        kinds = (
+            (s < last, self.add_middle, s),
+            (s == last, self.add_last, s),
+            ((s > last) & (s < 2 * last + 1), self.pass_middle, s - last - 1),
+            (s == 2 * last + 1, self.pass_last, s - last - 1),
+        )
+        for here, act, step in kinds:
+            if isinstance(t, int):
+                if here:
+                    act(step, k)
+            else:
+                pl.when(here)(partial(act, step, k))
+
+    def pump(self, count=1):
+        for _ in range(min(count, self.total - self.done)):
+            self.pump_one(self.done)
+            self.done += 1
+
+    def pumps_in(self, loop_steps, each):
+        each = min(each, (self.total - self.done) // loop_steps)
+        base = self.done
+        self.done += each * loop_steps
+
+        def pump(index):
+            for piece in range(each):
+                self.pump_one(base + index * each + piece)
+
+        return pump
+
+    def run(self, until):
+        last = self.ring.n - 2
+        for first, end, act in (
+            (0, last, self.add_middle),
+            (last, last + 1, self.add_last),
+            (last + 1, 2 * last + 1, self.pass_middle),
+            (2 * last + 1, 2 * last + 2, self.pass_last),
+        ):
+            while self.done < min(end * self.subs, until) and self.done % self.subs:
+                self.pump()
+            step, stop = self.done // self.subs, min(end, until // self.subs)
+            if first <= step < stop:
+                base = last + 1 if first > last else 0
+
+                @pl.loop(step - base, stop - base)
+                def _(s):
+                    for k in range(self.subs):
+                        act(s, k)
+
+                self.done = stop * self.subs
+
+    def release_mine(self):
+        for k in range(self.subs):
+            self.reduce(0, k, self.mine.at[self.rows(self.ring.q, k)]).wait_send()
+
+    def finish(self, released=False):
+        self.run(self.total)
+        if not released:
+            self.release_mine()
+        last = self.ring.n - 2
+
+        @pl.loop(0, last + 2)
+        def _(s):
+            for k in range(self.subs):
+                self.from_core(s, k).wait_recv()
+                self.to_core(s, k, self.gathered(s, k)).wait_send()
+
+        @pl.loop(0, last + 1)
+        def _(s):
+            for k in range(self.subs):
+                self.gather(s, k, self.gathered(s, k)).wait_send()
+
+        @pl.loop(0, last)
+        def _(s):
+            for k in range(self.subs):
+                self.reduce(s + 1, k, self.summed(s, k)).wait_send()
+
+        for k in range(self.subs):
+            self.own(k).wait()
+
+
+def sum_kernel(n, parts, small, full, small_out, mine, small_held, small_sum, small_far, *rest):
+    ring_refs, (small_send, small_recv, local_sems) = rest[:-3], rest[-3:]
+    ring = Ring(n)
+    flow = RingSum(ring, mine, full, *ring_refs)
+
+    def small_step(s, first):
+        source = small if first else small_held.at[s - 1]
+        return remote(source, small_held.at[s], small_send.at[s], small_recv.at[s], ring.after)
+
+    load = pltpu.make_async_copy(parts, mine, local_sems.at[0])
+    load.start()
+    ring.meet()
+    small_step(0, True).start()
+    load.wait()
+    flow.start()
+
+    @pl.loop(0, n - 2)
+    def _(s):
+        for k in range(flow.subs):
+            flow.add_middle(s, k)
+        small_step(s, True).wait_recv()
+        small_step(s + 1, False).start()
+
+    flow.done = (n - 2) * flow.subs
+    flow.run(flow.half)
+    small_step(n - 2, True).wait_recv()
+    small_out[0] = small[...]
+
+    @pl.loop(0, n - 1)
+    def _(s):
+        small_out[0] += small_held[s]
+
+    between = remote(small_out.at[0], small_out.at[1], small_send.at[n - 1], small_recv.at[n - 1], ring.core)
+    between.start()
+    between.wait_recv()
+    small_sum[...] = small_out[0] + small_out[1]
+    across = remote(small_sum, small_far, small_send.at[n], small_recv.at[n], ring.chip)
+    across.start()
+    across.wait_recv()
+    small_out[2] = small_sum[...] + small_far[...]
+    flow.finish()
+
+    @pl.loop(0, n - 1)
+    def _(s):
+        small_step(s, True).wait_send()
+
+    between.wait_send()
+    across.wait_send()
+
+
+def sum_gradients(n, parts, small):
+    rows, model = parts.shape
+    anywhere = pl.BlockSpec(memory_space=pl.ANY)
+    inside = pl.BlockSpec(memory_space=pltpu.VMEM)
+    sems = pltpu.SemaphoreType.DMA
+    return pl.pallas_call(
+        partial(sum_kernel, n),
+        out_shape=(
+            jax.ShapeDtypeStruct((2, rows, model), bf16),
+            jax.ShapeDtypeStruct((3,) + small.shape, f32),
+        ),
+        in_specs=[anywhere, inside],
+        out_specs=[anywhere, inside],
+        scratch_shapes=[
+            pltpu.VMEM((rows, model), bf16),
+            pltpu.VMEM((n - 1,) + small.shape, f32),
+            pltpu.VMEM(small.shape, f32),
+            pltpu.VMEM(small.shape, f32),
+            *ring_scratch(n, rows, model, 6).values(),
+            sems((n + 1,)),
+            sems((n + 1,)),
+            sems((1,)),
+        ],
+        compiler_params=pltpu.CompilerParams(
+            collective_id=5, has_side_effects=True, vmem_limit_bytes=VMEM_LIMIT
+        ),
+        name="sum_gradients",
+    )(parts, small)
+
+
 def norm_back(rows, gain, grad):
     normed, scale = norm_parts(rows)
     inner = grad * gain
@@ -594,7 +902,7 @@
 SMALL_ROWS = 16
 
 
-def backward_kernel(layer, names, *refs):
+def backward_kernel(layer, n, ring_names, names, *refs):
     r = SimpleNamespace(**dict(zip(names, refs)))
     rec = layer == 1
     heads, length = r.row0.shape
@@ -607,7 +915,12 @@
     net, local = Net(r.send_sems, r.recv_sems), Local(r.local_sems)
     chunk = min(128, length)
 
-    place.meet()
+    ring = Ring(n)
+    r.act, r.pre_v = r.work.at[:model], r.work.at[model:]
+    if not rec:
+        parts = local.copy(r.parts, r.mine)
+    flow = RingSum(ring, r.work if rec else r.mine, r.full, *[getattr(r, name) for name in ring_names])
+    ring.meet()
     wdown = local.copy(r.wdown.at[layer], r.wdown_v)
     pre = local.copy(r.pre, r.pre_v)
     wup = local.copy(r.wup.at[layer], r.wup_v)
@@ -646,12 +959,10 @@
 
     scatter_count = [0]
 
-    def scatter():
+    def scatter(slot):
         index = scatter_count[0]
         scatter_count[0] += 1
-        return Scatter(
-            place, net, r.part.at[index], r.near.at[index], r.out.at[index], r.far.at[index]
-        )
+        return Scatter(place, net, r.part.at[slot], r.near.at[index], r.out.at[slot], r.far.at[index])
 
     def block_rows(block):
         return slice(block * length, (block + 1) * length)
@@ -698,7 +1009,7 @@
         add_small(SHIFT1, by_shift)
         add_small(DOWN_BIAS, jnp.sum(grad, axis=0, keepdims=True))
         total = grad + by_rows
-        r.dh[block] = total
+        r.ig_v[block, place.core_rows(), :] = total
         r.hg[pl.ds(place_row(block), place.quarter), :] = total.astype(bf16)
 
     def place_row(block):
@@ -732,9 +1043,11 @@
         qkv = r.qkv_v.at[block]
         prev = r.qkv_v.at[block - 1] if block > 0 else None
         state = r.sqkv_v.at[block] if rec else None
+        pump = flow.pumps_in(length // chunk, 1)
 
         @pl.loop(0, length // chunk)
         def _(index):
+            pump(index)
             at = pl.ds(pl.multiple_of(index * chunk, chunk), chunk)
             block_at = pl.ds(pl.multiple_of(block * length + index * chunk, chunk), chunk)
             for head in range(heads):
@@ -787,9 +1100,11 @@
 
     def recur_back():
         qkv, state = r.qkv_v.at[0], r.sqkv_v.at[0]
+        pump = flow.pumps_in(length // chunk, 1)
 
         @pl.loop(0, length // chunk)
         def _(index):
+            pump(index)
             at = pl.ds(pl.multiple_of(index * chunk, chunk), chunk)
             for head in range(heads):
                 q_at, k_at, v_at = (columns(head, part) for part in range(3))
@@ -841,7 +1156,7 @@
         add_small(GAIN0, by_gain)
         add_small(SHIFT0, by_shift)
         own = r.ig_v.at[block, place.core_rows()]
-        own[...] = r.dh[block] + by_rows
+        own[...] += by_rows
         return net.copy(own, own, place.core)
 
     def take_state(rows, from_state):
@@ -864,61 +1179,84 @@
                 folded, axis=0, keepdims=True
             )
 
-    at_qkv, at_out, at_up = 0, 3 * width, 4 * width
-    at_down = at_up + model
-    at_sqkv = at_down + hidden
-    at_sout = at_sqkv + 3 * width
-
-    feed = [scatter(), scatter()]
-    inputs = [scatter(), scatter()]
+    if rec:
+        at_qkv, at_sqkv = 0, 4 * width
+    else:
+        at_up, at_down, at_qkv = 0, model, model + hidden
+    at_out = 3 * width
+
+    feed = [scatter(0), scatter(1)]
+    inputs = [scatter(2 if rec else 0), scatter(1)]
     grads = [gather(r.g.at[block_rows(block)]) for block in range(2)]
     hiddens = [gather(r.hg.at[block_rows(block)]) for block in range(2)]
     if rec:
-        states = [scatter(), scatter()]
+        states = [scatter(0), scatter(0)]
         updates = gather(r.ug)
     for block in (1, 0):
         r.g[pl.ds(place_row(block), place.quarter), :] = own_grad(block).astype(bf16)
         grads[block].start()
     fill_bias(r.bias, r.row0)
+    if not rec:
+        local.wait(parts)
+        flow.start()
     grads[1].forward()
     local.wait(wdown, pre, wup)
     grads[1].finish()
+    if not rec:
+        flow.pump(2)
     feed_back(1)
     reduce_back([(r.dpre.at[block_rows(1)], r.wup_v)], feed[1])
     grads[0].forward()
+    if not rec:
+        flow.pump(2)
     grads[0].finish()
     feed_back(0)
     feed[1].middle()
+    if not rec:
+        flow.pump(2)
     reduce_back([(r.dpre.at[block_rows(0)], r.wup_v)], feed[0])
     local.wait(hidden_rows)
     take_feed(1, feed[1])
     hiddens[1].start()
     feed[0].middle()
     weight_grad(r.act, r.g, r.pre_v)
-    down_out = local.copy(r.pre_v, r.dw.at[at_down:at_sqkv])
     hiddens[1].forward()
+    local.wait(wn)
+    weight_grad(r.wn_v, r.dpre, r.act)
+    if rec:
+        flow.start()
+    else:
+        flow.pump(2)
+        feed_out = [local.copy(r.act, r.dw.at[at_up:at_down]), local.copy(r.pre_v, r.dw.at[at_down:at_qkv])]
     take_feed(0, feed[0])
     hiddens[0].start()
+    u_in = local.copy(r.u, r.wn_v)
     hiddens[1].finish()
     local.wait(*attention)
     branch_back(1)
+    flow.pump(1)
     attend_back(1)
     close_keys(1)
+    feed[0].release()
+    feed[1].release()
     if rec:
         close_state(1)
         state_back(1, states[1])
     hiddens[0].forward()
+    flow.pump(1)
     local.wait(wqkv)
     input_back(1, inputs[1])
     if rec:
         states[1].middle()
     hiddens[0].finish()
     branch_back(0)
+    flow.pump(1)
     inputs[1].middle()
     if rec:
         local.wait(*chain)
         gate = r.gate[...]
         by_state = take_state(r.s1_v[...], states[1])
+        states[1].release()
         before = r.state[place.core_rows(), :].astype(f32)
         add_small(
             GATE,
@@ -929,48 +1267,54 @@
     attend_back(0)
     if rec:
         updates.forward()
+        flow.pump(1)
         updates.finish()
         r.dsout[...] = dot_nt(r.ug[...], r.wsout_v[...]).astype(bf16)
         recur_back()
     close_keys(0)
+    flow.pump(1)
     input_back(0, inputs[0])
+    flow.pump(1)
     if rec:
         close_state(0)
         state_back(0, states[0])
+        flow.pump(1)
     sent = [take_input(1, inputs[1])]
     inputs[0].middle()
     if rec:
         states[0].middle()
-    local.wait(wn)
-    weight_grad(r.wn_v, r.dpre, r.act)
-    up_out = local.copy(r.act, r.dw.at[at_up:at_down])
-    u_in = local.copy(r.u, r.wn_v)
     weight_grad(r.att_v, r.hg, r.dpre, at_out)
-    if rec:
-        local.wait(down_out)
-        sn_in = local.copy(r.sn, r.pre_v)
+    flow.pump(1)
     close_bias()
     local.wait(u_in)
     projection_grad(r.wn_v, r.dqkv, r.dpre)
-    local.copy(r.dpre, r.dw.at[at_qkv:at_up])
-    if rec:
-        local.wait(sn_in, up_out)
+    local.copy(r.dpre, r.dw.at[at_qkv : at_qkv + 4 * width])
+    flow.pump(1)
+    if rec:
         r.dsqkv[block_rows(1), 0:width] = jnp.zeros((length, width), bf16)
-        projection_grad(r.pre_v, r.dsqkv, r.act)
-        weight_grad(r.sout_v.at[0], r.ug, r.act, at_sout - at_sqkv)
+        sn_in = local.copy(r.sn, r.wn_v)
+        flow.run(flow.half)
+        flow.release_mine()
+        local.wait(sn_in)
+        projection_grad(r.wn_v, r.dsqkv, r.act)
+        flow.pump(1)
+        weight_grad(r.sout_v.at[0], r.ug, r.act, at_out)
         local.copy(r.act, r.dw.at[at_sqkv:])
+        flow.pump(1)
     sent.append(take_input(0, inputs[0]))
     if rec:
         take_state(r.state[place.core_rows(), :].astype(f32), states[0])
+    flow.pump(1)
     local.copy(small, r.small)
     for made in sent:
         made.wait_recv()
     local.copy(r.ig_v, r.ig)
+    flow.finish(released=rec)
     local.drain()
     net.drain()
 
 
-def backward_layer(layer, block_len, small, row0, valid, weights, grad_rows, rows, state, kept):
+def backward_layer(layer, n, block_len, small, row0, valid, weights, grad_rows, rows, state, kept, parts=None):
     rec = layer == 1
     wqkv, wout, wup, wdown = weights[:4]
     model = rows.shape[2]
@@ -981,8 +1325,10 @@
     def held(shape, dtype):
         return jax.ShapeDtypeStruct(shape, dtype)
 
-    dw_rows = 4 * width + model + hidden + (4 * width if rec else 0)
+    dw_rows = 8 * width if rec else model + hidden + 4 * width
+    ring_rows = model + hidden if rec else parts.shape[0]
     outs = dict(
+        full=held((2, ring_rows, model), bf16),
         dw=held((dw_rows, model), bf16),
         small=held((SMALL_ROWS, model), f32),
         ig=held((2, 2 * quarter, model), f32),
@@ -996,14 +1342,16 @@
 
     stacked = dict(wqkv=wqkv, wout=wout, wup=wup, wdown=wdown)
     copied = dict(
-        qkv=kept.qkv, lse=kept.lse, att=flat(kept.att), wn=flat(kept.wn), pre=flat(kept.pre), h=kept.h
-    )
-    late = dict(u=flat(kept.u))
+        qkv=kept.qkv, lse=kept.lse, att=flat(kept.att), wn=flat(kept.wn), h=kept.h
+    )
+    late = dict(pre=flat(kept.pre), u=flat(kept.u))
     if rec:
         ins.update(state=state, sgain=small.sgain, sshift=small.sshift, gate=small.gate)
         copied.update(wsqkv=weights[4], wsout=weights[5])
         copied.update(sqkv=kept.sqkv, rlse=kept.rlse, sout=kept.sout, s1=kept.s1, z=kept.z)
         late.update(sn=flat(kept.sn))
+    else:
+        late.update(parts=parts)
     far_ins = {**stacked, **copied, **late}
     scatters = 6 if rec else 4
     copies = (3 * 6 + 3 * 5 + 2) if rec else (3 * 4 + 3 * 4 + 2)
@@ -1015,17 +1363,16 @@
     scratch.update(
         g=pltpu.VMEM((2 * block_len, model), bf16),
         hg=pltpu.VMEM((2 * block_len, model), bf16),
-        act=pltpu.VMEM((2 * block_len, hidden), bf16),
+        work=pltpu.VMEM((model + hidden, model), bf16),
         dpre=pltpu.VMEM((2 * block_len, hidden), bf16),
-        dh=pltpu.VMEM((2, quarter, model), f32),
         datt=pltpu.VMEM((2, block_len, width), bf16),
         dkv=pltpu.VMEM((2, block_len, 2 * width), f32),
         dqkv=pltpu.VMEM((2 * block_len, 3 * width), bf16),
         dbias=pltpu.VMEM((heads, min(128, block_len), 2 * block_len), f32),
         bias=pltpu.VMEM((heads, min(128, block_len), 2 * block_len), f32),
-        part=pltpu.VMEM((scatters, block_len, model), bf16),
+        part=pltpu.VMEM((scatters // 2, block_len, model), bf16),
         near=pltpu.VMEM((scatters, 2, quarter, model), bf16),
-        out=pltpu.VMEM((scatters, quarter, model), bf16),
+        out=pltpu.VMEM((scatters // 2, quarter, model), bf16),
         far=pltpu.VMEM((scatters, quarter, model), bf16),
         send_sems=pltpu.SemaphoreType.DMA((copies,)),
         recv_sems=pltpu.SemaphoreType.DMA((copies,)),
@@ -1038,10 +1385,14 @@
             dskv=pltpu.VMEM((block_len, 2 * width), f32),
             dsqkv=pltpu.VMEM((2 * block_len, 3 * width), bf16),
         )
+    else:
+        scratch.update(mine=pltpu.VMEM((ring_rows, model), bf16))
+    ring_refs = ring_scratch(n, ring_rows, model, 2)
+    scratch.update(ring_refs)
     anywhere = pl.BlockSpec(memory_space=pl.ANY)
     inside = pl.BlockSpec(memory_space=pltpu.VMEM)
     results = pl.pallas_call(
-        partial(backward_kernel, layer, [*ins, *far_ins, *outs, *scratch]),
+        partial(backward_kernel, layer, n, list(ring_refs), [*ins, *far_ins, *outs, *scratch]),
         out_shape=tuple(outs.values()),
         in_specs=[inside] * len(ins) + [anywhere] * len(far_ins),
         out_specs=[anywhere] * len(outs),
@@ -1054,238 +1405,50 @@
     return SimpleNamespace(**dict(zip(outs, results)))
 
 
-def ring_place(n, c, d):
-    if n % 2:
-        at = d
-
-        def index_at(p):
-            return p
-
-    else:
-        a, b = d // 2, d % 2
-        at = a + b * (n - 1 - 2 * a)
-
-        def index_at(p):
-            b = p // (n // 2)
-            return 2 * (p + b * (n - 1 - 2 * p)) + b
-
-    def flip(p):
-        return p + c * (n - 1 - 2 * p)
-
-    return flip(at), lambda p: index_at(flip(p))
-
-
-def sum_kernel(
-    n, subs, parts_1, parts_0, small, full, small_out, mine, held, small_held, small_sum, small_far,
-    rs_send, rs_recv, ag_send, ag_recv, core_send, core_recv, small_send, small_recv, local_sems,
+def place_kernel(
+    width, hidden, feed_1, rest_1, full_0, qkv, out, up, down, sqkv, sout, inward, outward, in_sems, out_sems
 ):
-    c, x, d = lax.axis_index("section"), lax.axis_index("mp"), lax.axis_index("dp")
-    q, index_at = ring_place(n, c, d)
-    after, before = {"dp": index_at((q + 1) % n)}, {"dp": index_at((q + n - 1) % n)}
-    core, chip = {"section": 1 - c}, {"mp": 1 - x}
-    chunk = mine.shape[0] // n
-    sub = chunk // subs
-
-    def rows(owner, k):
-        return pl.ds(pl.multiple_of(owner * chunk + k * sub, sub), sub)
-
-    def piece(k):
-        return slice(k * sub, (k + 1) * sub)
-
-    def remote(source, target, send, recv, to):
-        return pltpu.make_async_remote_copy(
-            src_ref=source, dst_ref=target, send_sem=send, recv_sem=recv, device_id=to, device_id_type=MESH
-        )
-
-    def reduce_first(k):
-        return remote(mine.at[rows(q, k)], held.at[0, piece(k)], rs_send.at[0, k], rs_recv.at[0, k], after)
-
-    def reduce_next(s, k):
-        return remote(held.at[s - 1, piece(k)], held.at[s, piece(k)], rs_send.at[s, k], rs_recv.at[s, k], after)
-
-    def gathered(s, k):
-        return full.at[c, rows((q + 1 - s + n) % n, k)]
-
-    def gather(s, k, source=None):
-        target = gathered(s, k)
-        source = target if source is None else source
-        return remote(source, target, ag_send.at[s, k], ag_recv.at[s, k], after)
-
-    def to_core(s, k, source=None):
-        target = gathered(s, k)
-        source = target if source is None else source
-        return remote(source, target, core_send.at[s, k], core_recv.at[s, k], core)
-
-    def from_core(s, k):
-        target = full.at[1 - c, rows((n - q - s + n) % n, k)]
-        return remote(target, target, core_send.at[s, k], core_recv.at[s, k], core)
-
-    def small_step(s, first):
-        source = small if first else small_held.at[s - 1]
-        return remote(source, small_held.at[s], small_send.at[s], small_recv.at[s], after)
-
-    barrier = pltpu.get_barrier_semaphore()
-    for other in (after, before, core, chip):
-        pl.semaphore_signal(barrier, inc=1, device_id=other, device_id_type=MESH)
-    size_1 = parts_1.shape[0]
-    loads = [
-        pltpu.make_async_copy(parts_1, mine.at[:size_1], local_sems.at[0]),
-        pltpu.make_async_copy(parts_0, mine.at[size_1:], local_sems.at[1]),
-    ]
-    for made in loads:
-        made.start()
-    pl.semaphore_wait(barrier, 4)
-    small_step(0, True).start()
-    for made in loads:
-        made.wait()
-    for k in range(subs):
-        reduce_first(k).start()
-
-    def add_own(s, k):
-        held[s, piece(k), :] = (
-            held[s, piece(k), :].astype(f32) + mine[rows((q + n - 1 - s) % n, k), :].astype(f32)
-        ).astype(bf16)
-
-    @pl.loop(0, n - 2)
-    def _(s):
-        for k in range(subs):
-            remote(held.at[s, piece(k)], held.at[s, piece(k)], rs_send.at[s, k], rs_recv.at[s, k], after).wait_recv()
-            add_own(s, k)
-            reduce_next(s + 1, k).start()
-        small_step(s, True).wait_recv()
-        small_step(s + 1, False).start()
-
-    last = n - 2
-    finals = []
-    for k in range(subs):
-        summed = held.at[last, piece(k)]
-        remote(summed, summed, rs_send.at[last, k], rs_recv.at[last, k], after).wait_recv()
-        add_own(last, k)
-        gather(0, k, summed).start()
-        to_core(0, k, summed).start()
-        made = pltpu.make_async_copy(summed, gathered(0, k), local_sems.at[k])
-        made.start()
-        finals.append(made)
-
-    small_step(last, True).wait_recv()
-    small_out[0] = small[...]
-
-    @pl.loop(0, n - 1)
-    def _(s):
-        small_out[0] += small_held[s]
-
-    between = remote(small_out.at[0], small_out.at[1], small_send.at[n - 1], small_recv.at[n - 1], core)
-    between.start()
-    between.wait_recv()
-    small_sum[...] = small_out[0] + small_out[1]
-    across = remote(small_sum, small_far, small_send.at[n], small_recv.at[n], chip)
-    across.start()
-    across.wait_recv()
-    small_out[2] = small_sum[...] + small_far[...]
-
-    @pl.loop(0, n - 2)
-    def _(s):
-        for k in range(subs):
-            gather(s, k, gathered(s + 1, k)).wait_recv()
-            gather(s + 1, k).start()
-            to_core(s + 1, k).start()
-
-    for k in range(subs):
-        gather(last, k, gathered(last + 1, k)).wait_recv()
-        to_core(last + 1, k).start()
-
-    @pl.loop(0, n)
-    def _(s):
-        for k in range(subs):
-            from_core(s, k).wait_recv()
-            to_core(s, k).wait_send()
-
-    @pl.loop(0, n - 1)
-    def _(s):
-        for k in range(subs):
-            remote(held.at[s, piece(k)], held.at[s, piece(k)], rs_send.at[s, k], rs_recv.at[s, k], after).wait_send()
-            gather(s, k).wait_send()
-        small_step(s, True).wait_send()
-
-    between.wait_send()
-    across.wait_send()
-    for made in finals:
-        made.wait()
-
-
-def sum_gradients(n, parts_1, parts_0, small):
-    total, model = parts_1.shape[0] + parts_0.shape[0], parts_1.shape[1]
-    chunk = total // n
-    subs = max(k for k in range(1, 9) if chunk % (16 * k) == 0)
-    anywhere = pl.BlockSpec(memory_space=pl.ANY)
-    inside = pl.BlockSpec(memory_space=pltpu.VMEM)
-    sems = pltpu.SemaphoreType.DMA
-    return pl.pallas_call(
-        partial(sum_kernel, n, subs),
-        out_shape=(
-            jax.ShapeDtypeStruct((2, total, model), bf16),
-            jax.ShapeDtypeStruct((3,) + small.shape, f32),
-        ),
-        in_specs=[anywhere, anywhere, inside],
-        out_specs=[anywhere, inside],
-        scratch_shapes=[
-            pltpu.VMEM((total, model), bf16),
-            pltpu.VMEM((n - 1, chunk, model), bf16),
-            pltpu.VMEM((n - 1,) + small.shape, f32),
-            pltpu.VMEM(small.shape, f32),
-            pltpu.VMEM(small.shape, f32),
-            sems((n - 1, subs)),
-            sems((n - 1, subs)),
-            sems((n - 1, subs)),
-            sems((n - 1, subs)),
-            sems((n, subs)),
-            sems((n, subs)),
-            sems((n + 1,)),
-            sems((n + 1,)),
-            sems((max(2, subs),)),
-        ],
-        compiler_params=pltpu.CompilerParams(
-            collective_id=5, has_side_effects=True, vmem_limit_bytes=VMEM_LIMIT
-        ),
-        name="sum_gradients",
-    )(parts_1, parts_0, small)
-
-
-def place_kernel(width, hidden, size_1, full, qkv, out, up, down, sqkv, sout, inward, outward, in_sems, out_sems):
-    model = full.shape[2]
-    base = (1 - lax.axis_index("section")) * size_1
+    model = full_0.shape[2]
+    layer = lax.axis_index("section")
     slots = inward.shape[0]
-    at_out, at_up = 3 * width, 4 * width
-    at_down = at_up + model
-    at_sqkv = at_down + hidden
-    at_sout = at_sqkv + 3 * width
+    at_rest = model + hidden
     jobs = []
     for half in range(2):
         columns = slice(half * width, (half + 1) * width)
 
-        def projection(target, row):
+        def projection(target):
             return [target.at[index : index + width, columns] for index in range(0, model, width)]
 
-        for part in range(3):
-            jobs.append((half, base + part * width, projection(qkv.at[0, part], part)))
-            jobs.append((half, at_sqkv + part * width, projection(sqkv.at[part], part)))
-        jobs.append((half, base + at_out, [out.at[0, columns]]))
-        jobs.append((half, at_sout, [sout.at[columns]]))
         for row in range(0, model, width):
             wide = slice(half * hidden, (half + 1) * hidden)
-            jobs.append((half, base + at_up + row, [up.at[0, row : row + width, wide]]))
+            jobs.append((half, (feed_1, row), row, [up.at[0, row : row + width, wide]]))
         for row in range(0, hidden, width):
             at = half * hidden + row
-            jobs.append((half, base + at_down + row, [down.at[0, at : at + width]]))
-
-    def load(index):
-        half, row, _ = jobs[index]
-        at = row if isinstance(row, int) else pl.multiple_of(row, width)
+            jobs.append((half, (feed_1, model + row), model + row, [down.at[0, at : at + width]]))
+        for part in range(3):
+            row = part * width
+            jobs.append((half, (rest_1, row), at_rest + row, projection(qkv.at[0, part])))
+            jobs.append((half, (rest_1, 4 * width + row), None, projection(sqkv.at[part])))
+        jobs.append((half, (rest_1, 3 * width), at_rest + 3 * width, [out.at[0, columns]]))
+        jobs.append((half, (rest_1, 7 * width), None, [sout.at[columns]]))
+
+    def load(index, start):
+        half, (array, row), row_0, _ = jobs[index]
         slot = index % slots
-        return pltpu.make_async_copy(full.at[half, pl.ds(at, width)], inward.at[slot], in_sems.at[slot])
+
+        def made(source, at):
+            return pltpu.make_async_copy(source.at[half, at : at + width], inward.at[slot], in_sems.at[slot])
+
+        if not start:
+            made(array, row).wait()
+        elif row_0 is None:
+            made(array, row).start()
+        else:
+            pl.when(layer == 1)(lambda: made(array, row).start())
+            pl.when(layer == 0)(lambda: made(full_0, row_0).start())
 
     def stores(index):
-        targets, slot = jobs[index][2], index % slots
+        targets, slot = jobs[index][3], index % slots
         step = model // len(targets)
         return [
             pltpu.make_async_copy(
@@ -1295,10 +1458,10 @@
         ]
 
     for index in range(slots):
-        load(index).start()
+        load(index, True)
     for index in range(len(jobs)):
         slot = index % slots
-        load(index).wait()
+        load(index, False)
         if index >= slots:
             for made in stores(index - slots):
                 made.wait()
@@ -1306,14 +1469,14 @@
         for made in stores(index):
             made.start()
         if index + slots < len(jobs):
-            load(index + slots).start()
+            load(index + slots, True)
     for index in range(len(jobs) - slots, len(jobs)):
         for made in stores(index):
             made.wait()
 
 
-def place_gradients(full, width, hidden, size_1):
-    model = full.shape[2]
+def place_gradients(feed_1, rest_1, full_0, width, hidden):
+    model = full_0.shape[2]
     anywhere = pl.BlockSpec(memory_space=pl.ANY)
     slots = 4
     shapes = (
@@ -1325,9 +1488,9 @@
         (2 * width, model),
     )
     return pl.pallas_call(
-        partial(place_kernel, width, hidden, size_1),
+        partial(place_kernel, width, hidden),
         out_shape=[jax.ShapeDtypeStruct(shape, f32) for shape in shapes],
-        in_specs=[anywhere],
+        in_specs=[anywhere] * 3,
         out_specs=[anywhere] * 6,
         scratch_shapes=[
             pltpu.VMEM((slots, width, model), bf16),
@@ -1337,7 +1500,7 @@
         ],
         compiler_params=pltpu.CompilerParams(vmem_limit_bytes=VMEM_LIMIT),
         name="place_gradients",
-    )(full)
+    )(feed_1, rest_1, full_0)
 
 
 def pack_small(arrays, width):
@@ -1394,14 +1557,15 @@
     kept1 = forward_layer(1, block_len, small, row0[1], valid, weights, kept0.acts, state)
     acts = jnp.where(core == 0, kept0.acts, kept1.acts)[None, :, :, None, :]
     final_state = kept1.final[:, None, :]
+    docs = lax.axis_size("dp")
     grad1 = backward_layer(
-        1, block_len, small, row0[1], valid, weights, cotangent[:, :, 0, :], kept0.acts, state, kept1
-    )
-    grad0 = backward_layer(0, block_len, small, row0[0], valid, weights, grad1.ig, rows, state, kept0)
+        1, docs, block_len, small, row0[1], valid, weights, cotangent[:, :, 0, :], kept0.acts, state, kept1
+    )
+    grad0 = backward_layer(
+        0, docs, block_len, small, row0[0], valid, weights, grad1.ig, rows, state, kept0, grad1.dw
+    )
     input_grads = jnp.where(core == 0, grad0.ig, grad1.ig)[None, :, :, None, :]
-    full, sums = sum_gradients(
-        lax.axis_size("dp"), grad1.dw, grad0.dw, jnp.concatenate([grad0.small, grad1.small])
-    )
+    full, sums = sum_gradients(docs, grad0.dw, jnp.concatenate([grad0.small, grad1.small]))
     width = heads * (w_qkv.shape[3] // chip_heads)
     sums = sums.reshape(3, 2, SMALL_ROWS, model)
     everywhere = sums[2]
@@ -1409,7 +1573,7 @@
     by_core = jnp.where(core == 0, sums[:2], sums[1::-1])
     by_core = lax.dynamic_index_in_dim(by_core, core, 1, keepdims=False)
     qkv_grad, out_grad, up_grad, down_grad, state_qkv_grad, state_out_grad = place_gradients(
-        full, width, hidden, grad1.dw.shape[0]
+        grad1.full, grad0.full, full, width, hidden
     )
     by_distance = by_core[:, BY_DISTANCE, : heads * block_len].reshape(chip_heads, block_len)
     by_bucket = jnp.sum(jnp.where(back_hot[:, :, None], by_distance.T[:, None, :], 0.0), axis=0)

time: 697 us -> 612 us (0.88)
  Pallas kernels: 658 us -> 572 us
    pallas_call x4, Pallas kernels: 489 us -> 404 us  [the longest x2 248 us: backward_layer(): pl.pallas_call(partial(backward_kernel, layer, n, list(ring_refs), [*ins,...]
where the time goes in v2:
time: 612 us; the launch traced here: 602 us
  Pallas kernels  572 us (93%)
  local copies, waits for them, and re-layouts  20.7 us (3%)
  other arithmetic  7.88 us (1%)
    pallas_call x2, Pallas kernels, backward_layer(): pl.pallas_call(partial(backward_kernel, layer, n, list(ring_refs), [*ins,...  248 us
    pallas_call x2, Pallas kernels, forward_layer(): pl.pallas_call(partial(forward_kernel, layer, [*ins, *far_ins, *outs, *sc...  155 us
    pallas_call x1, Pallas kernels, sum_gradients(): pl.pallas_call(partial(sum_kernel, n), out_shape=(jax.ShapeDtypeStruct((2...  138 us
    pallas_call x1, Pallas kernels, place_gradients(): pl.pallas_call(partial(place_kernel, width, hidden), out_shape=[jax.Shape...  17.8 us
    pallas_call x1, Pallas kernels, share_weights(): pl.pallas_call(partial(share_kernel, block_len), out_shape=(halved(qkv.sh...  13.3 us

profile of v2, /device:TPU:0, one launch (start us, length us, event | category | flops | bytes accessed | tf_op | source)
XLA Modules:
  0.0 602.0 jit_solution(15509812120326180513)
XLA Ops:
  0.7 1.2 slice.110
  1.9 0.8 slice.111
  2.6 0.1 reverse
  2.7 0.1 slice.153
  2.8 0.7 pad_add_fusion
  3.5 1.3 fusion.1.refs_6_.refs_5_
  4.8 1.3 add_divide_fusion
  6.1 0.8 copy.52
  6.9 0.1 reshape_squeeze.17
  7.0 0.7 bitcast_dynamic-update-slice_fusion.1
  7.7 0.7 bitcast_dynamic-update-slice_fusion
  8.4 0.7 constant_dynamic-update-slice_fusion.2
  9.1 0.7 constant_dynamic-update-slice_fusion.1
  9.8 0.6 reshape.140.small
  10.4 13.3 %share_weights.1 = (bf16[2,3,1024,256]{3,2,1,0:T(8,128)(2,1)}, bf16[2,256,1024]{2,1,0:T(8,128)(2,1)}, bf16[2,1024,1024]{2,1,0:T(8,128)(2,1)}, bf16[2,1024,1024]{...) custom-call(bf16[3,1024,512]{2,1,0:T(8,128)(2,1)} %bitcast.61, ...), custom_call_target="tpu_custom_call" | custom-call | tf_op jit(solution)/shard_map/share_weights/pallas_call | solution.py:203
  23.7 0.9 copy.62
  24.6 0.7 fusion.4
  25.3 0.1 slice_reduce_fusion.1
  25.4 0.6 squeeze.85.refs_2_.refs_3_
  26.0 0.6 squeeze.84.refs_1_.refs_2_
  26.6 0.6 squeeze.82.refs_2_.refs_3_
  27.2 0.6 squeeze.81.refs_1_.refs_2_
  27.8 0.1 reshape.142
  27.9 0.1 dynamic-slice_bitcast_fusion
  28.0 0.1 copy.53
  28.1 0.1 select_reduce_fusion.1
  28.2 0.6 slice_bitcast_fusion
  28.8 65.0 %forward_local.1 = (bf16[2,512,1024]{2,1,0:T(8,128)(2,1)}, bf16[2,512,768]{2,1,0:T(8,128)(2,1)}, f32[2,512,128]{2,1,0:T(8,128)}, bf16[2,512,256]{2,1,0:T(8,128)(...) custom-call(bf16[2,256,1024]{2,1,0:T(8,128)(2,1)} %bitcast.59, ...), custom_call_target="tpu_custom_call" | custom-call | tf_op jit(solution)/shard_map/forward_local/pallas_call | solution.py:580
  93.8 0.0 copy-start
  93.8 90.0 %forward_recurrent.1 = (bf16[2,512,1024]{2,1,0:T(8,128)(2,1)}, bf16[2,512,768]{2,1,0:T(8,128)(2,1)}, f32[2,512,128]{2,1,0:T(8,128)}, bf16[2,512,256]{2,1,0:T(8,1...) custom-call(bf16[2,256,1024]{2,1,0:T(8,128)(2,1)} %get-tuple-element, ...), custom_call_target="tpu_custom_call" | custom-call | tf_op jit(solution)/shard_map/forward_recurrent/pallas_call | solution.py:580
  183.8 0.0 copy-done
  183.8 1.1 select_bitcast_fusion.1
  184.9 141.2 %backward_recurrent.1 = (bf16[2,2048,1024]{2,1,0:T(8,128)(2,1)}, bf16[2048,1024]{1,0:T(8,128)(2,1)}, f32[16,1024]{1,0:T(8,128)}, f32[2,256,1024]{2,1,0:T(8,128)}) custom-call(bf16[2,256,1024]{2,1,0:T(8,128)(2,1)} %bitcast.74, bf16[2,256,1024]{2,1,0:T(8,128)(2,1)} %get-tuple-element.68.refs_0_.refs_1_, f32[2,1024]{1,0:T(2,128)} %squeeze.84.refs_1_.refs_2_, ...), custom_call_target="tpu_custom_call" | custom-call | tf_op jit(solution)/shard_map/backward_recurrent/pallas_call | solution.py:1394
  326.1 0.0 copy-start.1
  326.2 107.0 %backward_local.1 = (bf16[2,2048,1024]{2,1,0:T(8,128)(2,1)}, bf16[3072,1024]{1,0:T(8,128)(2,1)}, f32[16,1024]{1,0:T(8,128)}, f32[2,256,1024]{2,1,0:T(8,128)}) custom-call(f32[2,256,1024]{2,1,0:T(8,128)} %get-tuple-element.85.refs_0_, bf16[2,256,1024]{2,1,0:T(8,128)(2,1)} %bitcast.60, f32[2,1024]{1,0:T(2,128)} %squeeze.81.refs_1_.refs_2_, ...), custom_call_target="tpu_custom_call" | custom-call | tf_op jit(solution)/shard_map/backward_local/pallas_call | solution.py:1394
  433.2 0.0 copy-done.1
  433.2 2.0 select_bitcast_fusion
  435.2 0.0 copy-start.3
  435.2 0.0 copy-start.4
  435.2 0.0 copy-start.2
  435.2 3.5 copy.58
  438.7 0.0 copy-done.3
  438.7 0.0 copy-done.4
  438.7 0.7 pad_maximum_fusion.small
  439.4 0.0 copy-done.2
  439.4 2.0 copy.59
  441.4 137.8 %sum_gradients.1 = (bf16[2,3072,1024]{2,1,0:T(8,128)(2,1)}, f32[3,32,1024]{2,1,0:T(8,128)}) custom-call(bf16[3072,1024]{1,0:T(8,128)(2,1)} %get-tuple-element.96.parts, f32[32,1024]{1,0:T(8,128)} %pad_maximum_fusion.small), custom_call_target="tpu_custom_call" | custom-call | tf_op jit(solution)/shard_map/sum_gradients/pallas_call | solution.py:868
  579.2 0.9 slice.119
  580.1 1.0 slice.122
  581.1 0.6 fusion.2
  581.7 0.6 constant_dynamic-slice_fusion
  582.4 0.6 fusion.3
  583.1 0.7 select_reduce_fusion
  583.8 17.8 %place_gradients.1 = (f32[1,3,1024,512]{3,2,1,0:T(8,128)}, f32[1,512,1024]{2,1,0:T(8,128)}, f32[1,1024,2048]{2,1,0:T(8,128)}, f32[1,2048,1024]{2,1,0:T(8,128)}, ...) custom-call(bf16[2,2048,1024]{2,1,0:T(8,128)(2,1)} %get-tuple-element.100.feed_1, ...), custom_call_target="tpu_custom_call" | custom-call | tf_op jit(solution)/shard_map/place_gradients/pallas_call | solution.py:1490
  (9 shorter events, 0.1 us)
Async XLA Ops:
  93.8 90.0 %copy-start = (bf16[2,256,1024]{2,1,0:T(8,128)(2,1)S(1)}, bf16[2,256,1024]{2,1,0:T(8,128)(2,1)}, u32[]{:S(2)}) copy-start(bf16[2,256,1024]{2,1,0:T(8,128)(2,1)} %get-tuple-element.68.refs_0_.refs_1_) | copy-start | bytes 3145732
  326.1 107.0 %copy-start.1 = (f32[2,256,1024]{2,1,0:T(8,128)S(1)}, f32[2,256,1024]{2,1,0:T(8,128)}, u32[]{:S(2)}) copy-start(f32[2,256,1024]{2,1,0:T(8,128)} %get-tuple-element.85.refs_0_) | copy-start | bytes 6291460
  435.2 3.5 copy-start.3
  435.2 3.5 copy-start.4
  435.2 4.2 copy-start.2

commit v3 on v2

--- a/solution.py
+++ b/solution.py
@@ -164,9 +164,10 @@
         self.net.sent(self.first, self.second, self.across)
 
 
-def share_kernel(place_rows, qkv, out, up, down, sqkv, sout, small, *rest):
-    targets, staged, (local_sems, send_sems, recv_sems) = rest[:7], rest[7:14], rest[14:]
-    place = Place(place_rows)
+def share_kernel(block_len, qkv, out, up, down, sqkv, sout, small, cot, *rest):
+    targets, cot_all = rest[:7], rest[7]
+    staged, cot_staged, (local_sems, send_sems, recv_sems) = rest[8:15], rest[15], rest[16:]
+    place = Place(block_len)
     net, local = Net(send_sems, recv_sems), Local(local_sems)
     layer = place.c
 
@@ -181,19 +182,32 @@
     sent = [half(array, axis, 1 - place.c) for array, axis in shared] + [small]
     finals = [target.at[layer] for target in targets[:4]] + [targets[4], targets[5], targets[6].at[layer]]
     place.meet()
+    across, near = [], []
+    for block in range(2):
+        own, target = cot.at[block, place.core_rows()], cot_all.at[block, place.rows()]
+        across.append(net.copy(own, target, place.chip))
+        near.append(net.copy(own, target, place.core))
     for source, target in zip(sent, finals[:4] + finals[6:]):
-        net.copy(source, target, place.core)
+        near.append(net.copy(source, target, place.core))
+    cot_in = [local.copy(cot.at[block, place.core_rows()], cot_staged.at[block]) for block in range(2)]
     inward = [local.copy(source, stage) for source, stage in zip(kept, staged)]
+    for block in range(2):
+        local.wait(cot_in[block])
+        local.copy(cot_staged.at[block], cot_all.at[block, place.rows()])
     for index, stage, target in zip(inward, staged, finals):
         local.wait(index)
         local.copy(stage, target)
-    for made in net.copies:
+    for block in range(2):
+        across[block].wait_recv()
+        passed = cot_all.at[block, place.rows(x_other=True)]
+        near.append(net.copy(passed, passed, place.core))
+    for made in near:
         made.wait_recv()
     local.drain()
     net.drain()
 
 
-def share_weights(block_len, qkv, out, up, down, sqkv, sout, small):
+def share_weights(block_len, qkv, out, up, down, sqkv, sout, small, cot):
     def halved(shape, axis, stacked=True):
         shape = list(shape)
         shape[axis] //= 2
@@ -210,24 +224,26 @@
             halved(sqkv.shape, 2, False),
             halved(sout.shape, 0, False),
             jax.ShapeDtypeStruct((2,) + small.shape, f32),
+            jax.ShapeDtypeStruct((2, block_len, cot.shape[2]), bf16),
         ),
-        in_specs=[anywhere] * 7,
-        out_specs=[anywhere] * 7,
+        in_specs=[anywhere] * 8,
+        out_specs=[anywhere] * 8,
         scratch_shapes=[
             pltpu.VMEM(halved(array.shape, axis, False).shape, bf16)
             for array, axis in ((qkv, 2), (out, 0), (up, 1), (down, 0), (sqkv, 2), (sout, 0))
         ]
         + [
             pltpu.VMEM(small.shape, f32),
-            pltpu.SemaphoreType.DMA((14,)),
-            pltpu.SemaphoreType.DMA((5,)),
-            pltpu.SemaphoreType.DMA((5,)),
+            pltpu.VMEM((2, block_len // 4, cot.shape[2]), bf16),
+            pltpu.SemaphoreType.DMA((18,)),
+            pltpu.SemaphoreType.DMA((11,)),
+            pltpu.SemaphoreType.DMA((11,)),
         ],
         compiler_params=pltpu.CompilerParams(
             collective_id=0, has_side_effects=True, vmem_limit_bytes=VMEM_LIMIT
         ),
         name="share_weights",
-    )(qkv, out, up, down, sqkv, sout, small)
+    )(qkv, out, up, down, sqkv, sout, small, cot)
 
 
 def fill_bias(bias, row0):
@@ -400,7 +416,7 @@
             at = pl.ds(pl.multiple_of(index * step, step), step)
             pre = dot(r.wn_v[block], r.wup_v[:, at]) + r.up_bias[:, at]
             r.pre_v[block, :, at] = pre.astype(bf16)
-            r.act[block, :, at] = (0.5 * pre * (1.0 + lax.erf(pre * (0.5**0.5)))).astype(bf16)
+            r.act_v[block, :, at] = (0.5 * pre * (1.0 + lax.erf(pre * (0.5**0.5)))).astype(bf16)
 
     def take_result(block, from_down):
         rows = r.h_v[block] + from_down.finish() + r.down_bias[...]
@@ -436,17 +452,21 @@
     if rec:
         recur(0)
         reduce_from(r.sout_v.at[0], r.wsout_v, update[0])
+    else:
+        attend(0)
     first[1].forward()
     if rec:
         update[0].middle()
-    attend(0)
+        attend(0)
     reduce_from(r.att_v.at[0], r.wout_v, branch[0])
+    if not rec:
+        branch[0].middle()
     first[1].finish()
     project(r.u_v.at[1], r.wqkv_v, r.qkv_v.at[1])
     local.copy(r.u_v, r.u)
     local.copy(r.qkv_v, r.qkv)
-    branch[0].middle()
-    if rec:
+    if rec:
+        branch[0].middle()
         update_rows = update[0].finish()
         r.z_v[...] = update_rows
         state_rows = gate * r.state[place.core_rows(), :].astype(f32) + (1.0 - gate) * update_rows
@@ -466,7 +486,12 @@
         project(r.sn_v.at[1], r.wsqkv_v, r.sqkv_v.at[1])
         local.copy(r.sn_v, r.sn)
         local.copy(r.sqkv_v, r.sqkv)
+        recur(1)
+        reduce_from(r.sout_v.at[1], r.wsout_v, update[1])
+        local.copy(r.sout_v, r.sout)
+        local.copy(r.rlse_v, r.rlse)
         attend(1)
+        update[1].middle()
         reduce_from(r.att_v.at[1], r.wout_v, branch[1])
     local.copy(r.att_v, r.att)
     local.copy(r.lse_v, r.lse)
@@ -475,31 +500,25 @@
     second[0].finish()
     local.wait(*load_mlp)
     feed_up(0)
-    reduce_from(r.act.at[0], r.wdown_v, result[0])
+    reduce_from(r.act_v.at[0], r.wdown_v, result[0])
     take_branch(1, branch[1])
     second[1].start()
     local.copy(r.h_v, r.h)
     result[0].middle()
-    if rec:
-        recur(1)
-        reduce_from(r.sout_v.at[1], r.wsout_v, update[1])
-        local.copy(r.sout_v, r.sout)
-        local.copy(r.rlse_v, r.rlse)
     second[1].forward()
     second[1].finish()
     local.copy(r.wn_v, r.wn)
     feed_up(1)
     local.copy(r.pre_v, r.pre)
-    reduce_from(r.act.at[1], r.wdown_v, result[1])
+    local.copy(r.act_v, r.act)
+    reduce_from(r.act_v.at[1], r.wdown_v, result[1])
     sent = [take_result(0, result[0])]
     result[1].middle()
-    if rec:
-        update[1].middle()
-    sent.append(take_result(1, result[1]))
     if rec:
         own = r.final_v.at[place.core_rows()]
         own[...] = gate * r.s1_v[...] + (1.0 - gate) * update[1].finish()
         sent.append(net.copy(own, own, place.core))
+    sent.append(take_result(1, result[1]))
     for made in sent:
         made.wait_recv()
     local.copy(r.acts_v, r.acts)
@@ -527,6 +546,7 @@
         att=held((2, block_len, width), bf16),
         wn=held((2, block_len, model), bf16),
         pre=held((2, block_len, hidden), bf16),
+        act=held((2, block_len, hidden), bf16),
         h=held((2, quarter, model), f32),
         acts=held((2, 2 * quarter, model), bf16),
     )
@@ -560,7 +580,6 @@
         wout_v=pltpu.VMEM(wout.shape[1:], bf16),
         wup_v=pltpu.VMEM(wup.shape[1:], bf16),
         wdown_v=pltpu.VMEM(wdown.shape[1:], bf16),
-        act=pltpu.VMEM((2, block_len, hidden), bf16),
         bias=pltpu.VMEM((heads, min(128, block_len), 2 * block_len), f32),
         part=pltpu.VMEM((scatters, block_len, model), bf16),
         near=pltpu.VMEM((scatters, 2, quarter, model), bf16),
@@ -916,10 +935,34 @@
     chunk = min(128, length)
 
     ring = Ring(n)
-    r.act, r.pre_v = r.work.at[:model], r.work.at[model:]
-    if not rec:
+    r.act, r.by_down = r.work.at[:hidden], r.work.at[hidden:]
+    ring_refs = [[getattr(r, name) for name in flow_names] for flow_names in ring_names]
+    if rec:
+        up_flow = RingSum(ring, r.act, r.full.at[:, :model], *ring_refs[0])
+        down_flow = RingSum(ring, r.by_down, r.full.at[:, model:], *ring_refs[1])
+        act = [local.copy(r.act_in, r.act), local.copy(r.g_in, r.g)]
+    else:
+        rest_flow = RingSum(ring, r.mine, r.full, *ring_refs[0])
         parts = local.copy(r.parts, r.mine)
-    flow = RingSum(ring, r.work if rec else r.mine, r.full, *[getattr(r, name) for name in ring_names])
+        act = [local.copy(r.act_in, r.act)]
+    flows = []
+
+    def launch(flow):
+        flow.start()
+        flows.append(flow)
+
+    def tick(count=1):
+        for _ in range(count):
+            for flow in flows:
+                flow.pump()
+
+    def tick_at(index, *steps):
+        for step in steps:
+
+            @pl.when(index == step)
+            def _():
+                tick()
+
     ring.meet()
     wdown = local.copy(r.wdown.at[layer], r.wdown_v)
     pre = local.copy(r.pre, r.pre_v)
@@ -980,7 +1023,6 @@
             pre = r.pre_v[rows, at].astype(f32)
             by_act = dot_nt(r.g[rows, :], r.wdown_v[at, :])
             below = 0.5 * (1.0 + lax.erf(pre * (0.5**0.5)))
-            r.act[rows, at] = (pre * below).astype(bf16)
             by_pre = by_act * (below + pre * jnp.exp(-0.5 * pre * pre) * 0.3989422804014327)
             small[UP_BIAS : UP_BIAS + 1, at] += jnp.sum(by_pre, axis=0, keepdims=True)
             r.dpre[rows, at] = by_pre.astype(bf16)
@@ -1026,6 +1068,7 @@
 
     def projection_grad(normed, grads, target):
         for part in range(3):
+            tick()
             to = slice(part * width, (part + 1) * width)
 
             @pl.loop(0, model // width)
@@ -1043,11 +1086,10 @@
         qkv = r.qkv_v.at[block]
         prev = r.qkv_v.at[block - 1] if block > 0 else None
         state = r.sqkv_v.at[block] if rec else None
-        pump = flow.pumps_in(length // chunk, 1)
 
         @pl.loop(0, length // chunk)
         def _(index):
-            pump(index)
+            tick_at(index, *((1, 2, 3) if rec and block else (1, 3)))
             at = pl.ds(pl.multiple_of(index * chunk, chunk), chunk)
             block_at = pl.ds(pl.multiple_of(block * length + index * chunk, chunk), chunk)
             for head in range(heads):
@@ -1100,11 +1142,10 @@
 
     def recur_back():
         qkv, state = r.qkv_v.at[0], r.sqkv_v.at[0]
-        pump = flow.pumps_in(length // chunk, 1)
 
         @pl.loop(0, length // chunk)
         def _(index):
-            pump(index)
+            tick_at(index, 2)
             at = pl.ds(pl.multiple_of(index * chunk, chunk), chunk)
             for head in range(heads):
                 q_at, k_at, v_at = (columns(head, part) for part in range(3))
@@ -1187,54 +1228,70 @@
 
     feed = [scatter(0), scatter(1)]
     inputs = [scatter(2 if rec else 0), scatter(1)]
-    grads = [gather(r.g.at[block_rows(block)]) for block in range(2)]
+    if not rec:
+        grads = [gather(r.g.at[block_rows(block)]) for block in range(2)]
     hiddens = [gather(r.hg.at[block_rows(block)]) for block in range(2)]
     if rec:
         states = [scatter(0), scatter(0)]
         updates = gather(r.ug)
-    for block in (1, 0):
-        r.g[pl.ds(place_row(block), place.quarter), :] = own_grad(block).astype(bf16)
-        grads[block].start()
+    if not rec:
+        for block in (1, 0):
+            r.g[pl.ds(place_row(block), place.quarter), :] = own_grad(block).astype(bf16)
+            grads[block].start()
+        local.wait(parts)
+        launch(rest_flow)
     fill_bias(r.bias, r.row0)
-    if not rec:
-        local.wait(parts)
-        flow.start()
-    grads[1].forward()
+    local.wait(*act)
+    if rec:
+        weight_grad(r.act, r.g, r.by_down)
+        launch(down_flow)
+    else:
+        tick()
+        grads[1].forward()
+        tick()
+        grads[1].finish()
     local.wait(wdown, pre, wup)
-    grads[1].finish()
-    if not rec:
-        flow.pump(2)
     feed_back(1)
+    tick()
     reduce_back([(r.dpre.at[block_rows(1)], r.wup_v)], feed[1])
-    grads[0].forward()
-    if not rec:
-        flow.pump(2)
-    grads[0].finish()
+    if rec:
+        tick()
+    else:
+        grads[0].forward()
+        tick()
+        grads[0].finish()
     feed_back(0)
     feed[1].middle()
+    tick()
+    reduce_back([(r.dpre.at[block_rows(0)], r.wup_v)], feed[0])
+    tick()
+    feed[0].middle()
     if not rec:
-        flow.pump(2)
-    reduce_back([(r.dpre.at[block_rows(0)], r.wup_v)], feed[0])
+        weight_grad(r.act, r.g, r.by_down)
+        down_out = local.copy(r.by_down, r.dw.at[at_down:at_qkv])
+    tick()
+    local.wait(wn)
+    weight_grad(r.wn_v, r.dpre, r.act)
+    if rec:
+        launch(up_flow)
+        sn_in = local.copy(r.sn, r.pre_v)
+    else:
+        local.copy(r.act, r.dw.at[at_up:at_down])
+    tick()
+    u_in = local.copy(r.u, r.wn_v)
     local.wait(hidden_rows)
     take_feed(1, feed[1])
     hiddens[1].start()
-    feed[0].middle()
-    weight_grad(r.act, r.g, r.pre_v)
-    hiddens[1].forward()
-    local.wait(wn)
-    weight_grad(r.wn_v, r.dpre, r.act)
-    if rec:
-        flow.start()
-    else:
-        flow.pump(2)
-        feed_out = [local.copy(r.act, r.dw.at[at_up:at_down]), local.copy(r.pre_v, r.dw.at[at_down:at_qkv])]
+    tick(2)
     take_feed(0, feed[0])
     hiddens[0].start()
-    u_in = local.copy(r.u, r.wn_v)
+    tick(2)
+    hiddens[1].forward()
+    tick()
     hiddens[1].finish()
     local.wait(*attention)
     branch_back(1)
-    flow.pump(1)
+    tick()
     attend_back(1)
     close_keys(1)
     feed[0].release()
@@ -1242,17 +1299,17 @@
     if rec:
         close_state(1)
         state_back(1, states[1])
+        tick()
     hiddens[0].forward()
-    flow.pump(1)
     local.wait(wqkv)
     input_back(1, inputs[1])
     if rec:
         states[1].middle()
+    tick()
     hiddens[0].finish()
     branch_back(0)
-    flow.pump(1)
-    inputs[1].middle()
-    if rec:
+    if rec:
+        tick(2)
         local.wait(*chain)
         gate = r.gate[...]
         by_state = take_state(r.s1_v[...], states[1])
@@ -1264,52 +1321,53 @@
         )
         r.ug[place.rows(), :] = ((1.0 - gate) * by_state).astype(bf16)
         updates.start()
+    inputs[1].middle()
+    tick()
     attend_back(0)
+    tick()
     if rec:
         updates.forward()
-        flow.pump(1)
+        tick()
         updates.finish()
         r.dsout[...] = dot_nt(r.ug[...], r.wsout_v[...]).astype(bf16)
         recur_back()
+        tick()
     close_keys(0)
-    flow.pump(1)
     input_back(0, inputs[0])
-    flow.pump(1)
+    tick()
     if rec:
         close_state(0)
         state_back(0, states[0])
-        flow.pump(1)
+        tick()
     sent = [take_input(1, inputs[1])]
     inputs[0].middle()
+    tick()
     if rec:
         states[0].middle()
     weight_grad(r.att_v, r.hg, r.dpre, at_out)
-    flow.pump(1)
     close_bias()
     local.wait(u_in)
     projection_grad(r.wn_v, r.dqkv, r.dpre)
     local.copy(r.dpre, r.dw.at[at_qkv : at_qkv + 4 * width])
-    flow.pump(1)
+    tick()
     if rec:
         r.dsqkv[block_rows(1), 0:width] = jnp.zeros((length, width), bf16)
-        sn_in = local.copy(r.sn, r.wn_v)
-        flow.run(flow.half)
-        flow.release_mine()
         local.wait(sn_in)
-        projection_grad(r.wn_v, r.dsqkv, r.act)
-        flow.pump(1)
-        weight_grad(r.sout_v.at[0], r.ug, r.act, at_out)
-        local.copy(r.act, r.dw.at[at_sqkv:])
-        flow.pump(1)
+        projection_grad(r.pre_v, r.dsqkv, r.g)
+        tick()
+        weight_grad(r.sout_v.at[0], r.ug, r.g, at_out)
+        local.copy(r.g, r.dw.at[at_sqkv:])
     sent.append(take_input(0, inputs[0]))
     if rec:
         take_state(r.state[place.core_rows(), :].astype(f32), states[0])
-    flow.pump(1)
     local.copy(small, r.small)
     for made in sent:
         made.wait_recv()
     local.copy(r.ig_v, r.ig)
-    flow.finish(released=rec)
+    while any(flow.done < flow.total for flow in flows):
+        tick()
+    for flow in flows:
+        flow.finish()
     local.drain()
     net.drain()
 
@@ -1342,19 +1400,19 @@
 
     stacked = dict(wqkv=wqkv, wout=wout, wup=wup, wdown=wdown)
     copied = dict(
-        qkv=kept.qkv, lse=kept.lse, att=flat(kept.att), wn=flat(kept.wn), h=kept.h
-    )
-    late = dict(pre=flat(kept.pre), u=flat(kept.u))
+        qkv=kept.qkv, lse=kept.lse, att=flat(kept.att), wn=flat(kept.wn), pre=flat(kept.pre), h=kept.h
+    )
+    late = dict(act_in=flat(kept.act), u=flat(kept.u))
     if rec:
         ins.update(state=state, sgain=small.sgain, sshift=small.sshift, gate=small.gate)
         copied.update(wsqkv=weights[4], wsout=weights[5])
         copied.update(sqkv=kept.sqkv, rlse=kept.rlse, sout=kept.sout, s1=kept.s1, z=kept.z)
-        late.update(sn=flat(kept.sn))
+        late.update(sn=flat(kept.sn), g_in=flat(parts))
     else:
         late.update(parts=parts)
     far_ins = {**stacked, **copied, **late}
     scatters = 6 if rec else 4
-    copies = (3 * 6 + 3 * 5 + 2) if rec else (3 * 4 + 3 * 4 + 2)
+    copies = (3 * 6 + 3 * 3 + 2) if rec else (3 * 4 + 3 * 4 + 2)
     scratch = dict(small_v=pltpu.VMEM(outs["small"].shape, f32), ig_v=pltpu.VMEM(outs["ig"].shape, f32))
     for name, array in stacked.items():
         scratch[name + "_v"] = pltpu.VMEM(array.shape[1:], array.dtype)
@@ -1363,7 +1421,7 @@
     scratch.update(
         g=pltpu.VMEM((2 * block_len, model), bf16),
         hg=pltpu.VMEM((2 * block_len, model), bf16),
-        work=pltpu.VMEM((model + hidden, model), bf16),
+        work=pltpu.VMEM((2 * hidden, model), bf16),
         dpre=pltpu.VMEM((2 * block_len, hidden), bf16),
         datt=pltpu.VMEM((2, block_len, width), bf16),
         dkv=pltpu.VMEM((2, block_len, 2 * width), f32),
@@ -1387,12 +1445,16 @@
         )
     else:
         scratch.update(mine=pltpu.VMEM((ring_rows, model), bf16))
-    ring_refs = ring_scratch(n, ring_rows, model, 2)
-    scratch.update(ring_refs)
+    ring_names = []
+    for flow_rows in (model, hidden) if rec else (ring_rows,):
+        flow_scratch = ring_scratch(n, flow_rows, model, 2)
+        flow_scratch = {name + str(len(ring_names)): kind for name, kind in flow_scratch.items()}
+        scratch.update(flow_scratch)
+        ring_names.append(list(flow_scratch))
     anywhere = pl.BlockSpec(memory_space=pl.ANY)
     inside = pl.BlockSpec(memory_space=pltpu.VMEM)
     results = pl.pallas_call(
-        partial(backward_kernel, layer, n, list(ring_refs), [*ins, *far_ins, *outs, *scratch]),
+        partial(backward_kernel, layer, n, ring_names, [*ins, *far_ins, *outs, *scratch]),
         out_shape=tuple(outs.values()),
         in_specs=[inside] * len(ins) + [anywhere] * len(far_ins),
         out_specs=[anywhere] * len(outs),
@@ -1532,8 +1594,9 @@
     hidden = w_up.shape[2] // 2
     valid = valid_mask[:, :, 0].astype(f32)
     packed = pack_small([norm_gain[0], norm_shift[0], down_bias[0], up_bias[0], rel_bias[0]], model)
-    *weights, small_all = share_weights(
-        block_len, w_qkv[0], w_out[0], w_up[0], w_down[0], w_state_qkv, w_state_out, packed
+    cot_rows = cotangent[:, :, 0, :]
+    *weights, small_all, cot_all = share_weights(
+        block_len, w_qkv[0], w_out[0], w_up[0], w_down[0], w_state_qkv, w_state_out, packed, cot_rows
     )
     gains, shifts, down_biases, up_biases, rels = unpack_small(
         small_all, [(2, model), (2, model), (1, model), (1, 2 * hidden), (bucket_count, chip_heads)]
@@ -1559,7 +1622,7 @@
     final_state = kept1.final[:, None, :]
     docs = lax.axis_size("dp")
     grad1 = backward_layer(
-        1, docs, block_len, small, row0[1], valid, weights, cotangent[:, :, 0, :], kept0.acts, state, kept1
+        1, docs, block_len, small, row0[1], valid, weights, cot_rows, kept0.acts, state, kept1, cot_all
     )
     grad0 = backward_layer(
         0, docs, block_len, small, row0[0], valid, weights, grad1.ig, rows, state, kept0, grad1.dw

time: 612 us -> 560 us (0.915); the launches traced: 602 us -> 557 us
  Pallas kernels: 572 us -> 527 us
    pallas_call x2, Pallas kernels: 248 us -> 200 us  [backward_layer(): pl.pallas_call(partial(backward_kernel, layer, n, ring_names, [*ins, *far...]
where the time goes in v3:
time: 560 us; the launch traced here: 557 us
  Pallas kernels  527 us (94%)
  local copies, waits for them, and re-layouts  20.7 us (4%)
  other arithmetic  7.88 us (1%)
    pallas_call x2, Pallas kernels, backward_layer(): pl.pallas_call(partial(backward_kernel, layer, n, ring_names, [*ins, *far...  200 us
    pallas_call x2, Pallas kernels, forward_layer(): pl.pallas_call(partial(forward_kernel, layer, [*ins, *far_ins, *outs, *sc...  154 us
    pallas_call x1, Pallas kernels, sum_gradients(): pl.pallas_call(partial(sum_kernel, n), out_shape=(jax.ShapeDtypeStruct((2...  138 us
    pallas_call x1, Pallas kernels, place_gradients(): pl.pallas_call(partial(place_kernel, width, hidden), out_shape=[jax.Shape...  17.8 us
    pallas_call x1, Pallas kernels, share_weights(): pl.pallas_call(partial(share_kernel, block_len), out_shape=(halved(qkv.sh...  17.7 us

profile of v3, /device:TPU:0, one launch (start us, length us, event | category | flops | bytes accessed | tf_op | source)
XLA Modules:
  0.0 556.9 jit_solution(13435647128903323446)
XLA Ops:
  0.7 1.2 slice.110
  1.9 0.8 slice.111
  2.6 0.1 reverse
  2.7 0.1 slice.153
  2.8 0.7 pad_add_fusion
  3.5 1.3 fusion.1.refs_6_.refs_5_
  4.8 1.3 add_divide_fusion
  6.1 0.8 copy.52
  6.9 0.1 reshape_squeeze.17
  7.0 0.7 bitcast_dynamic-update-slice_fusion.1
  7.7 0.7 bitcast_dynamic-update-slice_fusion
  8.4 0.7 constant_dynamic-update-slice_fusion.2
  9.1 0.7 constant_dynamic-update-slice_fusion.1
  9.8 0.6 reshape.149.small
  10.4 17.7 %share_weights.1 = (bf16[2,3,1024,256]{3,2,1,0:T(8,128)(2,1)}, bf16[2,256,1024]{2,1,0:T(8,128)(2,1)}, bf16[2,1024,1024]{2,1,0:T(8,128)(2,1)}, bf16[2,1024,1024]{...) custom-call(bf16[3,1024,512]{2,1,0:T(8,128)(2,1)} %bitcast.66, ...), custom_call_target="tpu_custom_call" | custom-call | tf_op jit(solution)/shard_map/share_weights/pallas_call | solution.py:217
  28.1 0.9 copy.62
  29.0 0.7 fusion.4
  29.7 0.1 slice_reduce_fusion.1
  29.8 0.6 squeeze.86.refs_2_.refs_3_
  30.4 0.6 squeeze.85.refs_1_.refs_2_
  31.0 0.6 squeeze.83.refs_2_.refs_3_
  31.6 0.6 squeeze.82.refs_1_.refs_2_
  32.2 0.1 reshape.151
  32.3 0.1 dynamic-slice_bitcast_fusion
  32.4 0.1 copy.53
  32.5 0.1 select_reduce_fusion.1
  32.6 0.6 slice_bitcast_fusion
  33.2 62.8 %forward_local.1 = (bf16[2,512,1024]{2,1,0:T(8,128)(2,1)}, bf16[2,512,768]{2,1,0:T(8,128)(2,1)}, f32[2,512,128]{2,1,0:T(8,128)}, bf16[2,512,256]{2,1,0:T(8,128)(...) custom-call(bf16[2,256,1024]{2,1,0:T(8,128)(2,1)} %bitcast.64, ...), custom_call_target="tpu_custom_call" | custom-call | tf_op jit(solution)/shard_map/forward_local/pallas_call | solution.py:599
  96.0 0.0 copy-start
  96.0 91.0 %forward_recurrent.1 = (bf16[2,512,1024]{2,1,0:T(8,128)(2,1)}, bf16[2,512,768]{2,1,0:T(8,128)(2,1)}, f32[2,512,128]{2,1,0:T(8,128)}, bf16[2,512,256]{2,1,0:T(8,1...) custom-call(bf16[2,256,1024]{2,1,0:T(8,128)(2,1)} %get-tuple-element, ...), custom_call_target="tpu_custom_call" | custom-call | tf_op jit(solution)/shard_map/forward_recurrent/pallas_call | solution.py:599
  187.0 0.0 copy-done
  187.1 1.1 select_bitcast_fusion.1
  188.1 109.7 %backward_recurrent.1 = (bf16[2,2048,1024]{2,1,0:T(8,128)(2,1)}, bf16[2048,1024]{1,0:T(8,128)(2,1)}, f32[16,1024]{1,0:T(8,128)}, f32[2,256,1024]{2,1,0:T(8,128)}) custom-call(bf16[2,256,1024]{2,1,0:T(8,128)(2,1)} %bitcast.63, bf16[2,256,1024]{2,1,0:T(8,128)(2,1)} %get-tuple-element.71.refs_0_.refs_1_, f32[2,1024]{1,0:T(2,128)} %squeeze.85.refs_1_.refs_2_, ...), custom_call_target="tpu_custom_call" | custom-call | tf_op jit(solution)/shard_map/backward_recurrent/pallas_call | solution.py:1456
  297.8 0.0 copy-start.1
  297.8 90.5 %backward_local.1 = (bf16[2,2048,1024]{2,1,0:T(8,128)(2,1)}, bf16[3072,1024]{1,0:T(8,128)(2,1)}, f32[16,1024]{1,0:T(8,128)}, f32[2,256,1024]{2,1,0:T(8,128)}) custom-call(f32[2,256,1024]{2,1,0:T(8,128)} %get-tuple-element.90.refs_0_, bf16[2,256,1024]{2,1,0:T(8,128)(2,1)} %bitcast.65, f32[2,1024]{1,0:T(2,128)} %squeeze.82.refs_1_.refs_2_, ...), custom_call_target="tpu_custom_call" | custom-call | tf_op jit(solution)/shard_map/backward_local/pallas_call | solution.py:1456
  388.4 0.0 copy-done.1
  388.4 2.0 select_bitcast_fusion
  390.4 0.0 copy-start.3
  390.4 0.0 copy-start.4
  390.4 0.0 copy-start.2
  390.4 3.5 copy.58
  393.9 0.0 copy-done.3
  393.9 0.0 copy-done.4
  393.9 0.7 pad_maximum_fusion.small
  394.6 0.0 copy-done.2
  394.6 2.0 copy.59
  396.6 137.7 %sum_gradients.1 = (bf16[2,3072,1024]{2,1,0:T(8,128)(2,1)}, f32[3,32,1024]{2,1,0:T(8,128)}) custom-call(bf16[3072,1024]{1,0:T(8,128)(2,1)} %get-tuple-element.102.parts, f32[32,1024]{1,0:T(8,128)} %pad_maximum_fusion.small), custom_call_target="tpu_custom_call" | custom-call | tf_op jit(solution)/shard_map/sum_gradients/pallas_call | solution.py:887
  534.4 0.9 slice.119
  535.3 1.0 slice.122
  536.3 0.6 fusion.2
  536.9 0.6 constant_dynamic-slice_fusion
  537.6 0.6 fusion.3
  538.2 0.7 select_reduce_fusion
  538.9 17.8 %place_gradients.1 = (f32[1,3,1024,512]{3,2,1,0:T(8,128)}, f32[1,512,1024]{2,1,0:T(8,128)}, f32[1,1024,2048]{2,1,0:T(8,128)}, f32[1,2048,1024]{2,1,0:T(8,128)}, ...) custom-call(bf16[2,2048,1024]{2,1,0:T(8,128)(2,1)} %get-tuple-element.106.feed_1, ...), custom_call_target="tpu_custom_call" | custom-call | tf_op jit(solution)/shard_map/place_gradients/pallas_call | solution.py:1552
  (9 shorter events, 0.1 us)
Async XLA Ops:
  96.0 91.1 %copy-start = (bf16[2,256,1024]{2,1,0:T(8,128)(2,1)S(1)}, bf16[2,256,1024]{2,1,0:T(8,128)(2,1)}, u32[]{:S(2)}) copy-start(bf16[2,256,1024]{2,1,0:T(8,128)(2,1)} %get-tuple-element.71.refs_0_.refs_1_) | copy-start | bytes 3145732
  297.8 90.6 %copy-start.1 = (f32[2,256,1024]{2,1,0:T(8,128)S(1)}, f32[2,256,1024]{2,1,0:T(8,128)}, u32[]{:S(2)}) copy-start(f32[2,256,1024]{2,1,0:T(8,128)} %get-tuple-element.90.refs_0_) | copy-start | bytes 6291460
  390.4 3.5 copy-start.3
  390.4 3.5 copy-start.4
  390.4 4.2 copy-start.2

commit v4 on v3

--- a/solution.py
+++ b/solution.py
@@ -164,9 +164,10 @@
         self.net.sent(self.first, self.second, self.across)
 
 
-def share_kernel(block_len, qkv, out, up, down, sqkv, sout, small, cot, *rest):
-    targets, cot_all = rest[:7], rest[7]
-    staged, cot_staged, (local_sems, send_sems, recv_sems) = rest[8:15], rest[15], rest[16:]
+def share_kernel(block_len, qkv, out, up, down, sqkv, sout, cot, *rest):
+    smalls, targets, cot_all, small_all = rest[:5], rest[5:11], rest[11], rest[12:17]
+    staged, cot_staged, small_staged = rest[17:23], rest[23], rest[24:29]
+    local_sems, send_sems, recv_sems = rest[29:]
     place = Place(block_len)
     net, local = Net(send_sems, recv_sems), Local(local_sems)
     layer = place.c
@@ -178,23 +179,24 @@
         return array.at[tuple(index)]
 
     shared = ((qkv, 2), (out, 0), (up, 1), (down, 0))
-    kept = [half(array, axis, place.c) for array, axis in shared + ((sqkv, 2), (sout, 0))] + [small]
-    sent = [half(array, axis, 1 - place.c) for array, axis in shared] + [small]
-    finals = [target.at[layer] for target in targets[:4]] + [targets[4], targets[5], targets[6].at[layer]]
+    kept = [small.at[0] for small in smalls]
+    kept += [half(array, axis, place.c) for array, axis in shared + ((sqkv, 2), (sout, 0))]
+    sent = [small.at[0] for small in smalls] + [half(array, axis, 1 - place.c) for array, axis in shared]
+    finals = [target.at[layer] for target in (*small_all, *targets[:4])] + [targets[4], targets[5]]
     place.meet()
     across, near = [], []
     for block in range(2):
         own, target = cot.at[block, place.core_rows()], cot_all.at[block, place.rows()]
         across.append(net.copy(own, target, place.chip))
         near.append(net.copy(own, target, place.core))
-    for source, target in zip(sent, finals[:4] + finals[6:]):
+    for source, target in zip(sent, finals):
         near.append(net.copy(source, target, place.core))
     cot_in = [local.copy(cot.at[block, place.core_rows()], cot_staged.at[block]) for block in range(2)]
-    inward = [local.copy(source, stage) for source, stage in zip(kept, staged)]
+    inward = [local.copy(source, stage) for source, stage in zip(kept, (*small_staged, *staged))]
     for block in range(2):
         local.wait(cot_in[block])
         local.copy(cot_staged.at[block], cot_all.at[block, place.rows()])
-    for index, stage, target in zip(inward, staged, finals):
+    for index, stage, target in zip(inward, (*small_staged, *staged), finals):
         local.wait(index)
         local.copy(stage, target)
     for block in range(2):
@@ -207,13 +209,14 @@
     net.drain()
 
 
-def share_weights(block_len, qkv, out, up, down, sqkv, sout, small, cot):
+def share_weights(block_len, qkv, out, up, down, sqkv, sout, cot, *smalls):
     def halved(shape, axis, stacked=True):
         shape = list(shape)
         shape[axis] //= 2
         return jax.ShapeDtypeStruct(([2] if stacked else []) + shape, bf16)
 
     anywhere = pl.BlockSpec(memory_space=pl.ANY)
+    count = 7 + len(smalls)
     return pl.pallas_call(
         partial(share_kernel, block_len),
         out_shape=(
@@ -223,33 +226,57 @@
             halved(down.shape, 0),
             halved(sqkv.shape, 2, False),
             halved(sout.shape, 0, False),
-            jax.ShapeDtypeStruct((2,) + small.shape, f32),
             jax.ShapeDtypeStruct((2, block_len, cot.shape[2]), bf16),
+            *(jax.ShapeDtypeStruct((2,) + small.shape[1:], f32) for small in smalls),
         ),
-        in_specs=[anywhere] * 8,
-        out_specs=[anywhere] * 8,
+        in_specs=[anywhere] * count,
+        out_specs=[anywhere] * count,
         scratch_shapes=[
             pltpu.VMEM(halved(array.shape, axis, False).shape, bf16)
             for array, axis in ((qkv, 2), (out, 0), (up, 1), (down, 0), (sqkv, 2), (sout, 0))
         ]
+        + [pltpu.VMEM((2, block_len // 4, cot.shape[2]), bf16)]
+        + [pltpu.VMEM(small.shape[1:], f32) for small in smalls]
         + [
-            pltpu.VMEM(small.shape, f32),
-            pltpu.VMEM((2, block_len // 4, cot.shape[2]), bf16),
-            pltpu.SemaphoreType.DMA((18,)),
-            pltpu.SemaphoreType.DMA((11,)),
-            pltpu.SemaphoreType.DMA((11,)),
+            pltpu.SemaphoreType.DMA((2 * count + 2,)),
+            pltpu.SemaphoreType.DMA((count + 4,)),
+            pltpu.SemaphoreType.DMA((count + 4,)),
         ],
         compiler_params=pltpu.CompilerParams(
             collective_id=0, has_side_effects=True, vmem_limit_bytes=VMEM_LIMIT
         ),
         name="share_weights",
-    )(qkv, out, up, down, sqkv, sout, small, cot)
+    )(qkv, out, up, down, sqkv, sout, cot, *smalls)
+
+
+def back_hot(buckets, count):
+    length = buckets.shape[1]
+    hot = lax.broadcasted_iota(jnp.int32, (count, length), 0) == buckets
+    both = lax.broadcasted_iota(jnp.int32, (length, length), 0) + lax.broadcasted_iota(
+        jnp.int32, (length, length), 1
+    )
+    turn = (both == 0) | (both == length)
+    return dot(jnp.where(hot, 1.0, 0.0).astype(bf16), jnp.where(turn, 1.0, 0.0).astype(bf16)).astype(bf16)
+
+
+def in_parts(values):
+    high = values.astype(bf16)
+    rest = values - high.astype(f32)
+    middle = rest.astype(bf16)
+    return high, middle, (rest - middle.astype(f32)).astype(bf16)
+
+
+def bias_rows(rel, buckets, c):
+    hot = back_hot(buckets, rel.shape[1])
+    rows = sum(dot(part, hot) for part in in_parts(rel))
+    heads = rel.shape[0] // 2
+    return jnp.where(c == 0, rows[:heads], rows[heads:])
 
 
 def fill_bias(bias, row0):
     head_count, length = row0.shape
     for head in range(head_count):
-        start = jnp.broadcast_to(row0[head : head + 1, :], (bias.shape[1], length))
+        start = jnp.broadcast_to(row0[head : head + 1], (bias.shape[1], length))
         rolled = pltpu.roll(start, 0, axis=1, stride=1, stride_axis=0)
         bias[head, :, :length] = rolled
         bias[head, :, length:] = rolled
@@ -276,7 +303,7 @@
     r = SimpleNamespace(**dict(zip(names, refs)))
     rec = layer == 1
     length = r.u_v.shape[1]
-    heads = r.row0.shape[0]
+    heads = r.rel.shape[1] // 2
     head_size = r.att_v.shape[2] // heads
     width = heads * head_size
     scale = head_size ** (-0.5)
@@ -291,8 +318,8 @@
     if rec:
         load_state = [local.copy(r.wsqkv, r.wsqkv_v), local.copy(r.wsout, r.wsout_v)]
 
-    gain = lambda index: r.gain[index : index + 1, :]
-    shift = lambda index: r.shift[index : index + 1, :]
+    gain = lambda index: r.gain[layer, index : index + 1, :]
+    shift = lambda index: r.shift[layer, index : index + 1, :]
 
     def gather(buffer):
         return Gather(place, net, buffer)
@@ -414,12 +441,13 @@
         @pl.loop(0, columns // step)
         def _(index):
             at = pl.ds(pl.multiple_of(index * step, step), step)
-            pre = dot(r.wn_v[block], r.wup_v[:, at]) + r.up_bias[:, at]
+            bias_at = pl.ds(pl.multiple_of(place.c * columns + index * step, step), step)
+            pre = dot(r.wn_v[block], r.wup_v[:, at]) + r.up_bias[layer, :, bias_at]
             r.pre_v[block, :, at] = pre.astype(bf16)
             r.act_v[block, :, at] = (0.5 * pre * (1.0 + lax.erf(pre * (0.5**0.5)))).astype(bf16)
 
     def take_result(block, from_down):
-        rows = r.h_v[block] + from_down.finish() + r.down_bias[...]
+        rows = r.h_v[block] + from_down.finish() + r.down_bias[layer]
         own = r.acts_v.at[block, place.core_rows()]
         own[...] = rows.astype(bf16)
         return net.copy(own, own, place.core)
@@ -431,14 +459,14 @@
     if rec:
         update = [scatter(), scatter()]
         state = [gather(r.sn_v.at[block]) for block in range(2)]
-        gate = r.gate[...]
+        gate = jax.nn.sigmoid(r.gate[...])
         norm_state(r.state[place.core_rows(), :].astype(f32), 0)
         state[0].start()
     norm_first(0)
     first[0].start()
     norm_first(1)
     first[1].start()
-    fill_bias(r.bias, r.row0)
+    fill_bias(r.bias, bias_rows(r.rel[layer], r.buckets[...], place.c))
     if rec:
         state[0].forward()
     first[0].forward()
@@ -528,13 +556,13 @@
     net.drain()
 
 
-def forward_layer(layer, block_len, small, row0, valid, weights, rows, state):
+def forward_layer(layer, block_len, small, valid, weights, rows, state):
     rec = layer == 1
     wqkv, wout, wup, wdown = weights[:4]
     model = rows.shape[2]
     width, hidden = wqkv.shape[3], wup.shape[2]
     quarter = block_len // 4
-    heads = row0.shape[0]
+    heads = small.rel.shape[1] // 2
 
     def held(shape, dtype):
         return jax.ShapeDtypeStruct(shape, dtype)
@@ -552,11 +580,12 @@
     )
     ins = dict(
         x=rows,
-        gain=small.gain[layer],
-        shift=small.shift[layer],
-        up_bias=small.up_bias[layer],
-        down_bias=small.down_bias[layer],
-        row0=row0,
+        gain=small.gain,
+        shift=small.shift,
+        up_bias=small.up_bias,
+        down_bias=small.down_bias,
+        rel=small.rel,
+        buckets=small.buckets,
         valid=valid,
     )
     far_ins = dict(wqkv=wqkv, wout=wout, wup=wup, wdown=wdown)
@@ -829,7 +858,7 @@
             self.own(k).wait()
 
 
-def sum_kernel(n, parts, small, full, small_out, mine, small_held, small_sum, small_far, *rest):
+def sum_kernel(n, parts, small_0, small_1, full, small_out, mine, small_held, small_sum, small_far, small, *rest):
     ring_refs, (small_send, small_recv, local_sems) = rest[:-3], rest[-3:]
     ring = Ring(n)
     flow = RingSum(ring, mine, full, *ring_refs)
@@ -840,6 +869,8 @@
 
     load = pltpu.make_async_copy(parts, mine, local_sems.at[0])
     load.start()
+    small[: small_0.shape[0]] = small_0[...]
+    small[small_0.shape[0] :] = small_1[...]
     ring.meet()
     small_step(0, True).start()
     load.wait()
@@ -879,8 +910,9 @@
     across.wait_send()
 
 
-def sum_gradients(n, parts, small):
+def sum_gradients(n, parts, small_0, small_1):
     rows, model = parts.shape
+    both = (small_0.shape[0] + small_1.shape[0], model)
     anywhere = pl.BlockSpec(memory_space=pl.ANY)
     inside = pl.BlockSpec(memory_space=pltpu.VMEM)
     sems = pltpu.SemaphoreType.DMA
@@ -888,15 +920,16 @@
         partial(sum_kernel, n),
         out_shape=(
             jax.ShapeDtypeStruct((2, rows, model), bf16),
-            jax.ShapeDtypeStruct((3,) + small.shape, f32),
+            jax.ShapeDtypeStruct((3,) + both, f32),
         ),
-        in_specs=[anywhere, inside],
+        in_specs=[anywhere, inside, inside],
         out_specs=[anywhere, inside],
         scratch_shapes=[
             pltpu.VMEM((rows, model), bf16),
-            pltpu.VMEM((n - 1,) + small.shape, f32),
-            pltpu.VMEM(small.shape, f32),
-            pltpu.VMEM(small.shape, f32),
+            pltpu.VMEM((n - 1,) + both, f32),
+            pltpu.VMEM(both, f32),
+            pltpu.VMEM(both, f32),
+            pltpu.VMEM(both, f32),
             *ring_scratch(n, rows, model, 6).values(),
             sems((n + 1,)),
             sems((n + 1,)),
@@ -906,7 +939,7 @@
             collective_id=5, has_side_effects=True, vmem_limit_bytes=VMEM_LIMIT
         ),
         name="sum_gradients",
-    )(parts, small)
+    )(parts, small_0, small_1)
 
 
 def norm_back(rows, gain, grad):
@@ -924,7 +957,7 @@
 def backward_kernel(layer, n, ring_names, names, *refs):
     r = SimpleNamespace(**dict(zip(names, refs)))
     rec = layer == 1
-    heads, length = r.row0.shape
+    heads, length = r.rel.shape[1] // 2, r.valid.shape[1]
     head_size = r.att_v.shape[1] // heads
     width = heads * head_size
     hidden = r.wup_v.shape[1]
@@ -986,7 +1019,7 @@
         ]
     wqkv = local.copy(r.wqkv.at[layer], r.wqkv_v)
 
-    gain = lambda index: r.gain[index : index + 1, :]
+    gain = lambda index: r.gain[layer, index : index + 1, :]
     small = r.small_v
     small[...] = jnp.zeros(small.shape, f32)
     r.dkv[...] = jnp.zeros(r.dkv.shape, f32)
@@ -1240,7 +1273,7 @@
             grads[block].start()
         local.wait(parts)
         launch(rest_flow)
-    fill_bias(r.bias, r.row0)
+    fill_bias(r.bias, bias_rows(r.rel[layer], r.buckets[...], place.c))
     local.wait(*act)
     if rec:
         weight_grad(r.act, r.g, r.by_down)
@@ -1311,7 +1344,7 @@
     if rec:
         tick(2)
         local.wait(*chain)
-        gate = r.gate[...]
+        gate = jax.nn.sigmoid(r.gate[...])
         by_state = take_state(r.s1_v[...], states[1])
         states[1].release()
         before = r.state[place.core_rows(), :].astype(f32)
@@ -1372,13 +1405,13 @@
     net.drain()
 
 
-def backward_layer(layer, n, block_len, small, row0, valid, weights, grad_rows, rows, state, kept, parts=None):
+def backward_layer(layer, n, block_len, small, valid, weights, grad_rows, rows, state, kept, parts=None):
     rec = layer == 1
     wqkv, wout, wup, wdown = weights[:4]
     model = rows.shape[2]
     width, hidden = wqkv.shape[3], wup.shape[2]
     quarter = block_len // 4
-    heads = row0.shape[0]
+    heads = small.rel.shape[1] // 2
 
     def held(shape, dtype):
         return jax.ShapeDtypeStruct(shape, dtype)
@@ -1392,7 +1425,7 @@
         ig=held((2, 2 * quarter, model), f32),
     )
     ins = dict(
-        gy=grad_rows, x=rows, gain=small.gain[layer], shift=small.shift[layer], row0=row0, valid=valid
+        gy=grad_rows, x=rows, gain=small.gain, rel=small.rel, buckets=small.buckets, valid=valid
     )
 
     def flat(array):
@@ -1468,11 +1501,21 @@
 
 
 def place_kernel(
-    width, hidden, feed_1, rest_1, full_0, qkv, out, up, down, sqkv, sout, inward, outward, in_sems, out_sems
+    width, hidden, feed_1, rest_1, full_0, acts_0, acts_1, igs_0, igs_1, state, sums, buckets,
+    qkv, out, up, down, sqkv, sout, acts, igs, final, gain, shift, rel, up_bias, down_bias, sgain, sshift, gate,
+    inward, outward, acts_v, igs_v, state_v, igs_tiles, state_tiles, in_sems, out_sems, row_sems,
 ):
     model = full_0.shape[2]
     layer = lax.axis_index("section")
     slots = inward.shape[0]
+
+    rows_in = []
+    for index, (first, second, target) in enumerate(((acts_0, acts_1, acts_v), (igs_0, igs_1, igs_v))):
+        pl.when(layer == 0)(pltpu.make_async_copy(first, target, row_sems.at[index]).start)
+        pl.when(layer == 1)(pltpu.make_async_copy(second, target, row_sems.at[index]).start)
+        rows_in.append(pltpu.make_async_copy(first, target, row_sems.at[index]))
+    rows_in.append(pltpu.make_async_copy(state, state_v, row_sems.at[2]))
+    rows_in[2].start()
     at_rest = model + hidden
     jobs = []
     for half in range(2):
@@ -1532,54 +1575,89 @@
             made.start()
         if index + slots < len(jobs):
             load(index + slots, True)
+    mine = [jnp.where(layer == 0, sums[index, :SMALL_ROWS], sums[index, SMALL_ROWS:]) for index in range(3)]
+    gain[0] = mine[2][GAIN0 : GAIN1 + 1]
+    shift[0] = mine[2][SHIFT0 : SHIFT1 + 1]
+    down_bias[...] = mine[2][DOWN_BIAS : DOWN_BIAS + 1]
+    for target, row in ((sgain, SGAIN), (sshift, SSHIFT), (gate, GATE)):
+        target[...] = sums[2, SMALL_ROWS + row : SMALL_ROWS + row + 1]
+    by_core = [jnp.where(layer == 0, mine[0], mine[1]), jnp.where(layer == 0, mine[1], mine[0])]
+    heads, length = rel.shape[1] // 2, buckets.shape[1]
+    hot = back_hot(buckets[...], rel.shape[2])
+    for half in range(2):
+        up_bias[:, half * hidden : (half + 1) * hidden] = by_core[half][UP_BIAS : UP_BIAS + 1, :hidden]
+        for head in range(heads):
+            row = by_core[half][BY_DISTANCE : BY_DISTANCE + 1, head * length : (head + 1) * length]
+            at = half * heads + head
+            row = jnp.broadcast_to(row, (16, length))
+            rel[0, at : at + 1, :] = sum(dot_nt(part, hot) for part in in_parts(row))[:1]
+
+    rows_out = []
+    rows_in[0].wait()
+    rows_out.append(pltpu.make_async_copy(acts_v, acts, row_sems.at[0]))
+    rows_out[0].start()
+    tiles = model // 128
+    for index, source, target in ((1, igs_v, igs_tiles), (2, state_v, state_tiles)):
+        rows_in[index].wait()
+        for tile in range(tiles):
+            target[..., tile, :] = source[..., tile * 128 : (tile + 1) * 128]
+        rows_out.append(pltpu.make_async_copy(target, igs if index == 1 else final, row_sems.at[index]))
+        rows_out[index].start()
     for index in range(len(jobs) - slots, len(jobs)):
         for made in stores(index):
             made.wait()
-
-
-def place_gradients(feed_1, rest_1, full_0, width, hidden):
+    for made in rows_out:
+        made.wait()
+
+
+def place_gradients(feed_1, rest_1, full_0, acts, igs, final, sums, buckets, bucket_count, chip_heads, width, hidden):
     model = full_0.shape[2]
     anywhere = pl.BlockSpec(memory_space=pl.ANY)
-    slots = 4
-    shapes = (
-        (1, 3, model, 2 * width),
-        (1, 2 * width, model),
-        (1, model, 2 * hidden),
-        (1, 2 * hidden, model),
-        (3, model, 2 * width),
-        (2 * width, model),
+    inside = pl.BlockSpec(memory_space=pltpu.VMEM)
+    slots, tiles = 4, model // 128
+    blocks, rows = acts[0].shape[:2]
+    far_shapes = (
+        ((1, 3, model, 2 * width), f32),
+        ((1, 2 * width, model), f32),
+        ((1, model, 2 * hidden), f32),
+        ((1, 2 * hidden, model), f32),
+        ((3, model, 2 * width), f32),
+        ((2 * width, model), f32),
+        ((blocks, rows, model), bf16),
+        ((blocks, rows, tiles, 128), f32),
+        ((rows, tiles, 128), f32),
+    )
+    near_shapes = (
+        (1, 2, model),
+        (1, 2, model),
+        (1, chip_heads, bucket_count),
+        (1, 2 * hidden),
+        (1, model),
+        (1, model),
+        (1, model),
+        (1, model),
     )
     return pl.pallas_call(
         partial(place_kernel, width, hidden),
-        out_shape=[jax.ShapeDtypeStruct(shape, f32) for shape in shapes],
-        in_specs=[anywhere] * 3,
-        out_specs=[anywhere] * 6,
+        out_shape=[jax.ShapeDtypeStruct(*kind) for kind in far_shapes]
+        + [jax.ShapeDtypeStruct(shape, f32) for shape in near_shapes],
+        in_specs=[anywhere] * 8 + [inside] * 2,
+        out_specs=[anywhere] * len(far_shapes) + [inside] * len(near_shapes),
         scratch_shapes=[
             pltpu.VMEM((slots, width, model), bf16),
             pltpu.VMEM((slots, width, model), f32),
+            pltpu.VMEM((blocks, rows, model), bf16),
+            pltpu.VMEM((blocks, rows, model), f32),
+            pltpu.VMEM((rows, model), f32),
+            pltpu.VMEM((blocks, rows, tiles, 128), f32),
+            pltpu.VMEM((rows, tiles, 128), f32),
             pltpu.SemaphoreType.DMA((slots,)),
             pltpu.SemaphoreType.DMA((slots, model // width)),
+            pltpu.SemaphoreType.DMA((3,)),
         ],
         compiler_params=pltpu.CompilerParams(vmem_limit_bytes=VMEM_LIMIT),
         name="place_gradients",
-    )(feed_1, rest_1, full_0)
-
-
-def pack_small(arrays, width):
-    flat = jnp.concatenate([array.astype(f32).reshape(-1) for array in arrays])
-    return jnp.pad(flat, (0, -flat.size % (8 * width))).reshape(-1, width)
-
-
-def unpack_small(packed, shapes):
-    flat = packed.reshape(packed.shape[0], -1)
-    found, at = [], 0
-    for shape in shapes:
-        size = 1
-        for extent in shape:
-            size *= extent
-        found.append(flat[:, at : at + size].reshape((packed.shape[0],) + tuple(shape)))
-        at += size
-    return found
+    )(feed_1, rest_1, full_0, *acts, *igs, final, sums, buckets)
 
 
 def local_part(
@@ -1588,76 +1666,59 @@
 ):
     block_len = valid_mask.shape[1]
     model = tokens.shape[3]
-    core = lax.axis_index("section")
     bucket_count, chip_heads = rel_bias.shape[1:]
-    heads = chip_heads // 2
-    hidden = w_up.shape[2] // 2
+    docs = lax.axis_size("dp")
     valid = valid_mask[:, :, 0].astype(f32)
-    packed = pack_small([norm_gain[0], norm_shift[0], down_bias[0], up_bias[0], rel_bias[0]], model)
     cot_rows = cotangent[:, :, 0, :]
-    *weights, small_all, cot_all = share_weights(
-        block_len, w_qkv[0], w_out[0], w_up[0], w_down[0], w_state_qkv, w_state_out, packed, cot_rows
-    )
-    gains, shifts, down_biases, up_biases, rels = unpack_small(
-        small_all, [(2, model), (2, model), (1, model), (1, 2 * hidden), (bucket_count, chip_heads)]
+    rows = tokens[:, :, 0, :]
+    state = state_init[:, 0, :]
+    smalls = (
+        norm_gain, norm_shift, up_bias[:, None, :], down_bias[:, None, :], jnp.swapaxes(rel_bias, 1, 2)
+    )
+    *weights, cot_all, gains, shifts, up_biases, down_biases, rels = share_weights(
+        block_len, w_qkv[0], w_out[0], w_up[0], w_down[0], w_state_qkv, w_state_out, cot_rows, *smalls
     )
     small = SimpleNamespace(
         gain=gains,
         shift=shifts,
+        up_bias=up_biases,
         down_bias=down_biases,
-        up_bias=lax.dynamic_slice_in_dim(up_biases, core * hidden, hidden, 2),
+        rel=rels,
+        buckets=buckets[None],
         sgain=state_gain[None],
         sshift=state_shift[None],
-        gate=jax.nn.sigmoid(gate_bias)[None],
-    )
-    rels = lax.dynamic_slice_in_dim(rels, core * heads, heads, 2)
-    back = jnp.concatenate([buckets[:1], buckets[:0:-1]])
-    back_hot = back[:, None] == jnp.arange(bucket_count)[None, :]
-    row0 = jnp.sum(jnp.where(back_hot[None, None], jnp.swapaxes(rels, 1, 2)[:, :, None, :], 0.0), axis=-1)
-    rows = tokens[:, :, 0, :]
-    state = state_init[:, 0, :]
-    kept0 = forward_layer(0, block_len, small, row0[0], valid, weights, rows, state)
-    kept1 = forward_layer(1, block_len, small, row0[1], valid, weights, kept0.acts, state)
-    acts = jnp.where(core == 0, kept0.acts, kept1.acts)[None, :, :, None, :]
-    final_state = kept1.final[:, None, :]
-    docs = lax.axis_size("dp")
-    grad1 = backward_layer(
-        1, docs, block_len, small, row0[1], valid, weights, cot_rows, kept0.acts, state, kept1, cot_all
-    )
-    grad0 = backward_layer(
-        0, docs, block_len, small, row0[0], valid, weights, grad1.ig, rows, state, kept0, grad1.dw
-    )
-    input_grads = jnp.where(core == 0, grad0.ig, grad1.ig)[None, :, :, None, :]
-    full, sums = sum_gradients(docs, grad0.dw, jnp.concatenate([grad0.small, grad1.small]))
-    width = heads * (w_qkv.shape[3] // chip_heads)
-    sums = sums.reshape(3, 2, SMALL_ROWS, model)
-    everywhere = sums[2]
-    own = lax.dynamic_index_in_dim(everywhere, core, 0, keepdims=False)
-    by_core = jnp.where(core == 0, sums[:2], sums[1::-1])
-    by_core = lax.dynamic_index_in_dim(by_core, core, 1, keepdims=False)
-    qkv_grad, out_grad, up_grad, down_grad, state_qkv_grad, state_out_grad = place_gradients(
-        grad1.full, grad0.full, full, width, hidden
-    )
-    by_distance = by_core[:, BY_DISTANCE, : heads * block_len].reshape(chip_heads, block_len)
-    by_bucket = jnp.sum(jnp.where(back_hot[:, :, None], by_distance.T[:, None, :], 0.0), axis=0)
+        gate=gate_bias[None],
+    )
+    kept0 = forward_layer(0, block_len, small, valid, weights, rows, state)
+    kept1 = forward_layer(1, block_len, small, valid, weights, kept0.acts, state)
+    grad1 = backward_layer(1, docs, block_len, small, valid, weights, cot_rows, kept0.acts, state, kept1, cot_all)
+    grad0 = backward_layer(0, docs, block_len, small, valid, weights, grad1.ig, rows, state, kept0, grad1.dw)
+    full, sums = sum_gradients(docs, grad0.dw, grad0.small, grad1.small)
+    (
+        qkv_grad, out_grad, up_grad, down_grad, state_qkv_grad, state_out_grad, acts, input_grads, final,
+        gain_grad, shift_grad, rel_grad, up_bias_grad, down_bias_grad, sgain_grad, sshift_grad, gate_grad,
+    ) = place_gradients(
+        grad1.full, grad0.full, full, (kept0.acts, kept1.acts), (grad0.ig, grad1.ig), kept1.final, sums,
+        small.buckets, bucket_count, chip_heads, weights[0].shape[3], weights[2].shape[2],
+    )
     return (
-        acts,
-        input_grads,
-        final_state,
-        own[GAIN0 : GAIN1 + 1][None],
-        own[SHIFT0 : SHIFT1 + 1][None],
+        acts[None, :, :, None, :],
+        input_grads.reshape(1, 2, -1, 1, model),
+        final.reshape(-1, 1, model),
+        gain_grad,
+        shift_grad,
         qkv_grad,
         out_grad,
-        by_bucket[None],
+        jnp.swapaxes(rel_grad, 1, 2),
         up_grad,
-        by_core[:, UP_BIAS, :hidden].reshape(1, 2 * hidden),
+        up_bias_grad,
         down_grad,
-        own[DOWN_BIAS][None],
-        everywhere[1, SGAIN],
-        everywhere[1, SSHIFT],
+        down_bias_grad,
+        sgain_grad[0],
+        sshift_grad[0],
         state_qkv_grad,
         state_out_grad,
-        everywhere[1, GATE],
+        gate_grad[0],
     )
 
 

time: 560 us -> 545 us (0.973); the launches traced: 557 us -> 536 us
  local copies, waits for them, and re-layouts: 20.7 us -> 0 us
  other arithmetic: 7.88 us -> 1.28 us
  Pallas kernels: 527 us -> 533 us
    unnamed x20 -> x0, local copies, waits for them, and re-layouts: 10.2 us -> none
    slice x12 -> x0, local copies, waits for them, and re-layouts: 6.46 us -> none  [the longest x2 1.95 us: local_part(): back = jnp.concatenate([buckets[:1], buckets[:0:-1]])]
where the time goes in v4:
time: 545 us; the launch traced here: 536 us
  Pallas kernels  533 us (98%)
    pallas_call x2, Pallas kernels, backward_layer(): pl.pallas_call(partial(backward_kernel, layer, n, ring_names, [*ins, *far...  200 us
    pallas_call x2, Pallas kernels, forward_layer(): pl.pallas_call(partial(forward_kernel, layer, [*ins, *far_ins, *outs, *sc...  154 us
    pallas_call x1, Pallas kernels, sum_gradients(): pl.pallas_call(partial(sum_kernel, n), out_shape=(jax.ShapeDtypeStruct((2...  138 us
    pallas_call x1, Pallas kernels, place_gradients(): pl.pallas_call(partial(place_kernel, width, hidden), out_shape=[jax.Shape...  23.2 us
    pallas_call x1, Pallas kernels, share_weights(): pl.pallas_call(partial(share_kernel, block_len), out_shape=(halved(qkv.sh...  17.9 us

profile of v4, /device:TPU:0, one launch (start us, length us, event | category | flops | bytes accessed | tf_op | source)
XLA Modules:
  0.0 535.6 jit_solution(15615502573576804620)
XLA Ops:
  0.7 1.3 fusion.refs_7_.refs_5_
  1.9 17.9 %share_weights.1 = (bf16[2,3,1024,256]{3,2,1,0:T(8,128)(2,1)}, bf16[2,256,1024]{2,1,0:T(8,128)(2,1)}, bf16[2,1024,1024]{2,1,0:T(8,128)(2,1)}, bf16[2,1024,1024]{...) custom-call(bf16[3,1024,512]{2,1,0:T(8,128)(2,1)} %bitcast.43, ...), custom_call_target="tpu_custom_call" | custom-call | tf_op jit(solution)/shard_map/share_weights/pallas_call | solution.py:220
  19.8 63.5 %forward_local.1 = (bf16[2,512,1024]{2,1,0:T(8,128)(2,1)}, bf16[2,512,768]{2,1,0:T(8,128)(2,1)}, f32[2,512,128]{2,1,0:T(8,128)}, bf16[2,512,256]{2,1,0:T(8,128)(...) custom-call(bf16[2,256,1024]{2,1,0:T(8,128)(2,1)} %bitcast.39, ...), custom_call_target="tpu_custom_call" | custom-call | tf_op jit(solution)/shard_map/forward_local/pallas_call | solution.py:628
  83.3 91.0 %forward_recurrent.1 = (bf16[2,512,1024]{2,1,0:T(8,128)(2,1)}, bf16[2,512,768]{2,1,0:T(8,128)(2,1)}, f32[2,512,128]{2,1,0:T(8,128)}, bf16[2,512,256]{2,1,0:T(8,1...) custom-call(bf16[2,256,1024]{2,1,0:T(8,128)(2,1)} %get-tuple-element, ...), custom_call_target="tpu_custom_call" | custom-call | tf_op jit(solution)/shard_map/forward_recurrent/pallas_call | solution.py:628
  174.3 108.6 %backward_recurrent.1 = (bf16[2,2048,1024]{2,1,0:T(8,128)(2,1)}, bf16[2048,1024]{1,0:T(8,128)(2,1)}, f32[16,1024]{1,0:T(8,128)}, f32[2,256,1024]{2,1,0:T(8,128)}) custom-call(bf16[2,256,1024]{2,1,0:T(8,128)(2,1)} %bitcast.38, bf16[2,256,1024]{2,1,0:T(8,128)(2,1)} %get-tuple-element.90.refs_0_.refs_1_.acts_0, ...), custom_call_target="tpu_custom_call" | custom-call | tf_op jit(solution)/shard_map/backward_recurrent/pallas_call | solution.py:1489
  282.9 91.1 %backward_local.1 = (bf16[2,2048,1024]{2,1,0:T(8,128)(2,1)}, bf16[3072,1024]{1,0:T(8,128)(2,1)}, f32[16,1024]{1,0:T(8,128)}, f32[2,256,1024]{2,1,0:T(8,128)}) custom-call(f32[2,256,1024]{2,1,0:T(8,128)} %get-tuple-element.109.refs_0_.igs_1, bf16[2,256,1024]{2,1,0:T(8,128)(2,1)} %bitcast.40, f32[2,2,1024]{2,1,0:T(2,128)} %get-tuple-element.81.refs_1_.refs_2_, ...), custom_call_target="tpu_custom_call" | custom-call | tf_op jit(solution)/shard_map/backward_local/pallas_call | solution.py:1489
  374.0 137.9 %sum_gradients.1 = (bf16[2,3072,1024]{2,1,0:T(8,128)(2,1)}, f32[3,32,1024]{2,1,0:T(8,128)}) custom-call(bf16[3072,1024]{1,0:T(8,128)(2,1)} %get-tuple-element.120.parts, f32[16,1024]{1,0:T(8,128)} %get-tuple-element.121.small_0, f32[16,1024]{1,0:T(8,128)} %get-tuple-element.122.small_1), custom_call_target="tpu_custom_call" | custom-call | tf_op jit(solution)/shard_map/sum_gradients/pallas_call | solution.py:919
  511.9 23.2 %place_gradients.1 = (f32[1,3,1024,512]{3,2,1,0:T(8,128)}, f32[1,512,1024]{2,1,0:T(8,128)}, f32[1,1024,2048]{2,1,0:T(8,128)}, f32[1,2048,1024]{2,1,0:T(8,128)}, ...) custom-call(bf16[2,2048,1024]{2,1,0:T(8,128)(2,1)} %get-tuple-elemen, ...), custom_call_target="tpu_custom_call" | custom-call | tf_op jit(solution)/shard_map/place_gradients/pallas_call | solution.py:1640

commit v5 on v4

--- a/solution.py
+++ b/solution.py
@@ -12,7 +12,7 @@
 f32, bf16 = jnp.float32, jnp.bfloat16
 eps = 1e-05
 negative = -1000000000.0
-VMEM_LIMIT = 60 * 1024 * 1024
+VMEM_LIMIT = 62 * 1024 * 1024
 
 
 def dot(left, right):
@@ -164,91 +164,6 @@
         self.net.sent(self.first, self.second, self.across)
 
 
-def share_kernel(block_len, qkv, out, up, down, sqkv, sout, cot, *rest):
-    smalls, targets, cot_all, small_all = rest[:5], rest[5:11], rest[11], rest[12:17]
-    staged, cot_staged, small_staged = rest[17:23], rest[23], rest[24:29]
-    local_sems, send_sems, recv_sems = rest[29:]
-    place = Place(block_len)
-    net, local = Net(send_sems, recv_sems), Local(local_sems)
-    layer = place.c
-
-    def half(array, axis, c):
-        width = array.shape[axis] // 2
-        index = [slice(None)] * len(array.shape)
-        index[axis] = pl.ds(pl.multiple_of(c * width, width), width)
-        return array.at[tuple(index)]
-
-    shared = ((qkv, 2), (out, 0), (up, 1), (down, 0))
-    kept = [small.at[0] for small in smalls]
-    kept += [half(array, axis, place.c) for array, axis in shared + ((sqkv, 2), (sout, 0))]
-    sent = [small.at[0] for small in smalls] + [half(array, axis, 1 - place.c) for array, axis in shared]
-    finals = [target.at[layer] for target in (*small_all, *targets[:4])] + [targets[4], targets[5]]
-    place.meet()
-    across, near = [], []
-    for block in range(2):
-        own, target = cot.at[block, place.core_rows()], cot_all.at[block, place.rows()]
-        across.append(net.copy(own, target, place.chip))
-        near.append(net.copy(own, target, place.core))
-    for source, target in zip(sent, finals):
-        near.append(net.copy(source, target, place.core))
-    cot_in = [local.copy(cot.at[block, place.core_rows()], cot_staged.at[block]) for block in range(2)]
-    inward = [local.copy(source, stage) for source, stage in zip(kept, (*small_staged, *staged))]
-    for block in range(2):
-        local.wait(cot_in[block])
-        local.copy(cot_staged.at[block], cot_all.at[block, place.rows()])
-    for index, stage, target in zip(inward, (*small_staged, *staged), finals):
-        local.wait(index)
-        local.copy(stage, target)
-    for block in range(2):
-        across[block].wait_recv()
-        passed = cot_all.at[block, place.rows(x_other=True)]
-        near.append(net.copy(passed, passed, place.core))
-    for made in near:
-        made.wait_recv()
-    local.drain()
-    net.drain()
-
-
-def share_weights(block_len, qkv, out, up, down, sqkv, sout, cot, *smalls):
-    def halved(shape, axis, stacked=True):
-        shape = list(shape)
-        shape[axis] //= 2
-        return jax.ShapeDtypeStruct(([2] if stacked else []) + shape, bf16)
-
-    anywhere = pl.BlockSpec(memory_space=pl.ANY)
-    count = 7 + len(smalls)
-    return pl.pallas_call(
-        partial(share_kernel, block_len),
-        out_shape=(
-            halved(qkv.shape, 2),
-            halved(out.shape, 0),
-            halved(up.shape, 1),
-            halved(down.shape, 0),
-            halved(sqkv.shape, 2, False),
-            halved(sout.shape, 0, False),
-            jax.ShapeDtypeStruct((2, block_len, cot.shape[2]), bf16),
-            *(jax.ShapeDtypeStruct((2,) + small.shape[1:], f32) for small in smalls),
-        ),
-        in_specs=[anywhere] * count,
-        out_specs=[anywhere] * count,
-        scratch_shapes=[
-            pltpu.VMEM(halved(array.shape, axis, False).shape, bf16)
-            for array, axis in ((qkv, 2), (out, 0), (up, 1), (down, 0), (sqkv, 2), (sout, 0))
-        ]
-        + [pltpu.VMEM((2, block_len // 4, cot.shape[2]), bf16)]
-        + [pltpu.VMEM(small.shape[1:], f32) for small in smalls]
-        + [
-            pltpu.SemaphoreType.DMA((2 * count + 2,)),
-            pltpu.SemaphoreType.DMA((count + 4,)),
-            pltpu.SemaphoreType.DMA((count + 4,)),
-        ],
-        compiler_params=pltpu.CompilerParams(
-            collective_id=0, has_side_effects=True, vmem_limit_bytes=VMEM_LIMIT
-        ),
-        name="share_weights",
-    )(qkv, out, up, down, sqkv, sout, cot, *smalls)
-
-
 def back_hot(buckets, count):
     length = buckets.shape[1]
     hot = lax.broadcasted_iota(jnp.int32, (count, length), 0) == buckets
@@ -312,11 +227,45 @@
     chunk = min(128, length)
 
     place.meet()
-    load = [local.copy(r.wqkv.at[layer], r.wqkv_v), local.copy(r.wout.at[layer], r.wout_v)]
-    load_mlp = [local.copy(r.wup.at[layer], r.wup_v), local.copy(r.wdown.at[layer], r.wdown_v)]
-    load_state = []
-    if rec:
+    if rec:
+        load = [local.copy(r.wqkv.at[layer], r.wqkv_v), local.copy(r.wout.at[layer], r.wout_v)]
+        load_mlp = [local.copy(r.wup.at[layer], r.wup_v), local.copy(r.wdown.at[layer], r.wdown_v)]
         load_state = [local.copy(r.wsqkv, r.wsqkv_v), local.copy(r.wsout, r.wsout_v)]
+    else:
+        def share(source, target, axis=None):
+            def half(c):
+                if axis is None:
+                    return source.at[0]
+                size = source.shape[axis] // 2
+                index = [slice(None)] * len(source.shape)
+                index[axis] = pl.ds(pl.multiple_of(c * size, size), size)
+                return source.at[tuple(index)]
+
+            target = target.at[place.c]
+            return net.copy(half(1 - place.c), target, place.core), local.copy(half(place.c), target)
+
+        def shared(*pairs):
+            for far, near in pairs:
+                far.wait_recv()
+                local.wait(near)
+
+        smalls = [
+            share(r.gain_own, r.gain),
+            share(r.shift_own, r.shift),
+            share(r.up_bias_own, r.up_bias),
+            share(r.down_bias_own, r.down_bias),
+            share(r.rel_own, r.rel),
+        ]
+        first_weights = [share(r.qkv_own, r.wqkv_s, 2), share(r.out_own, r.wout_s, 0)]
+        later_weights = [share(r.up_own, r.wup_s, 1), share(r.down_own, r.wdown_s, 0)]
+        state_weights = []
+        for source, target, axis in ((r.sqkv_own, r.wsqkv_s, 2), (r.sout_own, r.wsout_s, 0)):
+            size = source.shape[axis] // 2
+            at = pl.ds(pl.multiple_of(place.c * size, size), size)
+            part = source.at[:, :, at] if axis == 2 else source.at[at]
+            state_weights.append(local.copy(part, target))
+        r.wqkv_v, r.wout_v = r.wqkv_s.at[layer], r.wout_s.at[layer]
+        r.wup_v, r.wdown_v = r.wup_s.at[layer], r.wdown_s.at[layer]
 
     gain = lambda index: r.gain[layer, index : index + 1, :]
     shift = lambda index: r.shift[layer, index : index + 1, :]
@@ -357,52 +306,78 @@
 
             to.send(x_other)
 
-    def attend(block):
+    def head_columns(head):
+        return [slice(part * width + head * head_size, part * width + (head + 1) * head_size) for part in range(3)]
+
+    def pack(columns):
+        lane = lax.broadcasted_iota(jnp.int32, (chunk, 128), 1)
+        packed = jnp.zeros((chunk, 128), f32)
+        for index, column in enumerate(columns):
+            packed = jnp.where(lane == index, column, packed)
+        return packed
+
+    def attend_window(index, head, block):
         qkv = r.qkv_v.at[block]
         prev = r.qkv_v.at[block - 1] if block > 0 else None
-
+        at = pl.ds(pl.multiple_of(index * chunk, chunk), chunk)
+        q_at, k_at, v_at = head_columns(head)
+        logits, here = window_logits(
+            qkv[at, q_at],
+            qkv[:, k_at],
+            None if prev is None else prev[:, k_at],
+            r.bias[head, :, bias_columns(index, chunk, length)],
+            r.valid,
+            block,
+            index * chunk,
+            scale,
+        )
+        peak = jnp.max(logits, axis=-1, keepdims=True)
+        probs = jnp.exp(logits - peak)
+        total = jnp.sum(probs, axis=-1, keepdims=True)
+        if prev is None:
+            result = dot(probs.astype(bf16), qkv[:, v_at])
+        else:
+            result = dot(jnp.where(here, probs, 0.0).astype(bf16), qkv[:, v_at])
+            result += dot(jnp.where(here, 0.0, probs).astype(bf16), prev[:, v_at])
+        return peak, total, result
+
+    def attend_state(index, head, block, window):
+        peak_window, total_window, result_window = window
+        at = pl.ds(pl.multiple_of(index * chunk, chunk), chunk)
+        q_at, k_at, v_at = head_columns(head)
+        state = r.sqkv_v.at[block]
+        logits = dot_nt(r.qkv_v[block, at, q_at], state[:, k_at]) * scale
+        peak = jnp.maximum(peak_window, jnp.max(logits, axis=-1, keepdims=True))
+        less = jnp.exp(peak_window - peak)
+        probs = jnp.exp(logits - peak)
+        total = total_window * less + jnp.sum(probs, axis=-1, keepdims=True)
+        return peak, total, result_window * less + dot(probs.astype(bf16), state[:, v_at])
+
+    def attend(block, window=True, state=rec):
         @pl.loop(0, length // chunk)
         def _(index):
             at = pl.ds(pl.multiple_of(index * chunk, chunk), chunk)
-            lses = []
+            kept = []
             for head in range(heads):
-                q_at = slice(head * head_size, (head + 1) * head_size)
-                k_at = slice(width + head * head_size, width + (head + 1) * head_size)
-                v_at = slice(2 * width + head * head_size, 2 * width + (head + 1) * head_size)
-                query = qkv[at, q_at]
-                logits, here = window_logits(
-                    query,
-                    qkv[:, k_at],
-                    None if prev is None else prev[:, k_at],
-                    r.bias[head, :, bias_columns(index, chunk, length)],
-                    r.valid,
-                    block,
-                    index * chunk,
-                    scale,
-                )
-                peak = jnp.max(logits, axis=-1, keepdims=True)
-                if rec:
-                    state = r.sqkv_v.at[block]
-                    state_logits = dot_nt(query, state[:, k_at]) * scale
-                    peak = jnp.maximum(peak, jnp.max(state_logits, axis=-1, keepdims=True))
-                probs = jnp.exp(logits - peak)
-                total = jnp.sum(probs, axis=-1, keepdims=True)
-                if prev is None:
-                    result = dot(probs.astype(bf16), qkv[:, v_at])
+                q_at = head_columns(head)[0]
+                if window:
+                    found = attend_window(index, head, block)
                 else:
-                    result = dot(jnp.where(here, probs, 0.0).astype(bf16), qkv[:, v_at])
-                    result += dot(jnp.where(here, 0.0, probs).astype(bf16), prev[:, v_at])
-                if rec:
-                    state_probs = jnp.exp(state_logits - peak)
-                    total += jnp.sum(state_probs, axis=-1, keepdims=True)
-                    result += dot(state_probs.astype(bf16), state[:, v_at])
-                r.att_v[block, at, q_at] = (result / total).astype(bf16)
-                lses.append(peak + jnp.log(total))
-            lane = lax.broadcasted_iota(jnp.int32, (chunk, 128), 1)
-            packed = jnp.zeros((chunk, 128), f32)
-            for head in range(heads):
-                packed = jnp.where(lane == head, lses[head], packed)
-            r.lse_v[block, at, :] = packed
+                    found = (
+                        r.lse_v[block, at, 2 * head : 2 * head + 1],
+                        r.lse_v[block, at, 2 * head + 1 : 2 * head + 2],
+                        r.early[at, q_at],
+                    )
+                if state:
+                    found = attend_state(index, head, block, found)
+                if state or not rec:
+                    peak, total, result = found
+                    r.att_v[block, at, q_at] = (result / total).astype(bf16)
+                    kept.append(peak + jnp.log(total))
+                else:
+                    r.early[at, q_at] = found[2]
+                    kept.extend(found[:2])
+            r.lse_v[block, at, :] = pack(kept)
 
     def recur(block):
         qkv, state = r.qkv_v.at[block], r.sqkv_v.at[block]
@@ -423,11 +398,7 @@
                 r.sout_v[block, at, q_at] = (dot(probs.astype(bf16), qkv[:, v_at]) / total).astype(bf16)
                 lses.append(peak + jnp.log(total))
             if block == 0:
-                lane = lax.broadcasted_iota(jnp.int32, (chunk, 128), 1)
-                packed = jnp.zeros((chunk, 128), f32)
-                for head in range(heads):
-                    packed = jnp.where(lane == head, lses[head], packed)
-                r.rlse_v[at, :] = packed
+                r.rlse_v[at, :] = pack(lses)
 
     def take_branch(block, from_out):
         rows = r.x[block, place.core_rows(), :].astype(f32) + from_out.finish()
@@ -452,16 +423,25 @@
         own[...] = rows.astype(bf16)
         return net.copy(own, own, place.core)
 
+    def cotangent(block):
+        own = r.cot_v.at[block, place.rows()]
+        local.wait(local.copy(r.cot.at[block, place.core_rows()], own))
+        cot[block].start()
+
     branch = [scatter(), scatter()]
     result = [scatter(), scatter()]
     first = [gather(r.u_v.at[block]) for block in range(2)]
     second = [gather(r.wn_v.at[block]) for block in range(2)]
     if rec:
-        update = [scatter(), scatter()]
+        update = [scatter()]
         state = [gather(r.sn_v.at[block]) for block in range(2)]
         gate = jax.nn.sigmoid(r.gate[...])
         norm_state(r.state[place.core_rows(), :].astype(f32), 0)
         state[0].start()
+    else:
+        cot = [gather(r.cot_v.at[block]) for block in range(2)]
+        cotangent(1)
+        shared(*smalls)
     norm_first(0)
     first[0].start()
     norm_first(1)
@@ -469,13 +449,18 @@
     fill_bias(r.bias, bias_rows(r.rel[layer], r.buckets[...], place.c))
     if rec:
         state[0].forward()
+    if not rec:
+        cot[1].forward()
     first[0].forward()
     if rec:
         state[0].finish()
         local.wait(*load_state)
         project(r.sn_v.at[0], r.wsqkv_v, r.sqkv_v.at[0])
     first[0].finish()
-    local.wait(*load)
+    if rec:
+        local.wait(*load)
+    else:
+        shared(*first_weights)
     project(r.u_v.at[0], r.wqkv_v, r.qkv_v.at[0])
     if rec:
         recur(0)
@@ -503,6 +488,7 @@
         state[1].start()
         local.copy(r.z_v, r.z)
         local.copy(r.s1_v, r.s1)
+        attend(1, state=False)
     else:
         attend(1)
         reduce_from(r.att_v.at[1], r.wout_v, branch[1])
@@ -514,25 +500,42 @@
         project(r.sn_v.at[1], r.wsqkv_v, r.sqkv_v.at[1])
         local.copy(r.sn_v, r.sn)
         local.copy(r.sqkv_v, r.sqkv)
-        recur(1)
-        reduce_from(r.sout_v.at[1], r.wsout_v, update[1])
-        local.copy(r.sout_v, r.sout)
-        local.copy(r.rlse_v, r.rlse)
-        attend(1)
-        update[1].middle()
+        attend(1, window=False)
         reduce_from(r.att_v.at[1], r.wout_v, branch[1])
     local.copy(r.att_v, r.att)
     local.copy(r.lse_v, r.lse)
     second[0].forward()
     branch[1].middle()
     second[0].finish()
-    local.wait(*load_mlp)
+    if rec:
+        local.wait(*load_mlp)
+    else:
+        shared(*later_weights)
+        local.wait(*state_weights)
+        for source, target in (
+            (r.wqkv_s, r.wqkv),
+            (r.wout_s, r.wout),
+            (r.wup_s, r.wup),
+            (r.wdown_s, r.wdown),
+            (r.wsqkv_s, r.wsqkv),
+            (r.wsout_s, r.wsout),
+            (r.gain, r.gain_both),
+            (r.shift, r.shift_both),
+            (r.up_bias, r.up_bias_both),
+            (r.down_bias, r.down_bias_both),
+            (r.rel, r.rel_both),
+        ):
+            local.copy(source, target)
     feed_up(0)
     reduce_from(r.act_v.at[0], r.wdown_v, result[0])
     take_branch(1, branch[1])
     second[1].start()
     local.copy(r.h_v, r.h)
     result[0].middle()
+    if rec:
+        recur(1)
+        local.copy(r.sout_v, r.sout)
+        local.copy(r.rlse_v, r.rlse)
     second[1].forward()
     second[1].finish()
     local.copy(r.wn_v, r.wn)
@@ -542,25 +545,26 @@
     reduce_from(r.act_v.at[1], r.wdown_v, result[1])
     sent = [take_result(0, result[0])]
     result[1].middle()
-    if rec:
-        own = r.final_v.at[place.core_rows()]
-        own[...] = gate * r.s1_v[...] + (1.0 - gate) * update[1].finish()
-        sent.append(net.copy(own, own, place.core))
+    if not rec:
+        cotangent(0)
     sent.append(take_result(1, result[1]))
     for made in sent:
         made.wait_recv()
     local.copy(r.acts_v, r.acts)
-    if rec:
-        local.copy(r.final_v, r.final)
+    if not rec:
+        cot[0].forward()
+        cot[1].finish()
+        cot[0].finish()
+        local.copy(r.cot_v, r.cot_all)
     local.drain()
     net.drain()
 
 
-def forward_layer(layer, block_len, small, valid, weights, rows, state):
+def forward_layer(layer, block_len, small, valid, weights, rows, state, cot=None):
     rec = layer == 1
     wqkv, wout, wup, wdown = weights[:4]
     model = rows.shape[2]
-    width, hidden = wqkv.shape[3], wup.shape[2]
+    width, hidden = (wqkv.shape[3], wup.shape[2]) if rec else (wqkv.shape[2] // 2, wup.shape[1] // 2)
     quarter = block_len // 4
     heads = small.rel.shape[1] // 2
 
@@ -578,17 +582,18 @@
         h=held((2, quarter, model), f32),
         acts=held((2, 2 * quarter, model), bf16),
     )
-    ins = dict(
-        x=rows,
-        gain=small.gain,
-        shift=small.shift,
-        up_bias=small.up_bias,
-        down_bias=small.down_bias,
-        rel=small.rel,
-        buckets=small.buckets,
-        valid=valid,
+    ins = dict(x=rows, buckets=small.buckets, valid=valid)
+    names = ("gain", "shift", "up_bias", "down_bias", "rel")
+    smalls = {name: getattr(small, name) for name in names}
+    shapes = dict(
+        wqkv=(3, model, width),
+        wout=(width, model),
+        wup=(model, hidden),
+        wdown=(hidden, model),
+        wsqkv=(3, model, width),
+        wsout=(width, model),
     )
-    far_ins = dict(wqkv=wqkv, wout=wout, wup=wup, wdown=wdown)
+    scratch, given = {}, {}
     if rec:
         outs.update(
             sn=held((2, block_len, model), bf16),
@@ -597,18 +602,30 @@
             sout=held((2, block_len, width), bf16),
             s1=held((quarter, model), f32),
             z=held((quarter, model), f32),
-            final=held((2 * quarter, model), f32),
         )
-        ins.update(state=state, sgain=small.sgain, sshift=small.sshift, gate=small.gate)
-        far_ins.update(wsqkv=weights[4], wsout=weights[5])
-    scatters = 6 if rec else 4
-    copies = (3 * 6 + 3 * 6 + 3) if rec else (3 * 4 + 3 * 4 + 2)
-    scratch = {name + "_v": pltpu.VMEM(kind.shape, kind.dtype) for name, kind in outs.items()}
+        ins.update(state=state, sgain=small.sgain, sshift=small.sshift, gate=small.gate, **smalls)
+        far_ins = dict(wqkv=wqkv, wout=wout, wup=wup, wdown=wdown, wsqkv=weights[4], wsout=weights[5])
+        scratch.update({name + "_v": pltpu.VMEM(shape, bf16) for name, shape in shapes.items()})
+        scratch.update(early=pltpu.VMEM((block_len, width), f32))
+    else:
+        far_ins = dict(
+            qkv_own=wqkv, out_own=wout, up_own=wup, down_own=wdown, sqkv_own=weights[4], sout_own=weights[5]
+        )
+        far_ins.update({name + "_own": array for name, array in smalls.items()}, cot=cot)
+        given = dict(cot_all=held((2, block_len, model), bf16))
+        scratch.update(cot_v=pltpu.VMEM((2, block_len, model), bf16))
+        for name, shape in shapes.items():
+            shape = shape if name.startswith("ws") else (2, *shape)
+            given[name] = held(shape, bf16)
+            scratch[name + "_s"] = pltpu.VMEM(shape, bf16)
+        for name, array in smalls.items():
+            given[name + "_both"] = held((2, *array.shape[1:]), f32)
+            scratch[name] = pltpu.VMEM((2, *array.shape[1:]), f32)
+    scatters = 5 if rec else 4
+    copies = (3 * 6 + 3 * 5 + 2) if rec else (3 * 6 + 3 * 4 + 2 + 9)
+    scratch.update({name + "_v": pltpu.VMEM(kind.shape, kind.dtype) for name, kind in outs.items()})
+    outs.update(given)
     scratch.update(
-        wqkv_v=pltpu.VMEM(wqkv.shape[1:], bf16),
-        wout_v=pltpu.VMEM(wout.shape[1:], bf16),
-        wup_v=pltpu.VMEM(wup.shape[1:], bf16),
-        wdown_v=pltpu.VMEM(wdown.shape[1:], bf16),
         bias=pltpu.VMEM((heads, min(128, block_len), 2 * block_len), f32),
         part=pltpu.VMEM((scatters, block_len, model), bf16),
         near=pltpu.VMEM((scatters, 2, quarter, model), bf16),
@@ -616,13 +633,8 @@
         far=pltpu.VMEM((scatters, quarter, model), bf16),
         send_sems=pltpu.SemaphoreType.DMA((copies,)),
         recv_sems=pltpu.SemaphoreType.DMA((copies,)),
-        local_sems=pltpu.SemaphoreType.DMA((6 + len(outs),)),
+        local_sems=pltpu.SemaphoreType.DMA((len(far_ins) + len(outs) + 1,)),
     )
-    if rec:
-        scratch.update(
-            wsqkv_v=pltpu.VMEM(weights[4].shape, bf16),
-            wsout_v=pltpu.VMEM(weights[5].shape, bf16),
-        )
     anywhere = pl.BlockSpec(memory_space=pl.ANY)
     inside = pl.BlockSpec(memory_space=pltpu.VMEM)
     results = pl.pallas_call(
@@ -1017,7 +1029,10 @@
             local.copy(r.sout, r.sout_v),
             local.copy(r.rlse, r.rlse_v),
         ]
-    wqkv = local.copy(r.wqkv.at[layer], r.wqkv_v)
+    wqkv = [local.copy(r.wqkv.at[layer], r.wqkv_v)]
+    wqkv += [local.copy(r.x.at[block, place.core_rows()], r.x_v.at[block]) for block in range(2)]
+    if rec:
+        chain.append(local.copy(r.state.at[place.core_rows()], r.state_v))
 
     gain = lambda index: r.gain[layer, index : index + 1, :]
     small = r.small_v
@@ -1044,6 +1059,8 @@
         return slice(block * length, (block + 1) * length)
 
     def own_grad(block):
+        if rec:
+            return r.g[pl.ds(place_row(block), place.quarter), :].astype(f32)
         return r.gy[block, place.core_rows(), :].astype(bf16).astype(f32)
 
     def feed_back(block):
@@ -1076,6 +1093,18 @@
 
             to.send(x_other)
 
+    def update_last():
+        step = min(512, model)
+        for x_other in (True, False):
+            rows = place.chip_rows(x_other)
+
+            @pl.loop(0, model // step)
+            def _(index):
+                at = pl.ds(pl.multiple_of(index * step, step), step)
+                last_update.part[rows, at] = dot(r.sout_v[1, rows, :], r.wsout_v[:, at]).astype(bf16)
+
+            last_update.send(x_other)
+
     def take_feed(block, from_feed):
         by_norm = from_feed.finish()
         grad = own_grad(block)
@@ -1084,7 +1113,7 @@
         add_small(SHIFT1, by_shift)
         add_small(DOWN_BIAS, jnp.sum(grad, axis=0, keepdims=True))
         total = grad + by_rows
-        r.ig_v[block, place.core_rows(), :] = total
+        r.ig_v[block] = total
         r.hg[pl.ds(place_row(block), place.quarter), :] = total.astype(bf16)
 
     def place_row(block):
@@ -1100,14 +1129,14 @@
             target[to, :] = dot_tn(left[:, at], right[...]).astype(bf16)
 
     def projection_grad(normed, grads, target):
-        for part in range(3):
-            tick()
-            to = slice(part * width, (part + 1) * width)
-
-            @pl.loop(0, model // width)
-            def _(index):
-                at = pl.ds(pl.multiple_of(index * width, width), width)
-                target[to, at] = dot_tn(normed[:, at], grads[:, to]).astype(bf16)
+        @pl.loop(0, model // width)
+        def _(index):
+            tick_at(index, 0, 1, 2)
+            at = pl.ds(pl.multiple_of(index * width, width), width)
+            found = dot_tn(normed[:, at], grads[...]).astype(bf16)
+            for part in range(3):
+                to = slice(part * width, (part + 1) * width)
+                target[to, at] = found[:, to]
 
     def branch_back(block):
         r.datt[block] = dot_nt(r.hg[block_rows(block), :], r.wout_v[...]).astype(bf16)
@@ -1115,19 +1144,41 @@
     def columns(head, part):
         return slice(part * width + head * head_size, part * width + (head + 1) * head_size)
 
-    def attend_back(block):
+    def attend_back(block, window=True, state=rec):
         qkv = r.qkv_v.at[block]
         prev = r.qkv_v.at[block - 1] if block > 0 else None
-        state = r.sqkv_v.at[block] if rec else None
 
         @pl.loop(0, length // chunk)
         def _(index):
-            tick_at(index, *((1, 2, 3) if rec and block else (1, 3)))
+            if window:
+                tick_at(index, 1, 3)
             at = pl.ds(pl.multiple_of(index * chunk, chunk), chunk)
             block_at = pl.ds(pl.multiple_of(block * length + index * chunk, chunk), chunk)
             for head in range(heads):
                 q_at, k_at, v_at = (columns(head, part) for part in range(3))
-                query, key, value = qkv[at, q_at], qkv[:, k_at], qkv[:, v_at]
+                early_at = pl.ds(pl.multiple_of(index * width + head * head_size, head_size), head_size)
+                query = qkv[at, q_at]
+                lse = r.lse_v[block, at, head : head + 1]
+                grad = r.datt[block, at, q_at]
+                delta = jnp.sum(
+                    grad.astype(f32) * r.att_v[block_at, q_at].astype(f32), axis=-1, keepdims=True
+                )
+                by_query = None
+                if state:
+                    skv = r.sqkv_v.at[block]
+                    state_probs = jnp.exp(dot_nt(query, skv[:, k_at]) * scale - lse)
+                    by_state = state_probs * (dot_nt(grad, skv[:, v_at]) - delta) * scale
+                    low_state = by_state.astype(bf16)
+                    by_query = dot(low_state, skv[:, k_at])
+                    r.dskv[:, q_at] += dot_tn(low_state, query)
+                    r.dskv[:, k_at] += dot_tn(state_probs.astype(bf16), grad)
+                    if not window:
+                        r.h_v[0, :, early_at] = by_query
+                elif rec:
+                    by_query = r.h_v[0, :, early_at]
+                if not window:
+                    continue
+                key, value = qkv[:, k_at], qkv[:, v_at]
                 logits, here = window_logits(
                     query,
                     key,
@@ -1138,12 +1189,7 @@
                     index * chunk,
                     scale,
                 )
-                lse = r.lse_v[block, at, head : head + 1]
                 probs = jnp.exp(logits - lse)
-                grad = r.datt[block, at, q_at]
-                delta = jnp.sum(
-                    grad.astype(f32) * r.att_v[block_at, q_at].astype(f32), axis=-1, keepdims=True
-                )
                 by_probs = dot_nt(grad, value)
                 if prev is not None:
                     by_probs = jnp.where(here, by_probs, dot_nt(grad, prev[:, v_at]))
@@ -1153,24 +1199,18 @@
                 if prev is None:
                     low = by_logits.astype(bf16)
                     low_probs = probs.astype(bf16)
-                    by_query = dot(low, key)
+                    by_window = dot(low, key)
                 else:
                     low = jnp.where(here, by_logits, 0.0).astype(bf16)
                     low_probs = jnp.where(here, probs, 0.0).astype(bf16)
                     low_prev = jnp.where(here, 0.0, by_logits).astype(bf16)
                     low_probs_prev = jnp.where(here, 0.0, probs).astype(bf16)
-                    by_query = dot(low, key) + dot(low_prev, prev[:, k_at])
+                    by_window = dot(low, key) + dot(low_prev, prev[:, k_at])
                     r.dkv[block - 1, :, q_at] += dot_tn(low_prev, query)
                     r.dkv[block - 1, :, k_at] += dot_tn(low_probs_prev, grad)
                 r.dkv[block, :, q_at] += dot_tn(low, query)
                 r.dkv[block, :, k_at] += dot_tn(low_probs, grad)
-                if rec:
-                    state_probs = jnp.exp(dot_nt(query, state[:, k_at]) * scale - lse)
-                    by_state = state_probs * (dot_nt(grad, state[:, v_at]) - delta) * scale
-                    low_state = by_state.astype(bf16)
-                    by_query += dot(low_state, state[:, k_at])
-                    r.dskv[:, q_at] += dot_tn(low_state, query)
-                    r.dskv[:, k_at] += dot_tn(state_probs.astype(bf16), grad)
+                by_query = by_window if by_query is None else by_query + by_window
                 r.dqkv[block_at, q_at] = by_query.astype(bf16)
 
     def recur_back():
@@ -1223,15 +1263,18 @@
             to,
         )
 
+    def give(rows, target):
+        local.copy(rows, target)
+        return net.copy(rows, target, place.core)
+
     def take_input(block, from_input):
         by_norm = from_input.finish()
-        rows = r.x[block, place.core_rows(), :].astype(f32)
+        rows = r.x_v[block].astype(f32)
         by_rows, by_gain, by_shift = norm_back(rows, gain(0), by_norm)
         add_small(GAIN0, by_gain)
         add_small(SHIFT0, by_shift)
-        own = r.ig_v.at[block, place.core_rows()]
-        own[...] += by_rows
-        return net.copy(own, own, place.core)
+        r.ig_v[block] += by_rows
+        return give(r.ig_v.at[block], r.ig.at[block, place.core_rows()])
 
     def take_state(rows, from_state):
         by_rows, by_gain, by_shift = norm_back(rows, r.sgain[...], from_state.finish())
@@ -1266,6 +1309,7 @@
     hiddens = [gather(r.hg.at[block_rows(block)]) for block in range(2)]
     if rec:
         states = [scatter(0), scatter(0)]
+        last_update = scatter(2)
         updates = gather(r.ug)
     if not rec:
         for block in (1, 0):
@@ -1318,42 +1362,54 @@
     tick(2)
     take_feed(0, feed[0])
     hiddens[0].start()
-    tick(2)
+    tick()
+    if rec:
+        local.wait(*chain)
+        update_last()
+    tick()
     hiddens[1].forward()
     tick()
     hiddens[1].finish()
     local.wait(*attention)
     branch_back(1)
+    if rec:
+        last_update.middle()
     tick()
-    attend_back(1)
-    close_keys(1)
     feed[0].release()
     feed[1].release()
     if rec:
+        attend_back(1, window=False)
         close_state(1)
         state_back(1, states[1])
         tick()
-    hiddens[0].forward()
-    local.wait(wqkv)
+        hiddens[0].forward()
+        states[1].middle()
+        attend_back(1, state=False)
+    else:
+        attend_back(1)
+        hiddens[0].forward()
+    close_keys(1)
+    local.wait(*wqkv)
     input_back(1, inputs[1])
-    if rec:
-        states[1].middle()
     tick()
     hiddens[0].finish()
     branch_back(0)
-    if rec:
-        tick(2)
-        local.wait(*chain)
+    sent = []
+    if rec:
+        tick()
         gate = jax.nn.sigmoid(r.gate[...])
         by_state = take_state(r.s1_v[...], states[1])
         states[1].release()
-        before = r.state[place.core_rows(), :].astype(f32)
+        before = r.state_v[...].astype(f32)
         add_small(
             GATE,
             jnp.sum(by_state * (before - r.z_v[...]) * gate * (1.0 - gate), axis=0, keepdims=True),
         )
         r.ug[place.rows(), :] = ((1.0 - gate) * by_state).astype(bf16)
         updates.start()
+        r.s1_v[...] = gate * r.s1_v[...] + (1.0 - gate) * last_update.finish()
+        sent.append(give(r.s1_v, r.final.at[place.core_rows()]))
+        last_update.release()
     inputs[1].middle()
     tick()
     attend_back(0)
@@ -1372,7 +1428,7 @@
         close_state(0)
         state_back(0, states[0])
         tick()
-    sent = [take_input(1, inputs[1])]
+    sent.append(take_input(1, inputs[1]))
     inputs[0].middle()
     tick()
     if rec:
@@ -1392,11 +1448,10 @@
         local.copy(r.g, r.dw.at[at_sqkv:])
     sent.append(take_input(0, inputs[0]))
     if rec:
-        take_state(r.state[place.core_rows(), :].astype(f32), states[0])
+        take_state(r.state_v[...].astype(f32), states[0])
     local.copy(small, r.small)
     for made in sent:
         made.wait_recv()
-    local.copy(r.ig_v, r.ig)
     while any(flow.done < flow.total for flow in flows):
         tick()
     for flow in flows:
@@ -1425,7 +1480,7 @@
         ig=held((2, 2 * quarter, model), f32),
     )
     ins = dict(
-        gy=grad_rows, x=rows, gain=small.gain, rel=small.rel, buckets=small.buckets, valid=valid
+        gain=small.gain, rel=small.rel, buckets=small.buckets, valid=valid
     )
 
     def flat(array):
@@ -1435,24 +1490,29 @@
     copied = dict(
         qkv=kept.qkv, lse=kept.lse, att=flat(kept.att), wn=flat(kept.wn), pre=flat(kept.pre), h=kept.h
     )
-    late = dict(act_in=flat(kept.act), u=flat(kept.u))
-    if rec:
-        ins.update(state=state, sgain=small.sgain, sshift=small.sshift, gate=small.gate)
+    late = dict(act_in=flat(kept.act), u=flat(kept.u), x=rows)
+    if rec:
+        late.update(state=state)
+        ins.update(sgain=small.sgain, sshift=small.sshift, gate=small.gate)
         copied.update(wsqkv=weights[4], wsout=weights[5])
         copied.update(sqkv=kept.sqkv, rlse=kept.rlse, sout=kept.sout, s1=kept.s1, z=kept.z)
         late.update(sn=flat(kept.sn), g_in=flat(parts))
+        outs.update(final=held((2 * quarter, model), f32))
     else:
+        ins.update(gy=grad_rows)
         late.update(parts=parts)
     far_ins = {**stacked, **copied, **late}
-    scatters = 6 if rec else 4
-    copies = (3 * 6 + 3 * 3 + 2) if rec else (3 * 4 + 3 * 4 + 2)
-    scratch = dict(small_v=pltpu.VMEM(outs["small"].shape, f32), ig_v=pltpu.VMEM(outs["ig"].shape, f32))
+    scatters = 7 if rec else 4
+    slots = 3 if rec else 2
+    copies = (3 * 7 + 3 * 3 + 3) if rec else (3 * 4 + 3 * 4 + 2)
+    scratch = dict(small_v=pltpu.VMEM(outs["small"].shape, f32), ig_v=pltpu.VMEM((2, quarter, model), f32))
     for name, array in stacked.items():
         scratch[name + "_v"] = pltpu.VMEM(array.shape[1:], array.dtype)
     for name, array in copied.items():
         scratch[name + "_v"] = pltpu.VMEM(array.shape, array.dtype)
     scratch.update(
         g=pltpu.VMEM((2 * block_len, model), bf16),
+        x_v=pltpu.VMEM((2, quarter, model), bf16),
         hg=pltpu.VMEM((2 * block_len, model), bf16),
         work=pltpu.VMEM((2 * hidden, model), bf16),
         dpre=pltpu.VMEM((2 * block_len, hidden), bf16),
@@ -1461,19 +1521,20 @@
         dqkv=pltpu.VMEM((2 * block_len, 3 * width), bf16),
         dbias=pltpu.VMEM((heads, min(128, block_len), 2 * block_len), f32),
         bias=pltpu.VMEM((heads, min(128, block_len), 2 * block_len), f32),
-        part=pltpu.VMEM((scatters // 2, block_len, model), bf16),
+        part=pltpu.VMEM((slots, block_len, model), bf16),
         near=pltpu.VMEM((scatters, 2, quarter, model), bf16),
-        out=pltpu.VMEM((scatters // 2, quarter, model), bf16),
+        out=pltpu.VMEM((slots, quarter, model), bf16),
         far=pltpu.VMEM((scatters, quarter, model), bf16),
         send_sems=pltpu.SemaphoreType.DMA((copies,)),
         recv_sems=pltpu.SemaphoreType.DMA((copies,)),
-        local_sems=pltpu.SemaphoreType.DMA((len(far_ins) + 6,)),
+        local_sems=pltpu.SemaphoreType.DMA((len(far_ins) + 8,)),
     )
     if rec:
         scratch.update(
             ug=pltpu.VMEM((block_len, model), bf16),
             dsout=pltpu.VMEM((block_len, width), bf16),
             dskv=pltpu.VMEM((block_len, 2 * width), f32),
+            state_v=pltpu.VMEM((quarter, model), bf16),
             dsqkv=pltpu.VMEM((2 * block_len, 3 * width), bf16),
         )
     else:
@@ -1564,8 +1625,44 @@
 
     for index in range(slots):
         load(index, True)
+    def place_sums():
+        mine = [jnp.where(layer == 0, sums[index, :SMALL_ROWS], sums[index, SMALL_ROWS:]) for index in range(3)]
+        gain[0] = mine[2][GAIN0 : GAIN1 + 1]
+        shift[0] = mine[2][SHIFT0 : SHIFT1 + 1]
+        down_bias[...] = mine[2][DOWN_BIAS : DOWN_BIAS + 1]
+        for target, row in ((sgain, SGAIN), (sshift, SSHIFT), (gate, GATE)):
+            target[...] = sums[2, SMALL_ROWS + row : SMALL_ROWS + row + 1]
+        by_core = [jnp.where(layer == 0, mine[0], mine[1]), jnp.where(layer == 0, mine[1], mine[0])]
+        heads, length = rel.shape[1] // 2, buckets.shape[1]
+        hot = back_hot(buckets[...], rel.shape[2])
+        for half in range(2):
+            up_bias[:, half * hidden : (half + 1) * hidden] = by_core[half][UP_BIAS : UP_BIAS + 1, :hidden]
+            for head in range(heads):
+                row = by_core[half][BY_DISTANCE : BY_DISTANCE + 1, head * length : (head + 1) * length]
+                at = half * heads + head
+                row = jnp.broadcast_to(row, (16, length))
+                rel[0, at : at + 1, :] = sum(dot_nt(part, hot) for part in in_parts(row))[:1]
+
+    rows_out = []
+
+    def place_rows():
+        rows_in[0].wait()
+        rows_out.append(pltpu.make_async_copy(acts_v, acts, row_sems.at[0]))
+        rows_out[0].start()
+        tiles = model // 128
+        for index, source, target in ((1, igs_v, igs_tiles), (2, state_v, state_tiles)):
+            rows_in[index].wait()
+            for tile in range(tiles):
+                target[..., tile, :] = source[..., tile * 128 : (tile + 1) * 128]
+            rows_out.append(pltpu.make_async_copy(target, igs if index == 1 else final, row_sems.at[index]))
+            rows_out[index].start()
+
     for index in range(len(jobs)):
         slot = index % slots
+        if index == slots:
+            place_rows()
+        if index == 2 * slots:
+            place_sums()
         load(index, False)
         if index >= slots:
             for made in stores(index - slots):
@@ -1575,34 +1672,6 @@
             made.start()
         if index + slots < len(jobs):
             load(index + slots, True)
-    mine = [jnp.where(layer == 0, sums[index, :SMALL_ROWS], sums[index, SMALL_ROWS:]) for index in range(3)]
-    gain[0] = mine[2][GAIN0 : GAIN1 + 1]
-    shift[0] = mine[2][SHIFT0 : SHIFT1 + 1]
-    down_bias[...] = mine[2][DOWN_BIAS : DOWN_BIAS + 1]
-    for target, row in ((sgain, SGAIN), (sshift, SSHIFT), (gate, GATE)):
-        target[...] = sums[2, SMALL_ROWS + row : SMALL_ROWS + row + 1]
-    by_core = [jnp.where(layer == 0, mine[0], mine[1]), jnp.where(layer == 0, mine[1], mine[0])]
-    heads, length = rel.shape[1] // 2, buckets.shape[1]
-    hot = back_hot(buckets[...], rel.shape[2])
-    for half in range(2):
-        up_bias[:, half * hidden : (half + 1) * hidden] = by_core[half][UP_BIAS : UP_BIAS + 1, :hidden]
-        for head in range(heads):
-            row = by_core[half][BY_DISTANCE : BY_DISTANCE + 1, head * length : (head + 1) * length]
-            at = half * heads + head
-            row = jnp.broadcast_to(row, (16, length))
-            rel[0, at : at + 1, :] = sum(dot_nt(part, hot) for part in in_parts(row))[:1]
-
-    rows_out = []
-    rows_in[0].wait()
-    rows_out.append(pltpu.make_async_copy(acts_v, acts, row_sems.at[0]))
-    rows_out[0].start()
-    tiles = model // 128
-    for index, source, target in ((1, igs_v, igs_tiles), (2, state_v, state_tiles)):
-        rows_in[index].wait()
-        for tile in range(tiles):
-            target[..., tile, :] = source[..., tile * 128 : (tile + 1) * 128]
-        rows_out.append(pltpu.make_async_copy(target, igs if index == 1 else final, row_sems.at[index]))
-        rows_out[index].start()
     for index in range(len(jobs) - slots, len(jobs)):
         for made in stores(index):
             made.wait()
@@ -1614,7 +1683,7 @@
     model = full_0.shape[2]
     anywhere = pl.BlockSpec(memory_space=pl.ANY)
     inside = pl.BlockSpec(memory_space=pltpu.VMEM)
-    slots, tiles = 4, model // 128
+    slots, tiles = 8, model // 128
     blocks, rows = acts[0].shape[:2]
     far_shapes = (
         ((1, 3, model, 2 * width), f32),
@@ -1672,33 +1741,31 @@
     cot_rows = cotangent[:, :, 0, :]
     rows = tokens[:, :, 0, :]
     state = state_init[:, 0, :]
-    smalls = (
-        norm_gain, norm_shift, up_bias[:, None, :], down_bias[:, None, :], jnp.swapaxes(rel_bias, 1, 2)
-    )
-    *weights, cot_all, gains, shifts, up_biases, down_biases, rels = share_weights(
-        block_len, w_qkv[0], w_out[0], w_up[0], w_down[0], w_state_qkv, w_state_out, cot_rows, *smalls
-    )
     small = SimpleNamespace(
-        gain=gains,
-        shift=shifts,
-        up_bias=up_biases,
-        down_bias=down_biases,
-        rel=rels,
+        gain=norm_gain,
+        shift=norm_shift,
+        up_bias=up_bias[:, None, :],
+        down_bias=down_bias[:, None, :],
+        rel=jnp.swapaxes(rel_bias, 1, 2),
         buckets=buckets[None],
         sgain=state_gain[None],
         sshift=state_shift[None],
         gate=gate_bias[None],
     )
-    kept0 = forward_layer(0, block_len, small, valid, weights, rows, state)
+    own_weights = (w_qkv[0], w_out[0], w_up[0], w_down[0], w_state_qkv, w_state_out)
+    kept0 = forward_layer(0, block_len, small, valid, own_weights, rows, state, cot_rows)
+    small.gain, small.shift, small.rel = kept0.gain_both, kept0.shift_both, kept0.rel_both
+    small.up_bias, small.down_bias = kept0.up_bias_both, kept0.down_bias_both
+    weights = (kept0.wqkv, kept0.wout, kept0.wup, kept0.wdown, kept0.wsqkv, kept0.wsout)
     kept1 = forward_layer(1, block_len, small, valid, weights, kept0.acts, state)
-    grad1 = backward_layer(1, docs, block_len, small, valid, weights, cot_rows, kept0.acts, state, kept1, cot_all)
+    grad1 = backward_layer(1, docs, block_len, small, valid, weights, None, kept0.acts, state, kept1, kept0.cot_all)
     grad0 = backward_layer(0, docs, block_len, small, valid, weights, grad1.ig, rows, state, kept0, grad1.dw)
     full, sums = sum_gradients(docs, grad0.dw, grad0.small, grad1.small)
     (
         qkv_grad, out_grad, up_grad, down_grad, state_qkv_grad, state_out_grad, acts, input_grads, final,
         gain_grad, shift_grad, rel_grad, up_bias_grad, down_bias_grad, sgain_grad, sshift_grad, gate_grad,
     ) = place_gradients(
-        grad1.full, grad0.full, full, (kept0.acts, kept1.acts), (grad0.ig, grad1.ig), kept1.final, sums,
+        grad1.full, grad0.full, full, (kept0.acts, kept1.acts), (grad0.ig, grad1.ig), grad1.final, sums,
         small.buckets, bucket_count, chip_heads, weights[0].shape[3], weights[2].shape[2],
     )
     return (

time: 545 us -> 531 us (0.974)
  Pallas kernels: 533 us -> 518 us
    pallas_call x1 -> x0, Pallas kernels: 17.9 us -> none  [share_weights(): pl.pallas_call(partial(share_kernel, block_len), out_shape=(halved(qkv.sh...]
    pallas_call x2, Pallas kernels: 154 us -> 164 us  [forward_layer(): pl.pallas_call(partial(forward_kernel, layer, [*ins, *far_ins, *outs, *sc...]
where the time goes in v5:
time: 531 us; the launch traced here: 521 us
  Pallas kernels  518 us (98%)
    pallas_call x2, Pallas kernels, backward_layer(): pl.pallas_call(partial(backward_kernel, layer, n, ring_names, [*ins, *far...  196 us
    pallas_call x2, Pallas kernels, forward_layer(): pl.pallas_call(partial(forward_kernel, layer, [*ins, *far_ins, *outs, *sc...  164 us
    pallas_call x1, Pallas kernels, sum_gradients(): pl.pallas_call(partial(sum_kernel, n), out_shape=(jax.ShapeDtypeStruct((2...  138 us
    pallas_call x1, Pallas kernels, place_gradients(): pl.pallas_call(partial(place_kernel, width, hidden), out_shape=[jax.Shape...  20.7 us

profile of v5, /device:TPU:0, one launch (start us, length us, event | category | flops | bytes accessed | tf_op | source)
XLA Modules:
  0.0 520.9 jit_solution(10231397854023024007)
XLA Ops:
  0.7 1.3 fusion.refs_2_.refs_3_
  1.9 78.8 %forward_local.1 = (bf16[2,512,1024]{2,1,0:T(8,128)(2,1)}, bf16[2,512,768]{2,1,0:T(8,128)(2,1)}, f32[2,512,128]{2,1,0:T(8,128)}, bf16[2,512,256]{2,1,0:T(8,128)(...) custom-call(bf16[2,256,1024]{2,1,0:T(8,128)(2,1)} %bitcast.39, ...), custom_call_target="tpu_custom_call" | custom-call | tf_op jit(solution)/shard_map/forward_local/pallas_call | solution.py:640
  80.7 84.8 %forward_recurrent.1 = (bf16[2,512,1024]{2,1,0:T(8,128)(2,1)}, bf16[2,512,768]{2,1,0:T(8,128)(2,1)}, f32[2,512,128]{2,1,0:T(8,128)}, bf16[2,512,256]{2,1,0:T(8,1...) custom-call(bf16[2,256,1024]{2,1,0:T(8,128)(2,1)} %get-tuple-element, ...), custom_call_target="tpu_custom_call" | custom-call | tf_op jit(solution)/shard_map/forward_recurrent/pallas_call | solution.py:640
  165.6 106.1 %backward_recurrent.1 = (bf16[2,2048,1024]{2,1,0:T(8,128)(2,1)}, bf16[2048,1024]{1,0:T(8,128)(2,1)}, f32[16,1024]{1,0:T(8,128)}, f32[2,256,1024]{2,1,0:T(8,128)}, f32[256,1024]{1,0:T(8,128)}) custom-call(f32[2,2,1024]{2,1,0:T(2,128)} %get-tuple-element.81.refs_7_.refs_0_, f32[2,4,32]{2,1,0:T(4,128)} %get-tuple-element.82.refs_11_.refs_1_, ...), custom_call_target="tpu_custom_call" | custom-call | tf_op jit(solution)/shard_map/backward_recurrent/pallas_call | solution.py:1550
  271.6 89.9 %backward_local.1 = (bf16[2,2048,1024]{2,1,0:T(8,128)(2,1)}, bf16[3072,1024]{1,0:T(8,128)(2,1)}, f32[16,1024]{1,0:T(8,128)}, f32[2,256,1024]{2,1,0:T(8,128)}) custom-call(f32[2,2,1024]{2,1,0:T(2,128)} %get-tuple-element.81.refs_7_.refs_0_, f32[2,4,32]{2,1,0:T(4,128)} %get-tuple-element.82.refs_11_.refs_1_, s32[1,512]{1,0:T(1,128)} %bitcast.61, ...), custom_call_target="tpu_custom_call" | custom-call | tf_op jit(solution)/shard_map/backward_local/pallas_call | solution.py:1550
  361.6 138.1 %sum_gradients.1 = (bf16[2,3072,1024]{2,1,0:T(8,128)(2,1)}, f32[3,32,1024]{2,1,0:T(8,128)}) custom-call(bf16[3072,1024]{1,0:T(8,128)(2,1)} %get-tuple-element.120.parts, f32[16,1024]{1,0:T(8,128)} %get-tuple-element.121.small_0, f32[16,1024]{1,0:T(8,128)} %get-tuple-element.122.small_1), custom_call_target="tpu_custom_call" | custom-call | tf_op jit(solution)/shard_map/sum_gradients/pallas_call | solution.py:931
  499.7 20.7 %place_gradients.1 = (f32[1,3,1024,512]{3,2,1,0:T(8,128)}, f32[1,512,1024]{2,1,0:T(8,128)}, f32[1,1024,2048]{2,1,0:T(8,128)}, f32[1,2048,1024]{2,1,0:T(8,128)}, ...) custom-call(bf16[2,2048,1024]{2,1,0:T(8,128)(2,1)} %get-tuple-elemen, ...), custom_call_target="tpu_custom_call" | custom-call | tf_op jit(solution)/shard_map/place_gradients/pallas_call | solution.py:1709

commit v6 on v5

--- a/solution.py
+++ b/solution.py
@@ -214,58 +214,14 @@
     return jnp.where(keep, logits * scale + bias, negative), here
 
 
-def forward_kernel(layer, names, *refs):
-    r = SimpleNamespace(**dict(zip(names, refs)))
+def forward_stages(layer, r, place, net, local, scatter, slots):
     rec = layer == 1
     length = r.u_v.shape[1]
     heads = r.rel.shape[1] // 2
     head_size = r.att_v.shape[2] // heads
     width = heads * head_size
     scale = head_size ** (-0.5)
-    place = Place(length)
-    net, local = Net(r.send_sems, r.recv_sems), Local(r.local_sems)
     chunk = min(128, length)
-
-    place.meet()
-    if rec:
-        load = [local.copy(r.wqkv.at[layer], r.wqkv_v), local.copy(r.wout.at[layer], r.wout_v)]
-        load_mlp = [local.copy(r.wup.at[layer], r.wup_v), local.copy(r.wdown.at[layer], r.wdown_v)]
-        load_state = [local.copy(r.wsqkv, r.wsqkv_v), local.copy(r.wsout, r.wsout_v)]
-    else:
-        def share(source, target, axis=None):
-            def half(c):
-                if axis is None:
-                    return source.at[0]
-                size = source.shape[axis] // 2
-                index = [slice(None)] * len(source.shape)
-                index[axis] = pl.ds(pl.multiple_of(c * size, size), size)
-                return source.at[tuple(index)]
-
-            target = target.at[place.c]
-            return net.copy(half(1 - place.c), target, place.core), local.copy(half(place.c), target)
-
-        def shared(*pairs):
-            for far, near in pairs:
-                far.wait_recv()
-                local.wait(near)
-
-        smalls = [
-            share(r.gain_own, r.gain),
-            share(r.shift_own, r.shift),
-            share(r.up_bias_own, r.up_bias),
-            share(r.down_bias_own, r.down_bias),
-            share(r.rel_own, r.rel),
-        ]
-        first_weights = [share(r.qkv_own, r.wqkv_s, 2), share(r.out_own, r.wout_s, 0)]
-        later_weights = [share(r.up_own, r.wup_s, 1), share(r.down_own, r.wdown_s, 0)]
-        state_weights = []
-        for source, target, axis in ((r.sqkv_own, r.wsqkv_s, 2), (r.sout_own, r.wsout_s, 0)):
-            size = source.shape[axis] // 2
-            at = pl.ds(pl.multiple_of(place.c * size, size), size)
-            part = source.at[:, :, at] if axis == 2 else source.at[at]
-            state_weights.append(local.copy(part, target))
-        r.wqkv_v, r.wout_v = r.wqkv_s.at[layer], r.wout_s.at[layer]
-        r.wup_v, r.wdown_v = r.wup_s.at[layer], r.wdown_s.at[layer]
 
     gain = lambda index: r.gain[layer, index : index + 1, :]
     shift = lambda index: r.shift[layer, index : index + 1, :]
@@ -273,20 +229,14 @@
     def gather(buffer):
         return Gather(place, net, buffer)
 
-    scatter_count = [0]
-
-    def scatter():
-        index = scatter_count[0]
-        scatter_count[0] += 1
-        return Scatter(
-            place, net, r.part.at[index], r.near.at[index], r.out.at[index], r.far.at[index]
-        )
+    def own_rows(block):
+        return r.x[block, place.core_rows(), :].astype(f32)
 
     def norm_state(rows, index):
         r.sn_v[index, place.rows(), :] = layer_norm(rows, r.sgain[...], r.sshift[...]).astype(bf16)
 
     def norm_first(block):
-        rows = r.x[block, place.core_rows(), :].astype(f32)
+        rows = own_rows(block)
         r.u_v[block, place.rows(), :] = layer_norm(rows, gain(0), shift(0)).astype(bf16)
 
     def project(source, weights, target):
@@ -401,7 +351,7 @@
                 r.rlse_v[at, :] = pack(lses)
 
     def take_branch(block, from_out):
-        rows = r.x[block, place.core_rows(), :].astype(f32) + from_out.finish()
+        rows = own_rows(block) + from_out.finish()
         r.h_v[block] = rows
         r.wn_v[block, place.rows(), :] = layer_norm(rows, gain(1), shift(1)).astype(bf16)
 
@@ -423,232 +373,331 @@
         own[...] = rows.astype(bf16)
         return net.copy(own, own, place.core)
 
-    def cotangent(block):
-        own = r.cot_v.at[block, place.rows()]
-        local.wait(local.copy(r.cot.at[block, place.core_rows()], own))
-        cot[block].start()
-
-    branch = [scatter(), scatter()]
-    result = [scatter(), scatter()]
+    branch = [scatter(slots[0]), scatter(slots[1])]
+    result = [scatter(slots[2]), scatter(slots[3])]
     first = [gather(r.u_v.at[block]) for block in range(2)]
     second = [gather(r.wn_v.at[block]) for block in range(2)]
-    if rec:
-        update = [scatter()]
-        state = [gather(r.sn_v.at[block]) for block in range(2)]
-        gate = jax.nn.sigmoid(r.gate[...])
-        norm_state(r.state[place.core_rows(), :].astype(f32), 0)
-        state[0].start()
-    else:
-        cot = [gather(r.cot_v.at[block]) for block in range(2)]
-        cotangent(1)
-        shared(*smalls)
-    norm_first(0)
-    first[0].start()
-    norm_first(1)
-    first[1].start()
-    fill_bias(r.bias, bias_rows(r.rel[layer], r.buckets[...], place.c))
-    if rec:
-        state[0].forward()
-    if not rec:
-        cot[1].forward()
-    first[0].forward()
-    if rec:
-        state[0].finish()
-        local.wait(*load_state)
-        project(r.sn_v.at[0], r.wsqkv_v, r.sqkv_v.at[0])
-    first[0].finish()
-    if rec:
-        local.wait(*load)
-    else:
-        shared(*first_weights)
-    project(r.u_v.at[0], r.wqkv_v, r.qkv_v.at[0])
-    if rec:
-        recur(0)
-        reduce_from(r.sout_v.at[0], r.wsout_v, update[0])
-    else:
-        attend(0)
-    first[1].forward()
-    if rec:
-        update[0].middle()
-        attend(0)
-    reduce_from(r.att_v.at[0], r.wout_v, branch[0])
-    if not rec:
-        branch[0].middle()
-    first[1].finish()
-    project(r.u_v.at[1], r.wqkv_v, r.qkv_v.at[1])
-    local.copy(r.u_v, r.u)
-    local.copy(r.qkv_v, r.qkv)
-    if rec:
-        branch[0].middle()
-        update_rows = update[0].finish()
-        r.z_v[...] = update_rows
-        state_rows = gate * r.state[place.core_rows(), :].astype(f32) + (1.0 - gate) * update_rows
-        r.s1_v[...] = state_rows
-        norm_state(state_rows, 1)
-        state[1].start()
-        local.copy(r.z_v, r.z)
-        local.copy(r.s1_v, r.s1)
-        attend(1, state=False)
-    else:
-        attend(1)
-        reduce_from(r.att_v.at[1], r.wout_v, branch[1])
-    take_branch(0, branch[0])
-    second[0].start()
-    if rec:
-        state[1].forward()
-        state[1].finish()
-        project(r.sn_v.at[1], r.wsqkv_v, r.sqkv_v.at[1])
-        local.copy(r.sn_v, r.sn)
-        local.copy(r.sqkv_v, r.sqkv)
-        attend(1, window=False)
-        reduce_from(r.att_v.at[1], r.wout_v, branch[1])
-    local.copy(r.att_v, r.att)
-    local.copy(r.lse_v, r.lse)
-    second[0].forward()
-    branch[1].middle()
-    second[0].finish()
-    if rec:
-        local.wait(*load_mlp)
-    else:
-        shared(*later_weights)
-        local.wait(*state_weights)
-        for source, target in (
-            (r.wqkv_s, r.wqkv),
-            (r.wout_s, r.wout),
-            (r.wup_s, r.wup),
-            (r.wdown_s, r.wdown),
-            (r.wsqkv_s, r.wsqkv),
-            (r.wsout_s, r.wsout),
-            (r.gain, r.gain_both),
-            (r.shift, r.shift_both),
-            (r.up_bias, r.up_bias_both),
-            (r.down_bias, r.down_bias_both),
-            (r.rel, r.rel_both),
-        ):
-            local.copy(source, target)
-    feed_up(0)
-    reduce_from(r.act_v.at[0], r.wdown_v, result[0])
-    take_branch(1, branch[1])
-    second[1].start()
-    local.copy(r.h_v, r.h)
-    result[0].middle()
-    if rec:
-        recur(1)
-        local.copy(r.sout_v, r.sout)
-        local.copy(r.rlse_v, r.rlse)
-    second[1].forward()
-    second[1].finish()
-    local.copy(r.wn_v, r.wn)
-    feed_up(1)
-    local.copy(r.pre_v, r.pre)
-    local.copy(r.act_v, r.act)
-    reduce_from(r.act_v.at[1], r.wdown_v, result[1])
-    sent = [take_result(0, result[0])]
-    result[1].middle()
-    if not rec:
-        cotangent(0)
-    sent.append(take_result(1, result[1]))
+    return SimpleNamespace(**locals())
+
+
+def forward_kernel(names, *refs):
+    every = dict(zip(names, refs))
+    r = SimpleNamespace(**every)
+    own = [{name[:-2]: ref for name, ref in every.items() if name.endswith(mark)} for mark in ("_0", "_1")]
+    r0, r1 = (SimpleNamespace(**{**every, **part}) for part in own)
+    r1.x = r0.acts_v
+    place = Place(r0.u_v.shape[1])
+    net, local = Net(r.send_sems, r.recv_sems), Local(r.local_sems)
+    gate = jax.nn.sigmoid(r.gate[...])
+    scatter_count = [0]
+
+    def scatter(slot):
+        index = scatter_count[0]
+        scatter_count[0] += 1
+        return Scatter(place, net, r.part.at[slot], r.near.at[index], r.out.at[slot], r.far.at[index])
+
+    def share(source, target, axis=None):
+        def half(c):
+            if axis is None:
+                return source.at[0]
+            size = source.shape[axis] // 2
+            index = [slice(None)] * len(source.shape)
+            index[axis] = pl.ds(pl.multiple_of(c * size, size), size)
+            return source.at[tuple(index)]
+
+        target = target.at[place.c]
+        return net.copy(half(1 - place.c), target, place.core), local.copy(half(place.c), target)
+
+    def shared(*pairs):
+        for far, near in pairs:
+            far.wait_recv()
+            local.wait(near)
+
+    class Cotangent:
+        def __init__(self, block):
+            source, target = r.cot.at[block, place.core_rows()], r.cot_all.at[block, place.rows()]
+            self.block = block
+            self.across, self.near = net.copy(source, target, place.chip), net.copy(source, target, place.core)
+            self.staged = local.copy(source, r.cot_v.at[block])
+
+        def forward(self):
+            self.across.wait_recv()
+            passed = r.cot_all.at[self.block, place.rows(x_other=True)]
+            self.passed = net.copy(passed, passed, place.core)
+            local.wait(self.staged)
+            local.copy(r.cot_v.at[self.block], r.cot_all.at[self.block, place.rows()])
+
+        def finish(self):
+            self.near.wait_recv()
+            self.passed.wait_recv()
+
+    place.meet()
+    smalls = [
+        share(r.gain_own, r.gain),
+        share(r.shift_own, r.shift),
+        share(r.up_bias_own, r.up_bias),
+        share(r.down_bias_own, r.down_bias),
+        share(r.rel_own, r.rel),
+    ]
+    first_weights = [share(r.qkv_own, r.wqkv_s, 2), share(r.out_own, r.wout_s, 0)]
+    later_weights = [share(r.up_own, r.wup_s, 1), share(r.down_own, r.wdown_s, 0)]
+    state_weights = []
+    for source, target, axis in ((r.sqkv_own, r.wsqkv_v, 2), (r.sout_own, r.wsout_v, 0)):
+        size = source.shape[axis] // 2
+        at = pl.ds(pl.multiple_of(place.c * size, size), size)
+        part = source.at[:, :, at] if axis == 2 else source.at[at]
+        state_weights.append(local.copy(part, target))
+    for layer, one in enumerate((r0, r1)):
+        one.wqkv_v, one.wout_v = r.wqkv_s.at[layer], r.wout_s.at[layer]
+        one.wup_v, one.wdown_v = r.wup_s.at[layer], r.wdown_s.at[layer]
+    zero = forward_stages(0, r0, place, net, local, scatter, (0, 1, 2, 3))
+    one = forward_stages(1, r1, place, net, local, scatter, (1, 0, 2, 3))
+    update = scatter(0)
+    state = [one.gather(r1.sn_v.at[block]) for block in range(2)]
+    kept = []
+
+    def keep(source, target):
+        kept.append(local.copy(source, target))
+
+    one.norm_state(r.state[place.core_rows(), :].astype(f32), 0)
+    state[0].start()
+    shared(*smalls)
+    for block in range(2):
+        zero.norm_first(block)
+        zero.first[block].start()
+    fill_bias(r.bias, bias_rows(r.rel[0], r.buckets[...], place.c))
+    state[0].forward()
+    zero.first[0].forward()
+    shared(*first_weights)
+    zero.first[0].finish()
+    zero.project(r0.u_v.at[0], r0.wqkv_v, r0.qkv_v.at[0])
+    zero.attend(0)
+    zero.reduce_from(r0.att_v.at[0], r0.wout_v, zero.branch[0])
+    zero.first[1].forward()
+    zero.branch[0].middle()
+    state[0].finish()
+    local.wait(*state_weights)
+    one.project(r1.sn_v.at[0], r.wsqkv_v, r1.sqkv_v.at[0])
+    zero.first[1].finish()
+    zero.project(r0.u_v.at[1], r0.wqkv_v, r0.qkv_v.at[1])
+    keep(r0.u_v, r0.u)
+    keep(r0.qkv_v, r0.qkv)
+    zero.attend(1)
+    zero.reduce_from(r0.att_v.at[1], r0.wout_v, zero.branch[1])
+    zero.take_branch(0, zero.branch[0])
+    zero.second[0].start()
+    keep(r0.att_v, r0.att)
+    keep(r0.lse_v, r0.lse)
+    zero.branch[1].middle()
+    shared(*later_weights)
+    for source, target in (
+        (r.wqkv_s, r.wqkv),
+        (r.wout_s, r.wout),
+        (r.wup_s, r.wup),
+        (r.wdown_s, r.wdown),
+        (r.wsqkv_v, r.wsqkv),
+        (r.wsout_v, r.wsout),
+        (r.gain, r.gain_both),
+        (r.shift, r.shift_both),
+        (r.up_bias, r.up_bias_both),
+        (r.down_bias, r.down_bias_both),
+        (r.rel, r.rel_both),
+    ):
+        local.copy(source, target)
+    zero.second[0].forward()
+    zero.second[0].finish()
+    zero.feed_up(0)
+    zero.reduce_from(r0.act_v.at[0], r0.wdown_v, zero.result[0])
+    zero.take_branch(1, zero.branch[1])
+    zero.second[1].start()
+    keep(r0.h_v, r0.h)
+    zero.result[0].middle()
+    zero.second[1].forward()
+    zero.second[1].finish()
+    keep(r0.wn_v, r0.wn)
+    zero.feed_up(1)
+    keep(r0.pre_v, r0.pre)
+    keep(r0.act_v, r0.act)
+    zero.reduce_from(r0.act_v.at[1], r0.wdown_v, zero.result[1])
+    sent = [zero.take_result(0, zero.result[0])]
+    one.norm_first(0)
+    one.first[0].start()
+    zero.result[1].middle()
+    cotangents = [Cotangent(1)]
+    fill_bias(r.bias, bias_rows(r.rel[1], r.buckets[...], place.c))
+    for done in (*zero.branch, zero.result[0]):
+        done.release()
+    sent.append(zero.take_result(1, zero.result[1]))
+    one.norm_first(1)
+    one.first[1].start()
+    zero.result[1].release()
+    local.wait(*kept)
+    one.first[0].forward()
+    one.first[0].finish()
+    one.project(r1.u_v.at[0], r1.wqkv_v, r1.qkv_v.at[0])
+    one.recur(0)
+    one.reduce_from(r1.sout_v.at[0], r.wsout_v, update)
+    cotangents[0].forward()
+    update.middle()
+    one.attend(0)
+    one.reduce_from(r1.att_v.at[0], r1.wout_v, one.branch[0])
+    one.first[1].forward()
+    one.first[1].finish()
+    one.project(r1.u_v.at[1], r1.wqkv_v, r1.qkv_v.at[1])
+    local.copy(r1.u_v, r1.u)
+    local.copy(r1.qkv_v, r1.qkv)
+    one.branch[0].middle()
+    update_rows = update.finish()
+    update.release()
+    r1.z_v[...] = update_rows
+    state_rows = gate * r.state[place.core_rows(), :].astype(f32) + (1.0 - gate) * update_rows
+    r1.s1_v[...] = state_rows
+    one.norm_state(state_rows, 1)
+    state[1].start()
+    local.copy(r1.z_v, r1.z)
+    local.copy(r1.s1_v, r1.s1)
+    one.attend(1, state=False)
+    one.take_branch(0, one.branch[0])
+    one.second[0].start()
+    state[1].forward()
+    state[1].finish()
+    one.project(r1.sn_v.at[1], r.wsqkv_v, r1.sqkv_v.at[1])
+    local.copy(r1.sn_v, r1.sn)
+    local.copy(r1.sqkv_v, r1.sqkv)
+    one.attend(1, window=False)
+    one.reduce_from(r1.att_v.at[1], r1.wout_v, one.branch[1])
+    local.copy(r1.att_v, r1.att)
+    local.copy(r1.lse_v, r1.lse)
+    one.second[0].forward()
+    one.branch[1].middle()
+    one.second[0].finish()
+    one.feed_up(0)
+    one.reduce_from(r1.act_v.at[0], r1.wdown_v, one.result[0])
+    one.take_branch(1, one.branch[1])
+    one.second[1].start()
+    local.copy(r1.h_v, r1.h)
+    one.result[0].middle()
+    cotangents.append(Cotangent(0))
+    one.recur(1)
+    local.copy(r1.sout_v, r1.sout)
+    local.copy(r1.rlse_v, r1.rlse)
+    one.second[1].forward()
+    one.second[1].finish()
+    local.copy(r1.wn_v, r1.wn)
+    one.feed_up(1)
+    local.copy(r1.pre_v, r1.pre)
+    local.copy(r1.act_v, r1.act)
+    one.reduce_from(r1.act_v.at[1], r1.wdown_v, one.result[1])
+    sent.append(one.take_result(0, one.result[0]))
+    one.result[1].middle()
+    cotangents[1].forward()
+    sent.append(one.take_result(1, one.result[1]))
     for made in sent:
         made.wait_recv()
-    local.copy(r.acts_v, r.acts)
-    if not rec:
-        cot[0].forward()
-        cot[1].finish()
-        cot[0].finish()
-        local.copy(r.cot_v, r.cot_all)
+    local.copy(r0.acts_v, r0.acts)
+    local.copy(r1.acts_v, r1.acts)
+    for made in cotangents:
+        made.finish()
     local.drain()
     net.drain()
 
 
-def forward_layer(layer, block_len, small, valid, weights, rows, state, cot=None):
-    rec = layer == 1
-    wqkv, wout, wup, wdown = weights[:4]
+def forward_layers(block_len, small, valid, weights, rows, state, cot):
+    wqkv, wout, wup, wdown, wsqkv, wsout = weights
     model = rows.shape[2]
-    width, hidden = (wqkv.shape[3], wup.shape[2]) if rec else (wqkv.shape[2] // 2, wup.shape[1] // 2)
+    width, hidden = wqkv.shape[2] // 2, wup.shape[1] // 2
     quarter = block_len // 4
     heads = small.rel.shape[1] // 2
 
     def held(shape, dtype):
         return jax.ShapeDtypeStruct(shape, dtype)
 
-    outs = dict(
-        u=held((2, block_len, model), bf16),
+    local_kinds = dict(
         qkv=held((2, block_len, 3 * width), bf16),
         lse=held((2, block_len, 128), f32),
         att=held((2, block_len, width), bf16),
-        wn=held((2, block_len, model), bf16),
         pre=held((2, block_len, hidden), bf16),
         act=held((2, block_len, hidden), bf16),
         h=held((2, quarter, model), f32),
+    )
+    own_kinds = dict(
+        u=held((2, block_len, model), bf16),
+        wn=held((2, block_len, model), bf16),
         acts=held((2, 2 * quarter, model), bf16),
     )
-    ins = dict(x=rows, buckets=small.buckets, valid=valid)
-    names = ("gain", "shift", "up_bias", "down_bias", "rel")
-    smalls = {name: getattr(small, name) for name in names}
-    shapes = dict(
-        wqkv=(3, model, width),
-        wout=(width, model),
-        wup=(model, hidden),
-        wdown=(hidden, model),
-        wsqkv=(3, model, width),
-        wsout=(width, model),
-    )
-    scratch, given = {}, {}
-    if rec:
-        outs.update(
-            sn=held((2, block_len, model), bf16),
-            sqkv=held((2, block_len, 3 * width), bf16),
-            rlse=held((block_len, 128), f32),
-            sout=held((2, block_len, width), bf16),
-            s1=held((quarter, model), f32),
-            z=held((quarter, model), f32),
-        )
-        ins.update(state=state, sgain=small.sgain, sshift=small.sshift, gate=small.gate, **smalls)
-        far_ins = dict(wqkv=wqkv, wout=wout, wup=wup, wdown=wdown, wsqkv=weights[4], wsout=weights[5])
-        scratch.update({name + "_v": pltpu.VMEM(shape, bf16) for name, shape in shapes.items()})
-        scratch.update(early=pltpu.VMEM((block_len, width), f32))
-    else:
-        far_ins = dict(
-            qkv_own=wqkv, out_own=wout, up_own=wup, down_own=wdown, sqkv_own=weights[4], sout_own=weights[5]
-        )
-        far_ins.update({name + "_own": array for name, array in smalls.items()}, cot=cot)
-        given = dict(cot_all=held((2, block_len, model), bf16))
-        scratch.update(cot_v=pltpu.VMEM((2, block_len, model), bf16))
-        for name, shape in shapes.items():
-            shape = shape if name.startswith("ws") else (2, *shape)
-            given[name] = held(shape, bf16)
-            scratch[name + "_s"] = pltpu.VMEM(shape, bf16)
-        for name, array in smalls.items():
-            given[name + "_both"] = held((2, *array.shape[1:]), f32)
-            scratch[name] = pltpu.VMEM((2, *array.shape[1:]), f32)
-    scatters = 5 if rec else 4
-    copies = (3 * 6 + 3 * 5 + 2) if rec else (3 * 6 + 3 * 4 + 2 + 9)
-    scratch.update({name + "_v": pltpu.VMEM(kind.shape, kind.dtype) for name, kind in outs.items()})
-    outs.update(given)
+    rec_kinds = dict(
+        sn=held((2, block_len, model), bf16),
+        sqkv=held((2, block_len, 3 * width), bf16),
+        rlse=held((block_len, 128), f32),
+        sout=held((2, block_len, width), bf16),
+        s1=held((quarter, model), f32),
+        z=held((quarter, model), f32),
+    )
+    outs, scratch = {}, {}
+    for mark in ("_0", "_1"):
+        outs.update({name + mark: kind for name, kind in {**local_kinds, **own_kinds}.items()})
+        scratch.update({name + "_v" + mark: pltpu.VMEM(kind.shape, kind.dtype) for name, kind in own_kinds.items()})
+    outs.update({name + "_1": kind for name, kind in rec_kinds.items()})
+    scratch.update({name + "_v_1": pltpu.VMEM(kind.shape, kind.dtype) for name, kind in rec_kinds.items()})
+    scratch.update({name + "_v": pltpu.VMEM(kind.shape, kind.dtype) for name, kind in local_kinds.items()})
+    outs.update(cot_all=held((2, block_len, model), bf16))
+    ins = dict(
+        x=rows,
+        buckets=small.buckets,
+        valid=valid,
+        state=state,
+        sgain=small.sgain,
+        sshift=small.sshift,
+        gate=small.gate,
+    )
+    far_ins = dict(
+        qkv_own=wqkv, out_own=wout, up_own=wup, down_own=wdown, sqkv_own=wsqkv, sout_own=wsout, cot=cot
+    )
+    for name in ("gain", "shift", "up_bias", "down_bias", "rel"):
+        array = getattr(small, name)
+        far_ins[name + "_own"] = array
+        outs[name + "_both"] = held((2, *array.shape[1:]), f32)
+        scratch[name] = pltpu.VMEM((2, *array.shape[1:]), f32)
+    stacked = dict(wqkv=(3, model, width), wout=(width, model), wup=(model, hidden), wdown=(hidden, model))
+    for name, shape in stacked.items():
+        outs[name] = held((2, *shape), bf16)
+        scratch[name + "_s"] = pltpu.VMEM((2, *shape), bf16)
+    for name, shape in dict(wsqkv=(3, model, width), wsout=(width, model)).items():
+        outs[name] = held(shape, bf16)
+        scratch[name + "_v"] = pltpu.VMEM(shape, bf16)
+    scatters, gathers = 9, 12
+    copies = 3 * (scatters + gathers) + 4 + 9
     scratch.update(
+        cot_v=pltpu.VMEM((2, quarter, model), bf16),
+        early=pltpu.VMEM((block_len, width), f32),
         bias=pltpu.VMEM((heads, min(128, block_len), 2 * block_len), f32),
-        part=pltpu.VMEM((scatters, block_len, model), bf16),
+        part=pltpu.VMEM((4, block_len, model), bf16),
         near=pltpu.VMEM((scatters, 2, quarter, model), bf16),
-        out=pltpu.VMEM((scatters, quarter, model), bf16),
+        out=pltpu.VMEM((4, quarter, model), bf16),
         far=pltpu.VMEM((scatters, quarter, model), bf16),
         send_sems=pltpu.SemaphoreType.DMA((copies,)),
         recv_sems=pltpu.SemaphoreType.DMA((copies,)),
-        local_sems=pltpu.SemaphoreType.DMA((len(far_ins) + len(outs) + 1,)),
+        local_sems=pltpu.SemaphoreType.DMA((len(far_ins) + len(outs) + 4,)),
     )
     anywhere = pl.BlockSpec(memory_space=pl.ANY)
     inside = pl.BlockSpec(memory_space=pltpu.VMEM)
     results = pl.pallas_call(
-        partial(forward_kernel, layer, [*ins, *far_ins, *outs, *scratch]),
+        partial(forward_kernel, [*ins, *far_ins, *outs, *scratch]),
         out_shape=tuple(outs.values()),
         in_specs=[inside] * len(ins) + [anywhere] * len(far_ins),
         out_specs=[anywhere] * len(outs),
         scratch_shapes=list(scratch.values()),
         compiler_params=pltpu.CompilerParams(
-            collective_id=1 + layer, has_side_effects=True, vmem_limit_bytes=VMEM_LIMIT
+            collective_id=0, has_side_effects=True, vmem_limit_bytes=VMEM_LIMIT
         ),
-        name="forward_recurrent" if rec else "forward_local",
+        name="forward_layers",
     )(*ins.values(), *far_ins.values())
-    return SimpleNamespace(**dict(zip(outs, results)))
+    given = dict(zip(outs, results))
+    layers = [
+        SimpleNamespace(**{name[:-2]: array for name, array in given.items() if name.endswith(mark)})
+        for mark in ("_0", "_1")
+    ]
+    return (*layers, SimpleNamespace(**given))
 
 
 def ring_place(n, c, d):
@@ -1753,12 +1802,11 @@
         gate=gate_bias[None],
     )
     own_weights = (w_qkv[0], w_out[0], w_up[0], w_down[0], w_state_qkv, w_state_out)
-    kept0 = forward_layer(0, block_len, small, valid, own_weights, rows, state, cot_rows)
-    small.gain, small.shift, small.rel = kept0.gain_both, kept0.shift_both, kept0.rel_both
-    small.up_bias, small.down_bias = kept0.up_bias_both, kept0.down_bias_both
-    weights = (kept0.wqkv, kept0.wout, kept0.wup, kept0.wdown, kept0.wsqkv, kept0.wsout)
-    kept1 = forward_layer(1, block_len, small, valid, weights, kept0.acts, state)
-    grad1 = backward_layer(1, docs, block_len, small, valid, weights, None, kept0.acts, state, kept1, kept0.cot_all)
+    kept0, kept1, both = forward_layers(block_len, small, valid, own_weights, rows, state, cot_rows)
+    small.gain, small.shift, small.rel = both.gain_both, both.shift_both, both.rel_both
+    small.up_bias, small.down_bias = both.up_bias_both, both.down_bias_both
+    weights = (both.wqkv, both.wout, both.wup, both.wdown, both.wsqkv, both.wsout)
+    grad1 = backward_layer(1, docs, block_len, small, valid, weights, None, kept0.acts, state, kept1, both.cot_all)
     grad0 = backward_layer(0, docs, block_len, small, valid, weights, grad1.ig, rows, state, kept0, grad1.dw)
     full, sums = sum_gradients(docs, grad0.dw, grad0.small, grad1.small)
     (

time: 531 us -> 516 us (0.972)
  Pallas kernels: 518 us -> 503 us
    pallas_call x2 -> x1, Pallas kernels: 164 us -> 147 us  [forward_layers(): pl.pallas_call(partial(forward_kernel, [*ins, *far_ins, *outs, *scratch])...]
where the time goes in v6:
time: 516 us; the launch traced here: 505 us
  Pallas kernels  503 us (97%)
    pallas_call x2, Pallas kernels, backward_layer(): pl.pallas_call(partial(backward_kernel, layer, n, ring_names, [*ins, *far...  197 us
    pallas_call x1, Pallas kernels, forward_layers(): pl.pallas_call(partial(forward_kernel, [*ins, *far_ins, *outs, *scratch])...  147 us
    pallas_call x1, Pallas kernels, sum_gradients(): pl.pallas_call(partial(sum_kernel, n), out_shape=(jax.ShapeDtypeStruct((2...  138 us
    pallas_call x1, Pallas kernels, place_gradients(): pl.pallas_call(partial(place_kernel, width, hidden), out_shape=[jax.Shape...  20.7 us

profile of v6, /device:TPU:0, one launch (start us, length us, event | category | flops | bytes accessed | tf_op | source)
XLA Modules:
  0.0 505.4 jit_solution(15269040935056836593)
XLA Ops:
  0.7 1.3 fusion.refs_2_.refs_3_
  1.9 147.0 %forward_layers.1 = (bf16[2,512,768]{2,1,0:T(8,128)(2,1)}, f32[2,512,128]{2,1,0:T(8,128)}, bf16[2,512,256]{2,1,0:T(8,128)(2,1)}, bf16[2,512,1024]{2,1,0:T(8,128)...) custom-call(bf16[2,256,1024]{2,1,0:T(8,128)(2,1)} %bitcast.37, ...), custom_call_target="tpu_custom_call" | custom-call | tf_op jit(solution)/shard_map/forward_layers/pallas_call | solution.py:684
  149.0 107.1 %backward_recurrent.1 = (bf16[2,2048,1024]{2,1,0:T(8,128)(2,1)}, bf16[2048,1024]{1,0:T(8,128)(2,1)}, f32[16,1024]{1,0:T(8,128)}, f32[2,256,1024]{2,1,0:T(8,128)}, f32[256,1024]{1,0:T(8,128)}) custom-call(f32[2,2,1024]{2,1,0:T(2,128)} %get-tuple-element.78.refs_0_, f32[2,4,32]{2,1,0:T(4,128)} %get-tuple-element.79.refs_1_, s32[1,512]{1,0:T(1,128)} %bitcast.59, ...), custom_call_target="tpu_custom_call" | custom-call | tf_op jit(solution)/shard_map/backward_recurrent/pallas_call | solution.py:1599
  256.1 89.9 %backward_local.1 = (bf16[2,2048,1024]{2,1,0:T(8,128)(2,1)}, bf16[3072,1024]{1,0:T(8,128)(2,1)}, f32[16,1024]{1,0:T(8,128)}, f32[2,256,1024]{2,1,0:T(8,128)}) custom-call(f32[2,2,1024]{2,1,0:T(2,128)} %get-tuple-element.78.refs_0_, f32[2,4,32]{2,1,0:T(4,128)} %get-tuple-element.79.refs_1_, s32[1,512]{1,0:T(1,128)} %bitcast.60, ...), custom_call_target="tpu_custom_call" | custom-call | tf_op jit(solution)/shard_map/backward_local/pallas_call | solution.py:1599
  345.9 138.3 %sum_gradients.1 = (bf16[2,3072,1024]{2,1,0:T(8,128)(2,1)}, f32[3,32,1024]{2,1,0:T(8,128)}) custom-call(bf16[3072,1024]{1,0:T(8,128)(2,1)} %get-tuple-element.114.parts, f32[16,1024]{1,0:T(8,128)} %get-tuple-element.115.small_0, f32[16,1024]{1,0:T(8,128)} %get-tuple-element.116.small_1), custom_call_target="tpu_custom_call" | custom-call | tf_op jit(solution)/shard_map/sum_gradients/pallas_call | solution.py:980
  484.2 20.7 %place_gradients.1 = (f32[1,3,1024,512]{3,2,1,0:T(8,128)}, f32[1,512,1024]{2,1,0:T(8,128)}, f32[1,1024,2048]{2,1,0:T(8,128)}, f32[1,2048,1024]{2,1,0:T(8,128)}, ...) custom-call(bf16[2,2048,1024]{2,1,0:T(8,128)(2,1)} %get-tuple-elemen, ...), custom_call_target="tpu_custom_call" | custom-call | tf_op jit(solution)/shard_map/place_gradients/pallas_call | solution.py:1758
